TPU v7x, 32 devices: a whole 2x2x4 slice. The times are simulated.
32 devices in a mesh: seq: 2 (over core), ctx: 4 (over y, x), fsdp: 4 (over z).
Axes of the slice: x: 2, y: 2, z: 4, core: 2. Of those that a mesh axis runs over, the one named last changes fastest.
Arguments:
- tokens: bfloat16 [2, 3072, 896], P('seq', ('ctx', 'fsdp')), may hold values from -6 to 6
- out_grad: bfloat16 [2, 3072, 896], P('seq', ('ctx', 'fsdp')), may hold values from -6 to 6
- block_order: int32 [2, 4], P('seq'), may hold values from 0 to 3, each once within a row
- norm1_gain: bfloat16 [896], P('fsdp'), may hold values from 0.5 to 1.5
- q_weight: bfloat16 [896, 896], P('fsdp'), may hold values from -0.25 to 0.25
- q_bias: bfloat16 [896], P('fsdp'), may hold values from -1.25 to 1.25
- k_weight: bfloat16 [896, 128], P('fsdp'), may hold values from -0.25 to 0.25
- k_bias: bfloat16 [128], P('fsdp'), may hold values from -1.25 to 1.25
- v_weight: bfloat16 [896, 128], P('fsdp'), may hold values from -0.1875 to 0.1875
- v_bias: bfloat16 [128], P('fsdp'), may hold values from -1.25 to 1.25
- o_weight: bfloat16 [896, 896], P('fsdp'), may hold values from -0.375 to 0.375
- norm2_gain: bfloat16 [896], P('fsdp'), may hold values from 0.5 to 1.5
- gate_weight: bfloat16 [896, 4864], P('fsdp'), may hold values from -0.1875 to 0.1875
- up_weight: bfloat16 [896, 4864], P('fsdp'), may hold values from -0.1875 to 0.1875
- down_weight: bfloat16 [4864, 896], P('fsdp'), may hold values from -0.078125 to 0.078125
Outputs:
- layer_out: bfloat16 [2, 3072, 896], P('seq', ('ctx', 'fsdp'))
- tokens_grad: float32 [2, 3072, 896], P('seq', ('ctx', 'fsdp'))
- norm1_gain_grad: float32 [896], P('fsdp')
- q_weight_grad: float32 [896, 896], P('fsdp')
- q_bias_grad: float32 [896], P('fsdp')
- k_weight_grad: float32 [896, 128], P('fsdp')
- k_bias_grad: float32 [128], P('fsdp')
- v_weight_grad: float32 [896, 128], P('fsdp')
- v_bias_grad: float32 [128], P('fsdp')
- o_weight_grad: float32 [896, 896], P('fsdp')
- norm2_gain_grad: float32 [896], P('fsdp')
- gate_weight_grad: float32 [896, 4864], P('fsdp')
- up_weight_grad: float32 [896, 4864], P('fsdp')
- down_weight_grad: float32 [4864, 896], P('fsdp')
Inputs may be any that keep to these rules, and one draw needn't show every extreme that they name: `block_order`: each row is a permutation of 0 to 3.
All inputs are finite; a program needn't handle non-finite values.
Results may differ from a plain program's by a relative error of at most 0.04.
Values may be sent and summed in bfloat16 or wider, within the bound.
No kernel may reach another device: no remote copies, remote signals or barrier semaphores. Data moves between devices by JAX's collectives and lax.ppermute only.
A program may use at most 256 MiB of HBM per device.

v0:
```python
import math

import jax
import jax.numpy as jnp
from jax import lax
from jax.sharding import PartitionSpec as P

HEADS = 14
KV_HEADS = 2
HEAD = 64


NORM_EPS = 1e-06
ROPE_BASE = 1000000.0
MASKED = -1e30


def rope_tables(positions, head_dim):
    half_dim = head_dim // 2
    inverse = jnp.exp(
        jnp.arange(half_dim, dtype=jnp.float32) * (-math.log(ROPE_BASE) * 2.0 / head_dim)
    )
    angles = positions.astype(jnp.float32)[:, None] * inverse[None, :]
    return (jnp.cos(angles)[:, None, :], jnp.sin(angles)[:, None, :])


def rotate(values, cosine_table, sine_table):
    half_dim = values.shape[-1] // 2
    front_half = values[..., :half_dim]
    back_half = values[..., half_dim:]
    return jnp.concatenate(
        [
            front_half * cosine_table - back_half * sine_table,
            back_half * cosine_table + front_half * sine_table,
        ],
        -1,
    )


def contract_rows(left_side, right_side):
    return lax.dot_general(
        left_side, right_side, (((0,), (0,)), ((), ())), preferred_element_type=jnp.float32
    )


def times_transposed(left_side, right_side):
    return lax.dot_general(
        left_side, right_side, (((1,), (1,)), ((), ())), preferred_element_type=jnp.float32
    )


def rms_forward(values, gain_vec):
    inv_scale = lax.rsqrt(jnp.mean(values * values, -1, keepdims=True) + NORM_EPS)
    normed = values * inv_scale
    return (normed, inv_scale, (normed * gain_vec).astype(jnp.bfloat16))


def rms_backward(grad_out, normed, inv_scale, gain_vec):
    gain_grad = jnp.sum(grad_out * normed, 0)
    scaled = grad_out * gain_vec
    grad_in = inv_scale * (scaled - normed * jnp.mean(scaled * normed, -1, keepdims=True))
    return (grad_in, gain_grad)


def group_heads(values, kv_heads):
    tokens_here, head_count, head_dim = values.shape
    group_size = head_count // kv_heads
    return (
        values.reshape(tokens_here, kv_heads, group_size, head_dim)
        .transpose(1, 2, 0, 3)
        .reshape(kv_heads, group_size * tokens_here, head_dim)
    )


def ungroup_heads(values, tokens_here):
    kv_heads, row_count, head_dim = values.shape
    group_size = row_count // tokens_here
    return (
        values.reshape(kv_heads, group_size, tokens_here, head_dim)
        .transpose(2, 0, 1, 3)
        .reshape(tokens_here, kv_heads * group_size * head_dim)
    )


def scores_of(queries, query_rows_pos, keys_block, key_pos_block, score_scale):
    raw_scores = jnp.einsum("gqd,kgd->gqk", queries, keys_block, preferred_element_type=jnp.float32)
    allowed = key_pos_block[None, None, :] <= query_rows_pos[None, :, None]
    return (jnp.where(allowed, raw_scores * score_scale, MASKED), allowed)


def attend_forward(queries, query_rows_pos, key_blocks, value_blocks, key_pos_blocks, score_scale):
    kv_heads, row_count, head_dim = queries.shape
    query_top = jnp.max(query_rows_pos)

    def stats_step(carry, block_in):
        keys_block, key_pos_block = block_in

        def stats_active(stats_state):
            running_top, running_sum = stats_state
            scores, allowed = scores_of(
                queries, query_rows_pos, keys_block, key_pos_block, score_scale
            )
            new_top = jnp.maximum(running_top, jnp.max(scores, -1))
            exp_scores = jnp.where(allowed, jnp.exp(scores - new_top[..., None]), 0.0)
            return (new_top, running_sum * jnp.exp(running_top - new_top) + jnp.sum(exp_scores, -1))

        def stats_passed(stats_state):
            return stats_state

        return (
            lax.cond(jnp.min(key_pos_block) <= query_top, stats_active, stats_passed, carry),
            None,
        )

    start_top = jnp.full((kv_heads, row_count), MASKED, jnp.float32)
    start_sum = jnp.zeros((kv_heads, row_count), jnp.float32)
    (final_top, final_sum), unused = lax.scan(
        stats_step, (start_top, start_sum), (key_blocks, key_pos_blocks)
    )
    log_total = final_top + jnp.log(final_sum)

    def value_step(carry, block_in):
        keys_block, values_block, key_pos_block = block_in

        def value_active(running):
            scores, allowed = scores_of(
                queries, query_rows_pos, keys_block, key_pos_block, score_scale
            )
            prob_values = jnp.where(allowed, jnp.exp(scores - log_total[..., None]), 0.0).astype(
                jnp.bfloat16
            )
            return running + jnp.einsum(
                "gqk,kgd->gqd", prob_values, values_block, preferred_element_type=jnp.float32
            )

        def value_passed(running):
            return running

        return (
            lax.cond(jnp.min(key_pos_block) <= query_top, value_active, value_passed, carry),
            None,
        )

    start_out = jnp.zeros((kv_heads, row_count, head_dim), jnp.float32)
    output, unused_two = lax.scan(value_step, start_out, (key_blocks, value_blocks, key_pos_blocks))
    return (output, log_total)


def attend_backward(
    queries,
    query_rows_pos,
    key_blocks,
    value_blocks,
    key_pos_blocks,
    score_scale,
    log_total,
    grad_rows,
    row_delta,
):
    kv_heads, row_count, head_dim = queries.shape
    query_top = jnp.max(query_rows_pos)

    def back_step(carry, block_in):
        keys_block, values_block, key_pos_block = block_in
        block_rows = keys_block.shape[0]

        def back_active(running):
            scores, allowed = scores_of(
                queries, query_rows_pos, keys_block, key_pos_block, score_scale
            )
            prob_values = jnp.where(allowed, jnp.exp(scores - log_total[..., None]), 0.0)
            grad_values = jnp.einsum(
                "gqk,gqd->kgd",
                prob_values.astype(jnp.bfloat16),
                grad_rows,
                preferred_element_type=jnp.float32,
            )
            grad_probs = jnp.einsum(
                "gqd,kgd->gqk", grad_rows, values_block, preferred_element_type=jnp.float32
            )
            grad_scores = (prob_values * (grad_probs - row_delta[..., None]) * score_scale).astype(
                jnp.bfloat16
            )
            running = running + jnp.einsum(
                "gqk,kgd->gqd", grad_scores, keys_block, preferred_element_type=jnp.float32
            )
            grad_keys = jnp.einsum(
                "gqk,gqd->kgd", grad_scores, queries, preferred_element_type=jnp.float32
            )
            stacked = jnp.concatenate(
                [
                    grad_keys.reshape(block_rows, kv_heads * head_dim),
                    grad_values.reshape(block_rows, kv_heads * head_dim),
                ],
                1,
            )
            return (running, stacked)

        def back_passed(running):
            return (running, jnp.zeros((block_rows, 2 * kv_heads * head_dim), jnp.float32))

        return lax.cond(jnp.min(key_pos_block) <= query_top, back_active, back_passed, carry)

    start_grad = jnp.zeros((kv_heads, row_count, head_dim), jnp.float32)
    grad_queries, grad_terms = lax.scan(
        back_step, start_grad, (key_blocks, value_blocks, key_pos_blocks)
    )
    return (grad_queries, grad_terms.reshape(-1, 2 * kv_heads * head_dim))


def local(
    tokens,
    out_grad,
    block_order,
    norm1_gain,
    q_weight,
    q_bias,
    k_weight,
    k_bias,
    v_weight,
    v_bias,
    o_weight,
    norm2_gain,
    gate_weight,
    up_weight,
    down_weight,
):
    shards = (
        norm1_gain,
        q_weight,
        q_bias,
        k_weight,
        k_bias,
        v_weight,
        v_bias,
        o_weight,
        norm2_gain,
        gate_weight,
        up_weight,
        down_weight,
    )
    gathered = (
        lax.all_gather(norm1_gain, "fsdp", axis=0, tiled=True),
        lax.all_gather(q_weight, "fsdp", axis=0, tiled=True),
        lax.all_gather(q_bias, "fsdp", axis=0, tiled=True),
        lax.all_gather(k_weight, "fsdp", axis=0, tiled=True),
        lax.all_gather(k_bias, "fsdp", axis=0, tiled=True),
        lax.all_gather(v_weight, "fsdp", axis=0, tiled=True),
        lax.all_gather(v_bias, "fsdp", axis=0, tiled=True),
        lax.all_gather(o_weight, "fsdp", axis=0, tiled=True),
        lax.all_gather(norm2_gain, "fsdp", axis=0, tiled=True),
        lax.all_gather(gate_weight, "fsdp", axis=0, tiled=True),
        lax.all_gather(up_weight, "fsdp", axis=0, tiled=True),
        lax.all_gather(down_weight, "fsdp", axis=0, tiled=True),
    )
    (
        gain_one,
        w_query,
        b_query,
        w_key,
        b_key,
        w_value,
        b_value,
        w_out,
        gain_two,
        w_gate,
        w_up,
        w_down,
    ) = gathered
    tokens_here = tokens.shape[1]
    key_width = KV_HEADS * HEAD
    group_size = HEADS // KV_HEADS
    score_scale = HEAD ** (-0.5)
    block_len = tokens_here * lax.axis_size("fsdp")
    block_count = lax.axis_size("ctx")
    order_row = block_order[0]
    query_pos = (
        order_row[lax.axis_index("ctx")] * block_len
        + lax.axis_index("fsdp") * tokens_here
        + jnp.arange(tokens_here, dtype=jnp.int32)
    )
    key_pos_blocks = (
        order_row[:, None] * block_len + jnp.arange(block_len, dtype=jnp.int32)[None, :]
    )
    query_rows_pos = jnp.tile(query_pos, group_size)
    inputs = tokens[0].astype(jnp.float32)
    normed_one, scale_one, hidden_one = rms_forward(inputs, gain_one)
    query_pre = jnp.dot(hidden_one, w_query, preferred_element_type=jnp.float32) + b_query
    key_pre = jnp.dot(hidden_one, w_key, preferred_element_type=jnp.float32) + b_key
    value_pre = jnp.dot(hidden_one, w_value, preferred_element_type=jnp.float32) + b_value
    cosine_table, sine_table = rope_tables(query_pos, HEAD)
    query_rot = rotate(
        query_pre.reshape(tokens_here, HEADS, HEAD), cosine_table, sine_table
    ).astype(jnp.bfloat16)
    key_rot = rotate(key_pre.reshape(tokens_here, KV_HEADS, HEAD), cosine_table, sine_table).astype(
        jnp.bfloat16
    )
    kv_local = jnp.concatenate(
        [key_rot.reshape(tokens_here, key_width), value_pre.astype(jnp.bfloat16)], 1
    )
    kv_whole = lax.all_gather(kv_local, ("ctx", "fsdp"), axis=0, tiled=True)
    queries = group_heads(query_rot, KV_HEADS)
    key_blocks = kv_whole[:, :key_width].reshape(block_count, block_len, KV_HEADS, HEAD)
    value_blocks = kv_whole[:, key_width:].reshape(block_count, block_len, KV_HEADS, HEAD)
    output, log_total = attend_forward(
        queries, query_rows_pos, key_blocks, value_blocks, key_pos_blocks, score_scale
    )
    attended = ungroup_heads(output, tokens_here).astype(jnp.bfloat16)
    resid = inputs + jnp.dot(attended, w_out, preferred_element_type=jnp.float32)
    normed_two, scale_two, hidden_two = rms_forward(resid, gain_two)
    gate_pre = jnp.dot(hidden_two, w_gate, preferred_element_type=jnp.float32)
    up_pre = jnp.dot(hidden_two, w_up, preferred_element_type=jnp.float32)
    sigmoid_gate = jax.nn.sigmoid(gate_pre)
    silu_gate = gate_pre * sigmoid_gate
    activated = (silu_gate * up_pre).astype(jnp.bfloat16)
    result = resid + jnp.dot(activated, w_down, preferred_element_type=jnp.float32)
    layer_out = result.astype(jnp.bfloat16)[None]
    regathered = (
        lax.all_gather(shards[0], "fsdp", axis=0, tiled=True),
        lax.all_gather(shards[1], "fsdp", axis=0, tiled=True),
        lax.all_gather(shards[2], "fsdp", axis=0, tiled=True),
        lax.all_gather(shards[3], "fsdp", axis=0, tiled=True),
        lax.all_gather(shards[4], "fsdp", axis=0, tiled=True),
        lax.all_gather(shards[5], "fsdp", axis=0, tiled=True),
        lax.all_gather(shards[6], "fsdp", axis=0, tiled=True),
        lax.all_gather(shards[7], "fsdp", axis=0, tiled=True),
        lax.all_gather(shards[8], "fsdp", axis=0, tiled=True),
        lax.all_gather(shards[9], "fsdp", axis=0, tiled=True),
        lax.all_gather(shards[10], "fsdp", axis=0, tiled=True),
        lax.all_gather(shards[11], "fsdp", axis=0, tiled=True),
    )
    gain_one = regathered[0]
    w_query = regathered[1]
    w_key = regathered[3]
    w_value = regathered[5]
    w_out = regathered[7]
    gain_two = regathered[8]
    w_gate = regathered[9]
    w_up = regathered[10]
    w_down = regathered[11]
    down_in = out_grad[0]
    grad_top = down_in.astype(jnp.float32)
    grad_w_down = contract_rows(activated, down_in)
    grad_act = times_transposed(down_in, w_down)
    grad_gate = (grad_act * up_pre * sigmoid_gate * (1.0 + gate_pre * (1.0 - sigmoid_gate))).astype(
        jnp.bfloat16
    )
    grad_up = (grad_act * silu_gate).astype(jnp.bfloat16)
    grad_w_gate = contract_rows(hidden_two, grad_gate)
    grad_w_up = contract_rows(hidden_two, grad_up)
    grad_hidden_two = times_transposed(grad_gate, w_gate) + times_transposed(grad_up, w_up)
    grad_norm_two, grad_gain_two = rms_backward(grad_hidden_two, normed_two, scale_two, gain_two)
    grad_resid = grad_top + grad_norm_two
    grad_proj = grad_resid.astype(jnp.bfloat16)
    grad_w_out = contract_rows(attended, grad_proj)
    grad_att = times_transposed(grad_proj, w_out).astype(jnp.bfloat16)
    grad_rows = group_heads(grad_att.reshape(tokens_here, HEADS, HEAD), KV_HEADS)
    row_delta = jnp.sum(grad_rows.astype(jnp.float32) * output, -1)
    kv_back = lax.all_gather(kv_local, ("ctx", "fsdp"), axis=0, tiled=True)
    key_blocks = kv_back[:, :key_width].reshape(block_count, block_len, KV_HEADS, HEAD)
    value_blocks = kv_back[:, key_width:].reshape(block_count, block_len, KV_HEADS, HEAD)
    grad_queries, grad_terms = attend_backward(
        queries,
        query_rows_pos,
        key_blocks,
        value_blocks,
        key_pos_blocks,
        score_scale,
        log_total,
        grad_rows,
        row_delta,
    )
    grad_kv = lax.psum_scatter(grad_terms, ("ctx", "fsdp"), scatter_dimension=0, tiled=True)
    grad_q_pre = (
        rotate(
            ungroup_heads(grad_queries, tokens_here).reshape(tokens_here, HEADS, HEAD),
            cosine_table,
            -sine_table,
        )
        .reshape(tokens_here, HEADS * HEAD)
        .astype(jnp.bfloat16)
    )
    grad_k_pre = (
        rotate(
            grad_kv[:, :key_width].reshape(tokens_here, KV_HEADS, HEAD), cosine_table, -sine_table
        )
        .reshape(tokens_here, key_width)
        .astype(jnp.bfloat16)
    )
    grad_v_pre = grad_kv[:, key_width:].astype(jnp.bfloat16)
    grad_b_query = jnp.sum(grad_q_pre.astype(jnp.float32), 0)
    grad_b_key = jnp.sum(grad_k_pre.astype(jnp.float32), 0)
    grad_b_value = jnp.sum(grad_v_pre.astype(jnp.float32), 0)
    grad_w_query = contract_rows(hidden_one, grad_q_pre)
    grad_w_key = contract_rows(hidden_one, grad_k_pre)
    grad_w_value = contract_rows(hidden_one, grad_v_pre)
    grad_hidden_one = (
        times_transposed(grad_q_pre, w_query)
        + times_transposed(grad_k_pre, w_key)
        + times_transposed(grad_v_pre, w_value)
    )
    grad_norm_one, grad_gain_one = rms_backward(grad_hidden_one, normed_one, scale_one, gain_one)
    tokens_grad = (grad_resid + grad_norm_one)[None]
    shares = (
        lax.psum_scatter(
            grad_gain_one.astype(jnp.bfloat16), "fsdp", scatter_dimension=0, tiled=True
        ).astype(jnp.float32),
        lax.psum_scatter(
            grad_w_query.astype(jnp.bfloat16), "fsdp", scatter_dimension=0, tiled=True
        ).astype(jnp.float32),
        lax.psum_scatter(
            grad_b_query.astype(jnp.bfloat16), "fsdp", scatter_dimension=0, tiled=True
        ).astype(jnp.float32),
        lax.psum_scatter(
            grad_w_key.astype(jnp.bfloat16), "fsdp", scatter_dimension=0, tiled=True
        ).astype(jnp.float32),
        lax.psum_scatter(
            grad_b_key.astype(jnp.bfloat16), "fsdp", scatter_dimension=0, tiled=True
        ).astype(jnp.float32),
        lax.psum_scatter(
            grad_w_value.astype(jnp.bfloat16), "fsdp", scatter_dimension=0, tiled=True
        ).astype(jnp.float32),
        lax.psum_scatter(
            grad_b_value.astype(jnp.bfloat16), "fsdp", scatter_dimension=0, tiled=True
        ).astype(jnp.float32),
        lax.psum_scatter(
            grad_w_out.astype(jnp.bfloat16), "fsdp", scatter_dimension=0, tiled=True
        ).astype(jnp.float32),
        lax.psum_scatter(
            grad_gain_two.astype(jnp.bfloat16), "fsdp", scatter_dimension=0, tiled=True
        ).astype(jnp.float32),
        lax.psum_scatter(
            grad_w_gate.astype(jnp.bfloat16), "fsdp", scatter_dimension=0, tiled=True
        ).astype(jnp.float32),
        lax.psum_scatter(
            grad_w_up.astype(jnp.bfloat16), "fsdp", scatter_dimension=0, tiled=True
        ).astype(jnp.float32),
        lax.psum_scatter(
            grad_w_down.astype(jnp.bfloat16), "fsdp", scatter_dimension=0, tiled=True
        ).astype(jnp.float32),
    )
    totals = lax.psum(
        (
            shares[0],
            shares[1],
            shares[2],
            shares[3],
            shares[4],
            shares[5],
            shares[6],
            shares[7],
            shares[8],
            shares[9],
            shares[10],
            shares[11],
        ),
        ("seq", "ctx"),
    )
    return (
        layer_out,
        tokens_grad,
        totals[0],
        totals[1],
        totals[2],
        totals[3],
        totals[4],
        totals[5],
        totals[6],
        totals[7],
        totals[8],
        totals[9],
        totals[10],
        totals[11],
    )


def solution(mesh):
    in_specs = (
        P("seq", ("ctx", "fsdp"), None),
        P("seq", ("ctx", "fsdp"), None),
        P("seq", None),
        P("fsdp"),
        P("fsdp", None),
        P("fsdp"),
        P("fsdp", None),
        P("fsdp"),
        P("fsdp", None),
        P("fsdp"),
        P("fsdp", None),
        P("fsdp"),
        P("fsdp", None),
        P("fsdp", None),
        P("fsdp", None),
    )
    out_specs = (
        P("seq", ("ctx", "fsdp"), None),
        P("seq", ("ctx", "fsdp"), None),
        P("fsdp"),
        P("fsdp", None),
        P("fsdp"),
        P("fsdp", None),
        P("fsdp"),
        P("fsdp", None),
        P("fsdp"),
        P("fsdp", None),
        P("fsdp"),
        P("fsdp", None),
        P("fsdp", None),
        P("fsdp", None),
    )
    return jax.shard_map(local, mesh=mesh, in_specs=in_specs, out_specs=out_specs, check_vma=False)
```

profile of v0, /device:TPU:1, one launch (start us, length us, event | category | flops | bytes accessed | tf_op | source)
XLA Modules:
  0.0 1991.3 jit_solution(7543641837648737235)
XLA Ops:
  14.8 11.2 all-reduce.12
  26.1 13.3 all_gather.50
  45.0 12.5 all_gather.52
  66.8 54.7 %all-gather.7.cloned.1.call-done = bf16[3072,256]{1,0:T(8,128)(2,1)} async-done(((bf16[192,256]{1,0:T(8,128)(2,1)}), bf16[3072,256]{1,0:T(8,128)(2,1)}) %all-gather.7.cloned.1.call-update) | async-done | bytes 1572880 | tf_op jit(solution)/shard_map/all_gather | solution.py:301
  133.4 21.5 %while.43 = (s32[]{:T(128)}, f32[2,1344]{1,0:T(2,128)S(1)}, f32[2,1344]{1,0:T(2,128)S(1)}, s32[4,768]{1,0:T(4,128)S(1)}, s32[]{:T(128)}, /*index=5*/bf16[4,768,2...) while((s32[]{:T(128)}, f32[2,1344]{1,0:T(2,128)S(1)}, ...), condition=%wide.region_8.9_spmd.clone, body=%wide.region_2.8_spmd.clone.sunk | while | flops 281794560 | bytes 20330464 | solution.py:117
  135.4 6.8 conditional.9
  146.1 6.8 conditional.9
  155.0 19.4 while.44
  157.0 5.6 conditional.10
  166.5 5.7 conditional.10
  177.6 138.5 %all-gather.13.cloned.1.call-done = bf16[896,4864]{1,0:T(8,128)(2,1)} async-done(((bf16[224,4864]{1,0:T(8,128)(2,1)}), bf16[896,4864]{1,0:T(8,128)(2,1)}) %all-gather.13.cloned.1.call-update) | async-done | bytes 8716304 | tf_op jit(solution)/shard_map/all_gather | solution.py:252
  316.0 7.4 fusion.88
  323.5 147.2 %all-gather.15.cloned.1.call-done = bf16[896,4864]{1,0:T(8,128)(2,1)} async-done(((bf16[224,4864]{1,0:T(8,128)(2,1)}), bf16[896,4864]{1,0:T(8,128)(2,1)}) %all-gather.15.cloned.1.call-update) | async-done | bytes 8716304 | tf_op jit(solution)/shard_map/all_gather | solution.py:253
  470.7 7.4 fusion.89
  478.2 147.2 %all-gather.17.cloned.1.call-done = bf16[4864,896]{1,0:T(8,128)(2,1)} async-done(((bf16[1216,896]{1,0:T(8,128)(2,1)}), bf16[4864,896]{1,0:T(8,128)(2,1)}) %all-gather.17.cloned.1.call-update) | async-done | bytes 8716304 | tf_op jit(solution)/shard_map/all_gather | solution.py:254
  625.4 10.6 multiply_convert_fusion
  636.0 7.8 fusion.90
  650.3 35.7 %while.45 = (s32[]{:T(128)}, f32[2,1344,64]{1,2,0:T(8,128)S(1)}, f32[4,768,256]{2,1,0:T(8,128)}, s32[4,768]{1,0:T(4,128)S(1)}, s32[]{:T(128)}, /*index=5*/bf16[4...) while((s32[]{:T(128)}, f32[2,1344,64]{1,2,0:T(8,128)S(1)}, ...), condition=%wide.region_21.22_spmd.clone, body=%wide.region_17.0_spmd.clone.sunk | while | flops 1341186816 | bytes 48132096 | solution.py:205
  652.4 11.3 conditional.11
  670.2 11.4 conditional.11
  691.9 142.9 %reduce-scatter.9.cloned.1.call-done = f32[192,256]{1,0:T(8,128)} async-done(((f32[3072,256]{1,0:T(8,128)}), f32[192,256]{1,0:T(8,128)}) %reduce-scatter.9.cloned.1.call-update) | async-done | bytes 196624 | tf_op jit(solution)/shard_map/reduce_scatter | solution.py:373
  840.6 5.9 convolution_convert_fusion.2
  848.0 5.9 convolution_convert_fusion.1
  855.5 5.0 convolution_convert_fusion
  862.4 7.0 fusion.45
  873.6 37.1 %reduce-scatter.17.cloned.1.call-done = bf16[224,896]{1,0:T(8,128)(2,1)} async-done(((bf16[896,896]{1,0:T(8,128)(2,1)}), bf16[224,896]{1,0:T(8,128)(2,1)}) %reduce-scatter.17.cloned.1.call-update) | async-done | bytes 401424 | tf_op jit(solution)/shard_map/reduce_scatter | solution.py:426
  917.8 8.8 all-reduce.11
  929.9 20.8 %reduce-scatter.15.cloned.1.call-done = bf16[224,128]{1,0:T(8,128)(2,1)} async-done(((bf16[896,128]{1,0:T(8,128)(2,1)}), bf16[224,128]{1,0:T(8,128)(2,1)}) %reduce-scatter.15.cloned.1.call-update) | async-done | bytes 57360 | tf_op jit(solution)/shard_map/reduce_scatter | solution.py:420
  950.6 152.2 %reduce-scatter.19.cloned.1.call-done = bf16[224,4864]{1,0:T(8,128)(2,1)} async-done(((bf16[896,4864]{1,0:T(8,128)(2,1)}), bf16[224,4864]{1,0:T(8,128)(2,1)}) %reduce-scatter.19.cloned.1.call-update) | async-done | bytes 2179088 | tf_op jit(solution)/shard_map/reduce_scatter | solution.py:432
  1102.9 153.0 %reduce-scatter.21.cloned.1.call-done = bf16[224,4864]{1,0:T(8,128)(2,1)} async-done(((bf16[896,4864]{1,0:T(8,128)(2,1)}), bf16[224,4864]{1,0:T(8,128)(2,1)}) %reduce-scatter.21.cloned.1.call-update) | async-done | bytes 2179088 | tf_op jit(solution)/shard_map/reduce_scatter | solution.py:435
  1255.9 152.7 %reduce-scatter.23.cloned.1.call-done = bf16[1216,896]{1,0:T(8,128)(2,1)} async-done(((bf16[4864,896]{1,0:T(8,128)(2,1)}), bf16[1216,896]{1,0:T(8,128)(2,1)}) %reduce-scatter.23.cloned.1.call-update) | async-done | bytes 2179088 | tf_op jit(solution)/shard_map/reduce_scatter | solution.py:438
  1408.6 575.7 %all-reduce.14 = (f32[224]{0:T(256)}, f32[224,896]{1,0:T(8,128)}, f32[224]{0:T(256)}, f32[224,128]{1,0:T(8,128)}, f32[32]{0:T(128)}, /*index=5*/f32[224,128]{1,0...) all-reduce(f32[224]{0:T(256)S(1)} %dynamic-slice_convert_fusion.4, ...), channel_id=1, replica_groups=mesh['seq'=2,'ctx'=4,'fsdp'=4] {'seq','ctx'}, use_global_device_ids=true, to_apply=%region_26.27 | all-reduce | flops 3728096 | bytes 22370048 | tf_op jit(solution)/shard_map/psum | solution.py:442
  (264 shorter events, 131.4 us)
Async XLA Ops:
  7.2 56.4 %all-gather.9.cloned.1.call-start = ((), (), s32[]{:S(2)}) async-start(), calls=%async_computation.9 | async-start | bytes 2007040 | tf_op jit(solution)/shard_map/all_gather | solution.py:244
  7.9 113.6 %all-gather.7.cloned.1.call-start = ((), (), s32[]{:S(2)}) async-start(), calls=%async_computation.8 | async-start | bytes 1671168 | tf_op jit(solution)/shard_map/all_gather | solution.py:301
  26.1 37.5 %copy-start.27 = (f32[896]{0:T(1024)}, f32[896]{0:T(1024)S(1)}, u32[]{:S(2)}) copy-start(f32[896]{0:T(1024)S(1)} %convert_element_type.216) | copy-start | bytes 10756
  39.4 5.5 copy-start.20
  40.7 22.9 %copy-start.29 = (f32[192]{0:T(256)}, f32[192]{0:T(256)S(1)}, u32[]{:S(2)}) copy-start(f32[192]{0:T(256)S(1)} %add_rsqrt_fusion.1) | copy-start | bytes 2308
  44.8 21.1 %copy-start.23 = (f32[192,32]{0,1:T(8,128)}, f32[192,32]{0,1:T(8,128)S(1)}, u32[]{:S(2)}) copy-start(f32[192,32]{0,1:T(8,128)S(1)} %get-tuple-element.676) | copy-start | bytes 73732
  58.2 5.2 copy-start.33
  58.2 5.3 copy-start.1
  60.3 114.8 %all-gather.11.cloned.1.call-start = ((), (), s32[]{:S(2)}) async-start(), calls=%async_computation.10 | async-start | bytes 2007040 | tf_op jit(solution)/shard_map/all_gather | solution.py:250
  61.0 255.0 %all-gather.13.cloned.1.call-start = ((), (), s32[]{:S(2)}) async-start(), calls=%async_computation.11 | async-start | bytes 10895360 | tf_op jit(solution)/shard_map/all_gather | solution.py:252
  61.6 409.1 %all-gather.15.cloned.1.call-start = ((), (), s32[]{:S(2)}) async-start(), calls=%async_computation.12 | async-start | bytes 10895360 | tf_op jit(solution)/shard_map/all_gather | solution.py:253
  62.2 563.2 %all-gather.17.cloned.1.call-start = ((), (), s32[]{:S(2)}) async-start(), calls=%async_computation.13 | async-start | bytes 10895360 | tf_op jit(solution)/shard_map/all_gather | solution.py:254
  62.8 772.0 %reduce-scatter.9.cloned.1.call-start = ((), (), s32[]{:S(2)}) async-start(), calls=%async_computation.14 | async-start | bytes 3342336 | tf_op jit(solution)/shard_map/reduce_scatter | solution.py:373
  177.4 470.1 %copy-start.4 = (f32[192,896]{1,0:T(8,128)}, f32[192,896]{1,0:T(8,128)S(1)}, u32[]{:S(2)}) copy-start(f32[192,896]{1,0:T(8,128)S(1)} %get-tuple-element.680) | copy-start | bytes 2064388
  177.5 293.2 %copy-start.6 = (bf16[192,896]{1,0:T(8,128)(2,1)}, bf16[192,896]{1,0:T(8,128)(2,1)S(1)}, u32[]{:S(2)}) copy-start(bf16[192,896]{1,0:T(8,128)(2,1)S(1)} %multiply_convert_fusion.3) | copy-start | bytes 1032196
  323.5 301.9 %copy-start.18 = (bf16[1,192,896]{2,1,0:T(8,128)(2,1)S(1)}, bf16[1,192,896]{2,1,0:T(8,128)(2,1)}, u32[]{:S(2)}) copy-start(bf16[1,192,896]{2,1,0:T(8,128)(2,1)} %param.28) | copy-start | bytes 1032196
  636.0 7.9 copy-start.16
  636.0 7.9 copy-start.8
  636.0 7.9 copy-start
  643.9 4.7 copy-start.11
  686.0 187.6 %reduce-scatter.11.cloned.1.call-start = ((), (), s32[]{:S(2)}) async-start(), calls=%async_computation.15 | async-start | bytes 2007040 | tf_op jit(solution)/shard_map/reduce_scatter | solution.py:408
  686.5 3.5 copy-start.3
  689.9 150.7 %copy-start.7 = (bf16[192,896]{1,0:T(8,128)(2,1)S(1)}, bf16[192,896]{1,0:T(8,128)(2,1)}, u32[]{:S(2)}) copy-start(bf16[192,896]{1,0:T(8,128)(2,1)} %copy-done.6) | copy-start | bytes 1032196
  689.9 220.8 %reduce-scatter.17.cloned.1.call-start = ((), (), s32[]{:S(2)}) async-start(), calls=%async_computation.18 | async-start | bytes 2007040 | tf_op jit(solution)/shard_map/reduce_scatter | solution.py:426
  691.8 148.8 %copy-start.17 = (bf16[192,4864]{1,0:T(8,128)(2,1)S(1)}, bf16[192,4864]{1,0:T(8,128)(2,1)}, u32[]{:S(2)}) copy-start(bf16[192,4864]{1,0:T(8,128)(2,1)} %copy-done.16) | copy-start | bytes 5603332
  691.8 238.0 %reduce-scatter.13.cloned.1.call-start = ((), (), s32[]{:S(2)}) async-start(), calls=%async_computation.16 | async-start | bytes 286720 | tf_op jit(solution)/shard_map/reduce_scatter | solution.py:414
  838.2 112.4 %reduce-scatter.15.cloned.1.call-start = ((), (), s32[]{:S(2)}) async-start(), calls=%async_computation.17 | async-start | bytes 286720 | tf_op jit(solution)/shard_map/reduce_scatter | solution.py:420
  840.3 262.6 %reduce-scatter.19.cloned.1.call-start = ((), (), s32[]{:S(2)}) async-start(), calls=%async_computation.19 | async-start | bytes 10895360 | tf_op jit(solution)/shard_map/reduce_scatter | solution.py:432
  846.5 409.4 %reduce-scatter.21.cloned.1.call-start = ((), (), s32[]{:S(2)}) async-start(), calls=%async_computation.20 | async-start | bytes 10895360 | tf_op jit(solution)/shard_map/reduce_scatter | solution.py:435
  854.0 554.7 %reduce-scatter.23.cloned.1.call-start = ((), (), s32[]{:S(2)}) async-start(), calls=%async_computation.21 | async-start | bytes 10895360 | tf_op jit(solution)/shard_map/reduce_scatter | solution.py:438
  862.4 51.0 %copy-start.21 = (bf16[896,128]{1,0:T(8,128)(2,1)S(1)}, bf16[896,128]{1,0:T(8,128)(2,1)}, u32[]{:S(2)}) copy-start(bf16[896,128]{1,0:T(8,128)(2,1)} %copy-done.20) | copy-start | bytes 688132
  862.4 53.4 %copy-start.10 = (bf16[896,896]{1,0:T(8,128)(2,1)S(1)}, bf16[896,896]{1,0:T(8,128)(2,1)}, u32[]{:S(2)}) copy-start(bf16[896,896]{1,0:T(8,128)(2,1)} %all-gather.9.cloned.1.call-done) | copy-start | bytes 4816900
  (16 other events, 27.3 us)
Sparse Core Ops, SparseCore 0:
  9.6 44.5 all-gather.8
  60.4 61.0 all-gather.6
  123.1 37.2 all-gather.10
  161.8 154.1 all-gather.12
  317.5 153.2 all-gather.14
  472.1 153.2 all-gather.16
  686.1 148.6 reduce-scatter.8
  837.1 36.4 reduce-scatter.10
  875.9 34.7 reduce-scatter.16
  913.4 16.4 reduce-scatter.12
  932.8 17.7 reduce-scatter.14
  952.9 149.9 reduce-scatter.18
  1105.4 150.4 reduce-scatter.20
  1258.1 150.4 reduce-scatter.22
where the time goes:
time: 2000 us; the launch traced here: 1990 us
  waiting for transfers between devices  1150 us (58%)
  blocking collectives  622 us (31%)
  matrix products  116 us (6%)
  local copies, waits for them, and re-layouts  35 us (2%)
  other arithmetic  27.9 us (1%)
    psum x1, blocking collectives, local(): lax.psum((shares[0], shares[1], shares[2], shares[3], shares[4], shares[5...  576 us
    reduce_scatter x1, waiting for transfers between devices, local(): lax.psum_scatter(grad_w_up.astype(jnp.bfloat16), 'fsdp', scatter_dimensio...  153 us
    reduce_scatter x1, waiting for transfers between devices, local(): lax.psum_scatter(grad_w_down.astype(jnp.bfloat16), 'fsdp', scatter_dimens...  153 us
    reduce_scatter x1, waiting for transfers between devices, local(): lax.psum_scatter(grad_w_gate.astype(jnp.bfloat16), 'fsdp', scatter_dimens...  152 us
    all_gather x1, waiting for transfers between devices, local(): lax.all_gather(down_weight, 'fsdp', axis=0, tiled=True)  147 us
    all_gather x1, waiting for transfers between devices, local(): lax.all_gather(up_weight, 'fsdp', axis=0, tiled=True)  147 us
    reduce_scatter x1, waiting for transfers between devices, local(): lax.psum_scatter(grad_terms, ('ctx', 'fsdp'), scatter_dimension=0, tiled=...  143 us
    all_gather x1, waiting for transfers between devices, local(): lax.all_gather(gate_weight, 'fsdp', axis=0, tiled=True)  138 us
  transfers between devices with their start and end apart: 14, of which 12 were waited for; matrix products, arithmetic and copies ran while one was open for 6% of the time, Pallas kernels for 0%

commit v1 on v0

v1 whole, which is shorter than its diff:
```python
import math

import jax
import jax.numpy as jnp
from jax import lax
from jax.sharding import PartitionSpec as P

HEADS = 14
KV_HEADS = 2
HEAD = 64
GROUP = HEADS // KV_HEADS
NORM_EPS = 1e-06
ROPE_BASE = 1000000.0
MASKED = -1e30
BF16 = jnp.bfloat16
F32 = jnp.float32


def rope_tables(positions, head_dim):
    half_dim = head_dim // 2
    inverse = jnp.exp(
        jnp.arange(half_dim, dtype=jnp.float32) * (-math.log(ROPE_BASE) * 2.0 / head_dim)
    )
    angles = positions.astype(jnp.float32)[:, None] * inverse[None, :]
    return (jnp.cos(angles)[:, None, :], jnp.sin(angles)[:, None, :])


def rotate(values, cosine_table, sine_table):
    half_dim = values.shape[-1] // 2
    front_half = values[..., :half_dim]
    back_half = values[..., half_dim:]
    return jnp.concatenate(
        [
            front_half * cosine_table - back_half * sine_table,
            back_half * cosine_table + front_half * sine_table,
        ],
        -1,
    )


def matmul(left_side, right_side):
    return jnp.dot(left_side, right_side, preferred_element_type=F32)


def contract_rows(left_side, right_side):
    return lax.dot_general(
        left_side, right_side, (((0,), (0,)), ((), ())), preferred_element_type=F32
    )


def times_transposed(left_side, right_side):
    return lax.dot_general(
        left_side, right_side, (((1,), (1,)), ((), ())), preferred_element_type=F32
    )


def rms_forward(values, gain_vec):
    inv_scale = lax.rsqrt(jnp.mean(values * values, -1, keepdims=True) + NORM_EPS)
    normed = values * inv_scale
    return (normed, inv_scale, (normed * gain_vec).astype(BF16))


def rms_backward(grad_out, normed, inv_scale, gain_vec):
    gain_grad = jnp.sum(grad_out * normed, 0)
    scaled = grad_out * gain_vec
    grad_in = inv_scale * (scaled - normed * jnp.mean(scaled * normed, -1, keepdims=True))
    return (grad_in, gain_grad)


def group_heads(values):
    tokens_here = values.shape[0]
    return (
        values.reshape(tokens_here, KV_HEADS, GROUP, HEAD)
        .transpose(1, 2, 0, 3)
        .reshape(KV_HEADS, GROUP * tokens_here, HEAD)
    )


def ungroup_heads(values, tokens_here):
    return (
        values.reshape(KV_HEADS, GROUP, tokens_here, HEAD)
        .transpose(2, 0, 1, 3)
        .reshape(tokens_here, KV_HEADS * GROUP * HEAD)
    )


def scores_of(queries, query_rows_pos, keys_block, key_pos_block, score_scale):
    raw_scores = jnp.einsum("gqd,kgd->gqk", queries, keys_block, preferred_element_type=F32)
    allowed = key_pos_block[None, None, :] <= query_rows_pos[None, :, None]
    return (jnp.where(allowed, raw_scores * score_scale, MASKED), allowed)


def attend_forward(queries, query_rows_pos, key_blocks, value_blocks, key_pos_blocks, score_scale):
    kv_heads, row_count, head_dim = queries.shape
    query_top = jnp.max(query_rows_pos)

    def step(carry, block_in):
        keys_block, values_block, key_pos_block = block_in

        def active(state):
            running_top, running_sum, running = state
            scores, allowed = scores_of(
                queries, query_rows_pos, keys_block, key_pos_block, score_scale
            )
            new_top = jnp.maximum(running_top, jnp.max(scores, -1))
            exp_scores = jnp.where(allowed, jnp.exp(scores - new_top[..., None]), 0.0)
            shrink = jnp.exp(running_top - new_top)
            running = running * shrink[..., None] + jnp.einsum(
                "gqk,kgd->gqd", exp_scores.astype(BF16), values_block, preferred_element_type=F32
            )
            return (new_top, running_sum * shrink + jnp.sum(exp_scores, -1), running)

        def passed(state):
            return state

        return (lax.cond(jnp.min(key_pos_block) <= query_top, active, passed, carry), None)

    start = (
        jnp.full((kv_heads, row_count), MASKED, F32),
        jnp.zeros((kv_heads, row_count), F32),
        jnp.zeros((kv_heads, row_count, head_dim), F32),
    )
    (final_top, final_sum, output), unused = lax.scan(
        step, start, (key_blocks, value_blocks, key_pos_blocks)
    )
    return (output / final_sum[..., None], final_top + jnp.log(final_sum))


def attend_backward(
    queries,
    query_rows_pos,
    key_blocks,
    value_blocks,
    key_pos_blocks,
    score_scale,
    log_total,
    grad_rows,
    row_delta,
):
    kv_heads, row_count, head_dim = queries.shape
    query_top = jnp.max(query_rows_pos)

    def back_step(carry, block_in):
        keys_block, values_block, key_pos_block = block_in
        block_rows = keys_block.shape[0]

        def back_active(running):
            scores, allowed = scores_of(
                queries, query_rows_pos, keys_block, key_pos_block, score_scale
            )
            prob_values = jnp.where(allowed, jnp.exp(scores - log_total[..., None]), 0.0)
            grad_values = jnp.einsum(
                "gqk,gqd->kgd", prob_values.astype(BF16), grad_rows, preferred_element_type=F32
            )
            grad_probs = jnp.einsum(
                "gqd,kgd->gqk", grad_rows, values_block, preferred_element_type=F32
            )
            grad_scores = (prob_values * (grad_probs - row_delta[..., None]) * score_scale).astype(
                BF16
            )
            running = running + jnp.einsum(
                "gqk,kgd->gqd", grad_scores, keys_block, preferred_element_type=F32
            )
            grad_keys = jnp.einsum(
                "gqk,gqd->kgd", grad_scores, queries, preferred_element_type=F32
            )
            stacked = jnp.concatenate(
                [
                    grad_keys.reshape(block_rows, kv_heads * head_dim),
                    grad_values.reshape(block_rows, kv_heads * head_dim),
                ],
                1,
            )
            return (running, stacked.astype(BF16))

        def back_passed(running):
            return (running, jnp.zeros((block_rows, 2 * kv_heads * head_dim), BF16))

        return lax.cond(jnp.min(key_pos_block) <= query_top, back_active, back_passed, carry)

    start_grad = jnp.zeros((kv_heads, row_count, head_dim), F32)
    return lax.scan(back_step, start_grad, (key_blocks, value_blocks, key_pos_blocks))


def local(
    tokens,
    out_grad,
    block_order,
    norm1_gain,
    q_weight,
    q_bias,
    k_weight,
    k_bias,
    v_weight,
    v_bias,
    o_weight,
    norm2_gain,
    gate_weight,
    up_weight,
    down_weight,
):
    n_ctx = lax.axis_size("ctx")
    n_z = lax.axis_size("fsdp")
    tp = 4 if n_ctx % 4 == 0 else (2 if n_ctx % 2 == 0 else 1)
    here = lax.axis_index("ctx")
    zed = lax.axis_index("fsdp")
    core = lax.axis_index("seq")
    n_part = 2 * tp
    part = lax.rem(here, tp) * 2 + core
    first_core = core == 0

    def swap(v):
        return lax.ppermute(v, "seq", [(0, 1), (1, 0)])

    def hop(v, k):
        if k == 0:
            return v
        return lax.ppermute(v, "ctx", [(i, i ^ k) for i in range(n_ctx)])

    def gather_z(v):
        return lax.all_gather(v, "fsdp", axis=0, tiled=True)

    def scatter_z(v):
        return lax.psum_scatter(v, "fsdp", scatter_dimension=0, tiled=True)

    tokens_here, width = tokens.shape[1:]
    ff = gate_weight.shape[1]
    rows_here = q_weight.shape[0]
    q_half = GROUP * HEAD
    key_width = KV_HEADS * HEAD
    score_scale = HEAD ** (-0.5)
    block_len = tokens_here * n_z

    vec_len = 3 * rows_here + 2 * k_bias.shape[0]
    vec = jnp.concatenate([norm1_gain, norm2_gain, q_bias, k_bias, v_bias])
    half_width = q_half + 2 * HEAD
    vec_rows = 16
    vec = jnp.pad(vec, (0, vec_rows * half_width - vec_len)).reshape(vec_rows, half_width)
    qkv_half = jnp.concatenate(
        [
            lax.dynamic_slice_in_dim(q_weight, core * q_half, q_half, 1),
            lax.dynamic_slice_in_dim(k_weight, core * HEAD, HEAD, 1),
            lax.dynamic_slice_in_dim(v_weight, core * HEAD, HEAD, 1),
        ],
        1,
    )
    got = gather_z(jnp.concatenate([qkv_half, vec], 0)).reshape(n_z, -1, half_width)
    w_qkv_own = got[:, :rows_here].reshape(width, half_width)
    w_qkv_oth = swap(w_qkv_own)
    vecs = got[:, rows_here:].reshape(n_z, -1)
    gain_one = vecs[:, :rows_here].reshape(-1)
    gain_two = vecs[:, rows_here : 2 * rows_here].reshape(-1)
    b_query = vecs[:, 2 * rows_here : 3 * rows_here].reshape(-1)
    kb = k_bias.shape[0]
    b_key = vecs[:, 3 * rows_here : 3 * rows_here + kb].reshape(-1)
    b_value = vecs[:, 3 * rows_here + kb : 3 * rows_here + 2 * kb].reshape(-1)

    ff_z = ff // n_z
    piece = ff_z // n_part
    piece_pad = -(-piece // 32) * 32
    ff_half = n_z * piece_pad

    def ff_columns(w):
        cuts = []
        for j in range(n_z):
            cut = lax.dynamic_slice_in_dim(w, j * ff_z + part * piece, piece, 1)
            cuts.append(jnp.pad(cut, ((0, 0), (0, piece_pad - piece))))
        return jnp.concatenate(cuts, 1)

    gu_own = gather_z(jnp.concatenate([ff_columns(gate_weight), ff_columns(up_weight)], 1))
    gu_oth = swap(gu_own)
    down_cut = lax.dynamic_slice_in_dim(down_weight, part * piece, piece, 0)
    down_own = gather_z(jnp.pad(down_cut, ((0, piece_pad - piece), (0, 0))))
    down_oth = swap(down_own)
    o_half = gather_z(lax.dynamic_slice_in_dim(o_weight, core * (width // 2), width // 2, 1))
    o_oth = swap(o_half)
    w_out = jnp.where(
        first_core,
        jnp.concatenate([o_half, o_oth], 1),
        jnp.concatenate([o_oth, o_half], 1),
    )
    og_here = out_grad[0]
    og_all = jnp.concatenate([hop(og_here, k) for k in range(tp)], 0)

    order_row = block_order[0]
    query_pos = (
        order_row[here] * block_len
        + zed * tokens_here
        + jnp.arange(tokens_here, dtype=jnp.int32)
    )
    if n_ctx == tp:
        block_at = jnp.stack([order_row[here ^ k] for k in range(n_ctx)])
    else:
        block_at = order_row
    key_pos_blocks = (
        block_at[:, None] * block_len + jnp.arange(block_len, dtype=jnp.int32)[None, :]
    )
    query_rows_pos = jnp.tile(query_pos, GROUP)
    cosine_table, sine_table = rope_tables(query_pos, HEAD)

    inputs = tokens[0].astype(F32)
    normed_one, scale_one, hidden_one = rms_forward(inputs, gain_one)
    pre_own = matmul(hidden_one, w_qkv_own)
    pre_oth = matmul(hidden_one, w_qkv_oth)
    pre_a = jnp.where(first_core, pre_own, pre_oth)
    pre_b = jnp.where(first_core, pre_oth, pre_own)
    query_pre = jnp.concatenate([pre_a[:, :q_half], pre_b[:, :q_half]], 1) + b_query
    key_pre = (
        jnp.concatenate([pre_a[:, q_half : q_half + HEAD], pre_b[:, q_half : q_half + HEAD]], 1)
        + b_key
    )
    value_pre = jnp.concatenate([pre_a[:, q_half + HEAD :], pre_b[:, q_half + HEAD :]], 1) + b_value
    query_rot = rotate(
        query_pre.reshape(tokens_here, HEADS, HEAD), cosine_table, sine_table
    ).astype(BF16)
    key_rot = rotate(key_pre.reshape(tokens_here, KV_HEADS, HEAD), cosine_table, sine_table).astype(
        BF16
    )
    kv_local = jnp.concatenate(
        [key_rot.reshape(tokens_here, key_width), value_pre.astype(BF16)], 1
    )
    kv_block = gather_z(kv_local)
    if n_ctx == tp:
        kv_whole = jnp.stack([hop(kv_block, k) for k in range(n_ctx)])
    else:
        kv_whole = lax.all_gather(kv_block, "ctx", axis=0, tiled=False)
    key_blocks = kv_whole[..., :key_width].reshape(n_ctx, block_len, KV_HEADS, HEAD)
    value_blocks = kv_whole[..., key_width:].reshape(n_ctx, block_len, KV_HEADS, HEAD)
    queries = group_heads(query_rot)
    output, log_total = attend_forward(
        queries, query_rows_pos, key_blocks, value_blocks, key_pos_blocks, score_scale
    )
    attended = ungroup_heads(output, tokens_here).astype(BF16)
    resid = inputs + matmul(attended, w_out)
    normed_two, scale_two, hidden_two = rms_forward(resid, gain_two)

    h2_all = jnp.concatenate([hop(hidden_two, k) for k in range(tp)], 0)

    def scatter_plane(v):
        parts = v.astype(BF16).reshape(tp, tokens_here, width)
        total = parts[0].astype(F32)
        for k in range(1, tp):
            total = total + hop(parts[k], k).astype(F32)
        return total

    def ff_half_pass(w_gu, w_d):
        gu = matmul(h2_all, w_gu)
        gate = gu[:, :ff_half]
        up = gu[:, ff_half:]
        sig = jax.nn.sigmoid(gate)
        silu = gate * sig
        act = (silu * up).astype(BF16)
        grad_act = times_transposed(og_all, w_d)
        grad_gate = (grad_act * up * sig * (1.0 + gate * (1.0 - sig))).astype(BF16)
        grad_up = (grad_act * silu).astype(BF16)
        return act, jnp.concatenate([grad_gate, grad_up], 1)

    act_own, ggu_own = ff_half_pass(gu_own, down_own)
    act_oth, ggu_oth = ff_half_pass(gu_oth, down_oth)
    grad_h2 = scatter_plane(times_transposed(ggu_own, gu_own) + times_transposed(ggu_oth, gu_oth))
    result = resid + scatter_plane(matmul(act_own, down_own) + matmul(act_oth, down_oth))
    layer_out = result.astype(BF16)[None]

    def ff_reduce(own, oth):
        total = (own + swap(oth.astype(BF16)).astype(F32)).astype(BF16)
        mine = scatter_z(total)
        if n_ctx != tp:
            groups = [[g * tp + c for g in range(n_ctx // tp)] for c in range(tp)]
            mine = lax.psum(mine, "ctx", axis_index_groups=groups)
        pieces = [hop(mine, k) for k in range(tp)]
        sibling = swap(jnp.stack(pieces))
        both = jnp.concatenate([jnp.stack(pieces), sibling], 0)
        idx = jnp.arange(n_part, dtype=jnp.int32)
        where_at = (idx // 2 ^ lax.rem(here, tp)) + jnp.where(idx % 2 == core, 0, tp)
        return jnp.take(both, where_at, axis=0)

    d_down = ff_reduce(contract_rows(act_own, og_all), contract_rows(act_oth, og_all))
    grad_w_down = d_down[:, :piece].reshape(ff_z, width).astype(F32)
    d_gu = ff_reduce(contract_rows(h2_all, ggu_own), contract_rows(h2_all, ggu_oth))
    d_gu = d_gu.reshape(n_part, rows_here, 2, n_z, piece_pad)[..., :piece]
    d_gu = d_gu.transpose(2, 1, 3, 0, 4).reshape(2, rows_here, ff).astype(F32)
    grad_w_gate = d_gu[0]
    grad_w_up = d_gu[1]

    grad_norm_two, grad_gain_two = rms_backward(grad_h2, normed_two, scale_two, gain_two)
    grad_resid = og_here.astype(F32) + grad_norm_two
    grad_proj = grad_resid.astype(BF16)
    grad_att = times_transposed(grad_proj, w_out).astype(BF16)
    grad_rows = group_heads(grad_att)
    row_delta = jnp.sum(grad_rows.astype(F32) * output, -1)
    grad_queries, grad_terms = attend_backward(
        queries,
        query_rows_pos,
        key_blocks,
        value_blocks,
        key_pos_blocks,
        score_scale,
        log_total,
        grad_rows,
        row_delta,
    )
    if n_ctx == tp:
        kv_sum = grad_terms[0].astype(F32)
        for k in range(1, n_ctx):
            kv_sum = kv_sum + hop(grad_terms[k], k).astype(F32)
        kv_sum = kv_sum.astype(BF16)
    else:
        kv_sum = lax.psum_scatter(grad_terms, "ctx", scatter_dimension=0, tiled=False)
    grad_kv = scatter_z(kv_sum).astype(F32)

    grad_q_pre = (
        rotate(
            ungroup_heads(grad_queries, tokens_here).reshape(tokens_here, HEADS, HEAD),
            cosine_table,
            -sine_table,
        )
        .reshape(tokens_here, HEADS * HEAD)
        .astype(BF16)
    )
    grad_k_pre = (
        rotate(
            grad_kv[:, :key_width].reshape(tokens_here, KV_HEADS, HEAD), cosine_table, -sine_table
        )
        .reshape(tokens_here, key_width)
        .astype(BF16)
    )
    grad_v_pre = grad_kv[:, key_width:].astype(BF16)

    def column_halves(q, k, v):
        return [
            jnp.concatenate(
                [
                    q[:, g * q_half : (g + 1) * q_half],
                    k[:, g * HEAD : (g + 1) * HEAD],
                    v[:, g * HEAD : (g + 1) * HEAD],
                ],
                1,
            )
            for g in range(2)
        ]

    halves = column_halves(grad_q_pre, grad_k_pre, grad_v_pre)
    g_own = jnp.where(first_core, halves[0], halves[1])
    g_oth = jnp.where(first_core, halves[1], halves[0])
    grad_hidden_one = times_transposed(g_own, w_qkv_own) + times_transposed(g_oth, w_qkv_oth)
    grad_norm_one, grad_gain_one = rms_backward(grad_hidden_one, normed_one, scale_one, gain_one)
    tokens_grad = (grad_resid + grad_norm_one)[None]

    def reduce_full(part_sum):
        cols = part_sum.shape[1]
        cut = part_sum.astype(BF16).reshape(n_z, 2, rows_here // 2, cols)
        own = lax.dynamic_index_in_dim(cut, core, 1, keepdims=False)
        oth = lax.dynamic_index_in_dim(cut, 1 - core, 1, keepdims=False)
        both = (own.astype(F32) + swap(oth).astype(F32)).astype(BF16)
        mine = scatter_z(both.reshape(-1, cols))
        if n_ctx == tp:
            k = 1
            while k < n_ctx:
                mine = lax.optimization_barrier(mine)
                mine = (mine.astype(F32) + hop(mine, k).astype(F32)).astype(BF16)
                k *= 2
            mine = lax.optimization_barrier(mine)
        else:
            mine = lax.psum(mine, "ctx")
        other = swap(mine)
        whole = jnp.where(
            first_core, jnp.concatenate([mine, other], 0), jnp.concatenate([other, mine], 0)
        )
        return whole.astype(F32)

    grad_w_out = reduce_full(contract_rows(attended, grad_proj))
    grad_w_query = reduce_full(contract_rows(hidden_one, grad_q_pre))
    grad_w_kv = reduce_full(
        contract_rows(hidden_one, jnp.concatenate([grad_k_pre, grad_v_pre], 1))
    )
    sums = lax.psum(
        jnp.concatenate(
            [
                grad_gain_one,
                grad_gain_two,
                jnp.sum(grad_q_pre.astype(F32), 0),
                jnp.sum(grad_k_pre.astype(F32), 0),
                jnp.sum(grad_v_pre.astype(F32), 0),
            ]
        ),
        ("seq", "ctx", "fsdp"),
    )

    def own_share(start, size):
        share = size // n_z
        return lax.dynamic_slice_in_dim(sums, start + zed * share, share, 0)

    return (
        layer_out,
        tokens_grad,
        own_share(0, width),
        grad_w_query,
        own_share(2 * width, width),
        grad_w_kv[:, :key_width],
        own_share(3 * width, key_width),
        grad_w_kv[:, key_width:],
        own_share(3 * width + key_width, key_width),
        grad_w_out,
        own_share(width, width),
        grad_w_gate,
        grad_w_up,
        grad_w_down,
    )


def solution(mesh):
    in_specs = (
        P("seq", ("ctx", "fsdp"), None),
        P("seq", ("ctx", "fsdp"), None),
        P("seq", None),
        P("fsdp"),
        P("fsdp", None),
        P("fsdp"),
        P("fsdp", None),
        P("fsdp"),
        P("fsdp", None),
        P("fsdp"),
        P("fsdp", None),
        P("fsdp"),
        P("fsdp", None),
        P("fsdp", None),
        P("fsdp", None),
    )
    out_specs = (
        P("seq", ("ctx", "fsdp"), None),
        P("seq", ("ctx", "fsdp"), None),
        P("fsdp"),
        P("fsdp", None),
        P("fsdp"),
        P("fsdp", None),
        P("fsdp"),
        P("fsdp", None),
        P("fsdp"),
        P("fsdp", None),
        P("fsdp"),
        P("fsdp", None),
        P("fsdp", None),
        P("fsdp", None),
    )
    return jax.shard_map(local, mesh=mesh, in_specs=in_specs, out_specs=out_specs, check_vma=False)
```

time: 2000 us -> 615 us (0.31)
  waiting for transfers between devices: 1150 us -> 147 us
  blocking collectives: 622 us -> 88.3 us
  starting transfers between devices: 0.82 us -> 104 us
  local copies, waits for them, and re-layouts: 35 us -> 100 us
  matrix products: 116 us -> 89 us
  other arithmetic: 27.9 us -> 51 us
    reduce_scatter x8 -> x6, waiting for transfers between devices: 664 us -> 48.2 us  [scatter_z(): return lax.psum_scatter(v, 'fsdp', scatter_dimension=0, tiled=True)]
    psum x1, blocking collectives: 576 us -> 38.2 us  [local(): lax.psum(jnp.concatenate([grad_gain_one, grad_gain_two, jnp.sum(grad_q_pr...]
    all_gather x6 -> x3, waiting for transfers between devices: 488 us -> 0.02 us  [gather_z(): return lax.all_gather(v, 'fsdp', axis=0, tiled=True)]
    ppermute x0 -> x44, starting transfers between devices: none -> 103 us  [the longest x30 83.8 us: hop(): return lax.ppermute(v, 'ctx', [(i, i ^ k) for i in range(n_ctx)])]
    ppermute x0 -> x44, waiting for transfers between devices: none -> 99 us  [the longest x30 95.4 us: hop(): return lax.ppermute(v, 'ctx', [(i, i ^ k) for i in range(n_ctx)])]
    all_gather x2, blocking collectives: 25.9 us -> 50.1 us  [gather_z(): return lax.all_gather(v, 'fsdp', axis=0, tiled=True)]
    slice x3 -> x20, local copies, waits for them, and re-layouts: 3.34 us -> 25.6 us  [the longest x2 9.74 us: local(): grad_w_up = d_gu[1]]
    unnamed x2 -> x0, blocking collectives: 20 us -> none
  transfers between devices with their start and end apart: 14 -> 53, of which waited for: 12 -> 25; matrix products, arithmetic and copies ran while one was open for 6% -> 23% of each run, Pallas kernels for 0% -> 0%
where the time goes in v1:
time: 615 us; the launch traced here: 607 us
  waiting for transfers between devices  147 us (24%)
  starting transfers between devices  104 us (17%)
  local copies, waits for them, and re-layouts  100 us (16%)
  matrix products  89 us (14%)
  blocking collectives  88.3 us (14%)
  other arithmetic  51 us (8%)
  between operations  16.3 us (3%)
  loops' own time  11.2 us (2%)
    ppermute x30, waiting for transfers between devices, hop(): return lax.ppermute(v, 'ctx', [(i, i ^ k) for i in range(n_ctx)])  95.4 us
    ppermute x30, starting transfers between devices, hop(): return lax.ppermute(v, 'ctx', [(i, i ^ k) for i in range(n_ctx)])  83.8 us
    all_gather x2, blocking collectives, gather_z(): return lax.all_gather(v, 'fsdp', axis=0, tiled=True)  50.1 us
    reduce_scatter x6, waiting for transfers between devices, scatter_z(): return lax.psum_scatter(v, 'fsdp', scatter_dimension=0, tiled=True)  48.2 us
    psum x1, blocking collectives, local(): lax.psum(jnp.concatenate([grad_gain_one, grad_gain_two, jnp.sum(grad_q_pr...  38.2 us
    unnamed x103, local copies, waits for them, and re-layouts  23.2 us
    dot_general x7, matrix products, contract_rows(): lax.dot_general(left_side, right_side, (((0,), (0,)), ((), ())), preferre...  20 us
    ppermute x14, starting transfers between devices, swap(): return lax.ppermute(v, 'seq', [(0, 1), (1, 0)])  19.2 us
  transfers between devices with their start and end apart: 53, of which 25 were waited for; matrix products, arithmetic and copies ran while one was open for 23% of the time, Pallas kernels for 0%

profile of v1, /device:TPU:1, one launch (start us, length us, event | category | flops | bytes accessed | tf_op | source)
XLA Modules:
  0.0 606.9 jit_solution(6129080322975104950)
XLA Ops:
  17.9 31.1 %all_gather.17 = bf16[896,448]{1,0:T(8,128)(2,1)} all-gather(bf16[224,448]{1,0:T(8,128)(2,1)S(1)} %constant_dynamic-slice_fusion.11), channel_id=1, replica_groups=mesh['seq'=2,'ctx'=4,'fsdp'=4] {'fsdp'}, dimensions={0}, use_global_device_ids=true | all-gather | bytes 1003520 | tf_op jit(solution)/shard_map/all_gather | solution.py:221
  75.4 19.0 %all_gather.16 = bf16[768,256]{1,0:T(8,128)(2,1)S(1)} all-gather(bf16[192,256]{1,0:T(8,128)(2,1)S(1)} %pad_maximum_fusion.15), channel_id=1, replica_groups=mesh['seq'=2,'ctx'=4,'fsdp'=4] {'fsdp'}, dimensions={0}, use_global_device_ids=true | all-gather | bytes 491520 | tf_op jit(solution)/shard_map/all_gather | solution.py:221
  98.6 5.3 collective-permute-done.3
  104.0 9.7 %collective-permute-done.2 = bf16[768,256]{1,0:T(8,128)(2,1)} collective-permute-done((bf16[768,256]{1,0:T(8,128)(2,1)S(1)}, bf16[768,256]{1,0:T(8,128)(2,1)}, u32[]{:S(2)}, u32[]{:S(2)}) %collective-permute-start.2) | collective-permute-done | bytes 393248 | tf_op jit(solution)/shard_map/ppermute | solution.py:218
  121.1 29.9 %while.31 = (s32[]{:T(128)}, f32[2,1344]{1,0:T(2,128)S(1)}, f32[2,1344]{1,0:T(2,128)S(1)}, f32[2,1344,64]{1,2,0:T(8,128)S(1)}, s32[4,768]{1,0:T(4,128)S(1)}, /*i...) while((s32[]{:T(128)}, f32[2,1344]{1,0:T(2,128)S(1)}, ...), condition=%wide.region_8.9_spmd.clone, body=%wide.region_2.8_spmd.clone.sunk | while | flops 556701696 | bytes 31225872 | solution.py:123
  123.1 10.8 %conditional.6 = ((f32[2,1344]{1,0:T(2,128)S(1)}, f32[2,1344]{1,0:T(2,128)S(1)}, f32[2,1344,64]{1,2,0:T(8,128)S(1)})) conditional(s32[]{:T(128)} %convert_element_type.695, (f32[2,1344]{1,0:T(2,128)S(1)}, f32[2,1344]{1,0:T(2,128)S(1)}, f32[2,1344,64]{1,2,0:T(8,128)S(1)}) %tuple.141, (s32[1,768]{1,0:T(1,128)S(1)}, s32[192]{0:T(256)S(1)}, ...), branch_computations={%region_4.4_spmd, %region_5.7_spmd} | conditional | flops 556700928 | bytes 31219492 | solution.py:116
  139.7 10.8 %conditional.6 = ((f32[2,1344]{1,0:T(2,128)S(1)}, f32[2,1344]{1,0:T(2,128)S(1)}, f32[2,1344,64]{1,2,0:T(8,128)S(1)})) conditional(s32[]{:T(128)} %convert_element_type.695, (f32[2,1344]{1,0:T(2,128)S(1)}, f32[2,1344]{1,0:T(2,128)S(1)}, f32[2,1344,64]{1,2,0:T(8,128)S(1)}) %tuple.141, (s32[1,768]{1,0:T(1,128)S(1)}, s32[192]{0:T(256)S(1)}, ...), branch_computations={%region_4.4_spmd, %region_5.7_spmd} | conditional | flops 556700928 | bytes 31219492 | solution.py:116
  155.3 22.9 %collective-permute-start.6 = (bf16[192,896]{1,0:T(8,128)(2,1)S(1)}, bf16[192,896]{1,0:T(8,128)(2,1)}, u32[]{:S(2)}, u32[]{:S(2)}) collective-permute-start(bf16[192,896]{1,0:T(8,128)(2,1)S(1)} %multiply_convert_fusion.6), channel_id=1, source_target_pairs={{0,8},{4,12},{8,0},{12,4},{1,9},{5,13},{9,1},{13,5},{2,10},{6,14},... | collective-permute-start | bytes 1032200 | tf_op jit(solution)/shard_map/ppermute | solution.py:218
  180.6 7.4 %collective-permute-start.14 = (bf16[192,896]{1,0:T(8,128)(2,1)}, bf16[192,896]{1,0:T(8,128)(2,1)}, u32[]{:S(2)}, u32[]{:S(2)}) collective-permute-start(bf16[192,896]{1,0:T(8,128)(2,1)} %bitcast.37), channel_id=1, source_target_pairs={{0,8},{4,12},{8,0},{12,4},{1,9},{5,13},{9,1},{13,5},{2,10},{6,14},... | collective-permute-start | bytes 1032200 | tf_op jit(solution)/shard_map/ppermute | solution.py:218
  217.9 5.1 add_convert_fusion.1
  234.1 9.5 %collective-permute-done.17 = bf16[192,896]{1,0:T(8,128)(2,1)S(1)} collective-permute-done((bf16[192,896]{1,0:T(8,128)(2,1)S(1)}, bf16[192,896]{1,0:T(8,128)(2,1)S(1)}, u32[]{:S(2)}, u32[]{:S(2)}) %collective-permute-start.17) | collective-permute-done | bytes 344096 | tf_op jit(solution)/shard_map/ppermute | solution.py:218
  246.6 9.5 %collective-permute-done.11 = bf16[192,896]{1,0:T(8,128)(2,1)S(1)} collective-permute-done((bf16[192,896]{1,0:T(8,128)(2,1)S(1)}, bf16[192,896]{1,0:T(8,128)(2,1)S(1)}, u32[]{:S(2)}, u32[]{:S(2)}) %collective-permute-start.11) | collective-permute-done | bytes 344096 | tf_op jit(solution)/shard_map/ppermute | solution.py:218
  261.5 34.2 %while.32 = (s32[]{:T(128)}, f32[2,1344,64]{1,2,0:T(8,128)S(1)}, bf16[4,768,256]{2,1,0:T(8,128)(2,1)}, s32[4,768]{1,0:T(4,128)S(1)}, s32[]{:T(128)}, /*index=5*/...) while((s32[]{:T(128)}, f32[2,1344,64]{1,2,0:T(8,128)S(1)}, ...), condition=%wide.region_16.17_spmd.clone, body=%wide.region_12.16_spmd.clone.sunk | while | flops 1341973248 | bytes 45379584 | solution.py:182
  263.4 11.3 %conditional.7 = (f32[2,1344,64]{1,2,0:T(8,128)S(1)}, bf16[1,768,256]{1,2,0:T(8,128)(2,1)S(1)}) conditional(s32[]{:T(128)} %convert_element_type.696, f32[2,1344,64]{1,2,0:T(8,128)S(1)} %get-tuple-element.821, (s32[1,768]{1,0:T(1,128)S(1)}, s32[192]{0:T(256)S(1)}, bf16[4,768,2,64]{1,3,2,0:T(8,128)(2,1)}, s32[]{:T(128)}, ...), branch_computations={%region_14.14_spmd, %region_15.15_spmd} | conditional | flops 1341972480 | bytes 43799828 | solution.py:179
  283.5 11.3 %conditional.7 = (f32[2,1344,64]{1,2,0:T(8,128)S(1)}, bf16[1,768,256]{1,2,0:T(8,128)(2,1)S(1)}) conditional(s32[]{:T(128)} %convert_element_type.696, f32[2,1344,64]{1,2,0:T(8,128)S(1)} %get-tuple-element.821, (s32[1,768]{1,0:T(1,128)S(1)}, s32[192]{0:T(256)S(1)}, bf16[4,768,2,64]{1,3,2,0:T(8,128)(2,1)}, s32[]{:T(128)}, ...), branch_computations={%region_14.14_spmd, %region_15.15_spmd} | conditional | flops 1341972480 | bytes 43799828 | solution.py:179
  298.0 23.2 %collective-permute-start.20 = (bf16[768,256]{1,0:T(8,128)(2,1)}, bf16[768,256]{1,0:T(8,128)(2,1)}, u32[]{:S(2)}, u32[]{:S(2)}) collective-permute-start(bf16[768,256]{1,0:T(8,128)(2,1)} %get-tuple-element.546), channel_id=1, source_target_pairs={{0,8},{4,12},{8,0},{12,4},{1,9},{5,13},{9,1},{13,5},{2,10},{6,14},... | collective-permute-start | bytes 1179656 | tf_op jit(solution)/shard_map/ppermute | solution.py:218
  323.2 14.7 %collective-permute-done.20 = bf16[768,256]{1,0:T(8,128)(2,1)} collective-permute-done((bf16[768,256]{1,0:T(8,128)(2,1)}, bf16[768,256]{1,0:T(8,128)(2,1)}, u32[]{:S(2)}, u32[]{:S(2)}) %collective-permute-start.20) | collective-permute-done | bytes 393248 | tf_op jit(solution)/shard_map/ppermute | solution.py:218
  345.7 15.4 %reduce-scatter.7.cloned.1.call-done = bf16[192,256]{1,0:T(8,128)(2,1)} async-done(((bf16[768,256]{1,0:T(8,128)(2,1)}), bf16[192,256]{1,0:T(8,128)(2,1)}) %reduce-scatter.7.cloned.1.call-update) | async-done | bytes 98320 | tf_op jit(solution)/shard_map/reduce_scatter | solution.py:224
  393.3 5.4 add_convert_fusion
  403.2 38.2 %psum.7 = f32[2944]{0:T(1024)S(1)} all-reduce(f32[2944]{0:T(1024)S(1)} %constant_dynamic-update-slice_fusion.12), channel_id=1, replica_groups=mesh['seq'=2,'ctx'=4,'fsdp'=4] {'seq','ctx','fsdp'}, use_global_device_ids=true, to_apply=%region_24.25 | all-reduce | flops 2944 | bytes 23552 | tf_op jit(solution)/shard_map/psum | solution.py:476
  451.5 4.7 collective-permute-done.23
  462.7 7.2 %reduce-scatter.17.cloned.1.call-done = bf16[160,896]{1,0:T(8,128)(2,1)} async-done(((bf16[640,896]{1,0:T(8,128)(2,1)}), bf16[160,896]{1,0:T(8,128)(2,1)}) %reduce-scatter.17.cloned.1.call-update) | async-done | bytes 286736 | tf_op jit(solution)/shard_map/reduce_scatter | solution.py:224
  478.5 6.2 %collective-permute-done.42 = bf16[160,896]{1,0:T(8,128)(2,1)S(1)} collective-permute-done((bf16[160,896]{1,0:T(8,128)(2,1)}, bf16[160,896]{1,0:T(8,128)(2,1)S(1)}, u32[]{:S(2)}, u32[]{:S(2)}) %collective-permute-start.42) | collective-permute-done | bytes 286752 | tf_op jit(solution)/shard_map/ppermute | solution.py:218
  493.0 25.5 %reduce-scatter.15.cloned.1.call-done = bf16[224,1280]{1,0:T(8,128)(2,1)} async-done(((bf16[896,1280]{1,0:T(8,128)(2,1)}), bf16[224,1280]{1,0:T(8,128)(2,1)}) %reduce-scatter.15.cloned.1.call-update) | async-done | bytes 573456 | tf_op jit(solution)/shard_map/reduce_scatter | solution.py:224
  533.4 12.4 %collective-permute-done.37 = bf16[224,1280]{1,0:T(8,128)(2,1)} collective-permute-done((bf16[224,1280]{1,0:T(8,128)(2,1)}, bf16[224,1280]{1,0:T(8,128)(2,1)}, u32[]{:S(2)}, u32[]{:S(2)}) %collective-permute-start.37) | collective-permute-done | bytes 573472 | tf_op jit(solution)/shard_map/ppermute | solution.py:218
  557.7 5.3 gather_fusion
  563.0 7.6 %copy.301 = bf16[8,224,1280]{1,2,0:T(8,128)(2,1)} copy(bf16[8,224,1280]{2,1,0:T(8,128)(2,1)} %gather_fusion) | data formatting | bytes 9175040 | tf_op jit(solution)/shard_map/jit(_take)/gather | solution.py:375
  573.7 4.6 fusion.112
  578.3 5.1 copy.302
  583.4 5.6 copy.304
  589.0 5.2 copy.303
  594.2 5.7 copy.305
  (423 shorter events, 267.8 us)
Async XLA Ops:
  7.2 54.1 %all-gather.9.cloned.1.call-start = ((), (), s32[]{:S(2)}) async-start(), calls=%async_computation.14 | async-start | bytes 1474560 | tf_op jit(solution)/shard_map/all_gather | solution.py:221
  14.3 165.0 %all-gather.5.cloned.1.call-start = ((), (), s32[]{:S(2)}) async-start(), calls=%async_computation.6 | async-start | bytes 2867200 | tf_op jit(solution)/shard_map/all_gather | solution.py:221
  17.7 177.6 %all-gather.7.cloned.1.call-start = ((), (), s32[]{:S(2)}) async-start(), calls=%async_computation.7 | async-start | bytes 1433600 | tf_op jit(solution)/shard_map/all_gather | solution.py:221
  51.2 16.6 %collective-permute-start.4 = (bf16[896,448]{0,1:T(8,128)(2,1)}, bf16[896,448]{0,1:T(8,128)(2,1)}, u32[]{:S(2)}, u32[]{:S(2)}) collective-permute-start(bf16[896,448]{0,1:T(8,128)(2,1)} %copy.277), channel_id=1, source_target_pairs={{0,16},{16,0},{1,17},{17,1},{2,18},{18,2},{3,19},{19,3},{4,20},{20... | collective-permute-start | bytes 2408456 | tf_op jit(solution)/shard_map/ppermute | solution.py:213
  55.1 145.2 %collective-permute-start.15 = (bf16[192,896]{1,0:T(8,128)(2,1)}, bf16[192,896]{1,0:T(8,128)(2,1)}, u32[]{:S(2)}, u32[]{:S(2)}) collective-permute-start(bf16[192,896]{1,0:T(8,128)(2,1)} %bitcast.37), channel_id=1, source_target_pairs={{0,12},{4,8},{8,4},{12,0},{1,13},{5,9},{9,5},{13,1},{2,14},{6,10},... | collective-permute-start | bytes 1032200 | tf_op jit(solution)/shard_map/ppermute | solution.py:218
  58.0 303.1 %reduce-scatter.7.cloned.1.call-start = ((), (), s32[]{:S(2)}) async-start(), calls=%async_computation.8 | async-start | bytes 491520 | tf_op jit(solution)/shard_map/reduce_scatter | solution.py:224
  94.8 18.9 %collective-permute-start.2 = (bf16[768,256]{1,0:T(8,128)(2,1)S(1)}, bf16[768,256]{1,0:T(8,128)(2,1)}, u32[]{:S(2)}, u32[]{:S(2)}) collective-permute-start(bf16[768,256]{1,0:T(8,128)(2,1)S(1)} %all_gather.16), channel_id=1, source_target_pairs={{0,8},{4,12},{8,0},{12,4},{1,9},{5,13},{9,1},{13,5},{2,10},{6,14},... | collective-permute-start | bytes 1179656 | tf_op jit(solution)/shard_map/ppermute | solution.py:218
  95.7 17.9 %collective-permute-start.1 = (bf16[768,256]{1,0:T(8,128)(2,1)S(1)}, bf16[768,256]{1,0:T(8,128)(2,1)}, u32[]{:S(2)}, u32[]{:S(2)}) collective-permute-start(bf16[768,256]{1,0:T(8,128)(2,1)S(1)} %all_gather.16), channel_id=1, source_target_pairs={{0,4},{4,0},{8,12},{12,8},{1,5},{5,1},{9,13},{13,9},{2,6},{6,2},{1... | collective-permute-start | bytes 1179656 | tf_op jit(solution)/shard_map/ppermute | solution.py:218
  155.2 25.4 %collective-permute-start.7 = (bf16[192,896]{1,0:T(8,128)(2,1)S(1)}, bf16[192,896]{1,0:T(8,128)(2,1)S(1)}, u32[]{:S(2)}, u32[]{:S(2)}) collective-permute-start(bf16[192,896]{1,0:T(8,128)(2,1)S(1)} %multiply_convert_fusion.6), channel_id=1, source_target_pairs={{0,12},{4,8},{8,4},{12,0},{1,13},{5,9},{9,5},{13,1},{2,14},{6,10},... | collective-permute-start | bytes 1032200 | tf_op jit(solution)/shard_map/ppermute | solution.py:218
  155.3 37.2 %collective-permute-start.6 = (bf16[192,896]{1,0:T(8,128)(2,1)S(1)}, bf16[192,896]{1,0:T(8,128)(2,1)}, u32[]{:S(2)}, u32[]{:S(2)}) collective-permute-start(bf16[192,896]{1,0:T(8,128)(2,1)S(1)} %multiply_convert_fusion.6), channel_id=1, source_target_pairs={{0,8},{4,12},{8,0},{12,4},{1,9},{5,13},{9,1},{13,5},{2,10},{6,14},... | collective-permute-start | bytes 1032200 | tf_op jit(solution)/shard_map/ppermute | solution.py:218
  178.2 17.1 %collective-permute-start.5 = (bf16[192,896]{1,0:T(8,128)(2,1)S(1)}, bf16[192,896]{1,0:T(8,128)(2,1)}, u32[]{:S(2)}, u32[]{:S(2)}) collective-permute-start(bf16[192,896]{1,0:T(8,128)(2,1)S(1)} %multiply_convert_fusion.6), channel_id=1, source_target_pairs={{0,4},{4,0},{8,12},{12,8},{1,5},{5,1},{9,13},{13,9},{2,6},{6,2},{1... | collective-permute-start | bytes 1032200 | tf_op jit(solution)/shard_map/ppermute | solution.py:218
  179.3 31.4 %collective-permute-start.8 = (bf16[896,1280]{1,0:T(8,128)(2,1)}, bf16[896,1280]{1,0:T(8,128)(2,1)}, u32[]{:S(2)}, u32[]{:S(2)}) collective-permute-start(bf16[896,1280]{1,0:T(8,128)(2,1)} %all-gather.5.cloned.1.call-done), channel_id=1, source_target_pairs={{0,16},{16,0},{1,17},{17,1},{2,18},{18,2},{3,19},{19,3},{4,20},{20... | collective-permute-start | bytes 6881288 | tf_op jit(solution)/shard_map/ppermute | solution.py:213
  180.6 19.6 %collective-permute-start.14 = (bf16[192,896]{1,0:T(8,128)(2,1)}, bf16[192,896]{1,0:T(8,128)(2,1)}, u32[]{:S(2)}, u32[]{:S(2)}) collective-permute-start(bf16[192,896]{1,0:T(8,128)(2,1)} %bitcast.37), channel_id=1, source_target_pairs={{0,8},{4,12},{8,0},{12,4},{1,9},{5,13},{9,1},{13,5},{2,10},{6,14},... | collective-permute-start | bytes 1032200 | tf_op jit(solution)/shard_map/ppermute | solution.py:218
  195.3 19.5 %collective-permute-start.9 = (bf16[640,896]{1,0:T(8,128)(2,1)}, bf16[640,896]{1,0:T(8,128)(2,1)S(1)}, u32[]{:S(2)}, u32[]{:S(2)}) collective-permute-start(bf16[640,896]{1,0:T(8,128)(2,1)} %all-gather.7.cloned.1.call-done), channel_id=1, source_target_pairs={{0,16},{16,0},{1,17},{17,1},{2,18},{18,2},{3,19},{19,3},{4,20},{20... | collective-permute-start | bytes 3440648 | tf_op jit(solution)/shard_map/ppermute | solution.py:213
  223.2 20.5 %collective-permute-start.17 = (bf16[192,896]{1,0:T(8,128)(2,1)S(1)}, bf16[192,896]{1,0:T(8,128)(2,1)S(1)}, u32[]{:S(2)}, u32[]{:S(2)}) collective-permute-start(bf16[192,896]{1,0:T(8,128)(2,1)S(1)} %get-tuple-element.552), channel_id=1, source_target_pairs={{0,8},{4,12},{8,0},{12,4},{1,9},{5,13},{9,1},{13,5},{2,10},{6,14},... | collective-permute-start | bytes 1032200 | tf_op jit(solution)/shard_map/ppermute | solution.py:218
  226.2 17.4 %collective-permute-start.16 = (bf16[192,896]{1,0:T(8,128)(2,1)S(1)}, bf16[192,896]{1,0:T(8,128)(2,1)S(1)}, u32[]{:S(2)}, u32[]{:S(2)}) collective-permute-start(bf16[192,896]{1,0:T(8,128)(2,1)S(1)} %get-tuple-element.550), channel_id=1, source_target_pairs={{0,4},{4,0},{8,12},{12,8},{1,5},{5,1},{9,13},{13,9},{2,6},{6,2},{1... | collective-permute-start | bytes 1032200 | tf_op jit(solution)/shard_map/ppermute | solution.py:218
  227.7 19.0 %collective-permute-start.12 = (bf16[192,896]{1,0:T(8,128)(2,1)S(1)}, bf16[192,896]{1,0:T(8,128)(2,1)S(1)}, u32[]{:S(2)}, u32[]{:S(2)}) collective-permute-start(bf16[192,896]{1,0:T(8,128)(2,1)S(1)} %get-tuple-element.554), channel_id=1, source_target_pairs={{0,12},{4,8},{8,4},{12,0},{1,13},{5,9},{9,5},{13,1},{2,14},{6,10},... | collective-permute-start | bytes 1032200 | tf_op jit(solution)/shard_map/ppermute | solution.py:218
  228.9 27.3 %collective-permute-start.11 = (bf16[192,896]{1,0:T(8,128)(2,1)S(1)}, bf16[192,896]{1,0:T(8,128)(2,1)S(1)}, u32[]{:S(2)}, u32[]{:S(2)}) collective-permute-start(bf16[192,896]{1,0:T(8,128)(2,1)S(1)} %get-tuple-element.555), channel_id=1, source_target_pairs={{0,8},{4,12},{8,0},{12,4},{1,9},{5,13},{9,1},{13,5},{2,10},{6,14},... | collective-permute-start | bytes 1032200 | tf_op jit(solution)/shard_map/ppermute | solution.py:218
  231.8 24.3 %collective-permute-start.10 = (bf16[192,896]{1,0:T(8,128)(2,1)S(1)}, bf16[192,896]{1,0:T(8,128)(2,1)S(1)}, u32[]{:S(2)}, u32[]{:S(2)}) collective-permute-start(bf16[192,896]{1,0:T(8,128)(2,1)S(1)} %get-tuple-element.553), channel_id=1, source_target_pairs={{0,4},{4,0},{8,12},{12,8},{1,5},{5,1},{9,13},{13,9},{2,6},{6,2},{1... | collective-permute-start | bytes 1032200 | tf_op jit(solution)/shard_map/ppermute | solution.py:218
  298.0 25.3 %collective-permute-start.21 = (bf16[768,256]{1,0:T(8,128)(2,1)}, bf16[768,256]{1,0:T(8,128)(2,1)}, u32[]{:S(2)}, u32[]{:S(2)}) collective-permute-start(bf16[768,256]{1,0:T(8,128)(2,1)} %get-tuple-element.547), channel_id=1, source_target_pairs={{0,12},{4,8},{8,4},{12,0},{1,13},{5,9},{9,5},{13,1},{2,14},{6,10},... | collective-permute-start | bytes 1179656 | tf_op jit(solution)/shard_map/ppermute | solution.py:218
  298.0 40.0 %collective-permute-start.20 = (bf16[768,256]{1,0:T(8,128)(2,1)}, bf16[768,256]{1,0:T(8,128)(2,1)}, u32[]{:S(2)}, u32[]{:S(2)}) collective-permute-start(bf16[768,256]{1,0:T(8,128)(2,1)} %get-tuple-element.546), channel_id=1, source_target_pairs={{0,8},{4,12},{8,0},{12,4},{1,9},{5,13},{9,1},{13,5},{2,10},{6,14},... | collective-permute-start | bytes 1179656 | tf_op jit(solution)/shard_map/ppermute | solution.py:218
  321.2 18.7 %collective-permute-start.19 = (bf16[768,256]{1,0:T(8,128)(2,1)S(1)}, bf16[768,256]{1,0:T(8,128)(2,1)}, u32[]{:S(2)}, u32[]{:S(2)}) collective-permute-start(bf16[768,256]{1,0:T(8,128)(2,1)S(1)} %get-tuple-element.545), channel_id=1, source_target_pairs={{0,4},{4,0},{8,12},{12,8},{1,5},{5,1},{9,13},{13,9},{2,6},{6,2},{1... | collective-permute-start | bytes 1179656 | tf_op jit(solution)/shard_map/ppermute | solution.py:218
  342.2 59.8 %reduce-scatter.11.cloned.1.call-start = ((), (), s32[]{:S(2)}) async-start(), calls=%async_computation.10 | async-start | bytes 286720 | tf_op jit(solution)/shard_map/reduce_scatter | solution.py:224
  344.4 26.7 %collective-permute-start.22 = (bf16[4,112,896]{2,1,0:T(8,128)(2,1)}, bf16[4,112,896]{2,1,0:T(8,128)(2,1)}, u32[]{:S(2)}, u32[]{:S(2)}) collective-permute-start(bf16[4,112,896]{2,1,0:T(8,128)(2,1)} %dynamic-slice_bitcast_fusion.1), channel_id=1, source_target_pairs={{0,16},{16,0},{1,17},{17,1},{2,18},{18,2},{3,19},{19,3},{4,20},{20... | collective-permute-start | bytes 2408456 | tf_op jit(solution)/shard_map/ppermute | solution.py:213
  371.0 78.0 %reduce-scatter.9.cloned.1.call-start = ((), (), s32[]{:S(2)}) async-start(), calls=%async_computation.9 | async-start | bytes 1003520 | tf_op jit(solution)/shard_map/reduce_scatter | solution.py:224
  373.3 78.2 %reduce-scatter.13.cloned.1.call-start = ((), (), s32[]{:S(2)}) async-start(), calls=%async_computation.11 | async-start | bytes 1003520 | tf_op jit(solution)/shard_map/reduce_scatter | solution.py:224
  378.9 91.1 %reduce-scatter.17.cloned.1.call-start = ((), (), s32[]{:S(2)}) async-start(), calls=%async_computation.13 | async-start | bytes 1433600 | tf_op jit(solution)/shard_map/reduce_scatter | solution.py:224
  390.6 128.0 %reduce-scatter.15.cloned.1.call-start = ((), (), s32[]{:S(2)}) async-start(), calls=%async_computation.12 | async-start | bytes 2867200 | tf_op jit(solution)/shard_map/reduce_scatter | solution.py:224
  402.0 39.4 %collective-permute-start.27 = (bf16[112,256]{1,0:T(8,128)(2,1)}, bf16[112,256]{1,0:T(8,128)(2,1)S(1)}, u32[]{:S(2)}, u32[]{:S(2)}) collective-permute-start(bf16[112,256]{1,0:T(8,128)(2,1)} %reduce-scatter.11.cloned.1.call-done), channel_id=1, source_target_pairs={{0,4},{4,0},{8,12},{12,8},{1,5},{5,1},{9,13},{13,9},{2,6},{6,2},{1... | collective-permute-start | bytes 172040 | tf_op jit(solution)/shard_map/ppermute | solution.py:218
  472.6 16.3 %collective-permute-start.25 = (bf16[112,896]{1,0:T(8,128)(2,1)S(1)}, bf16[112,896]{1,0:T(8,128)(2,1)S(1)}, u32[]{:S(2)}, u32[]{:S(2)}) collective-permute-start(bf16[112,896]{1,0:T(8,128)(2,1)S(1)} %add_convert_fusion.8), channel_id=1, source_target_pairs={{0,16},{16,0},{1,17},{17,1},{2,18},{18,2},{3,19},{19,3},{4,20},{20... | collective-permute-start | bytes 602120 | tf_op jit(solution)/shard_map/ppermute | solution.py:213
  487.0 35.0 %collective-permute-start.43 = (bf16[4,160,896]{2,1,0:T(8,128)(2,1)}, bf16[4,160,896]{2,1,0:T(8,128)(2,1)}, u32[]{:S(2)}, u32[]{:S(2)}) collective-permute-start(bf16[4,160,896]{2,1,0:T(8,128)(2,1)} %pad_maximum_fusion.11), channel_id=1, source_target_pairs={{0,16},{16,0},{1,17},{17,1},{2,18},{18,2},{3,19},{19,3},{4,20},{20... | collective-permute-start | bytes 3440648 | tf_op jit(solution)/shard_map/ppermute | solution.py:213
  521.0 24.8 %collective-permute-start.37 = (bf16[224,1280]{1,0:T(8,128)(2,1)}, bf16[224,1280]{1,0:T(8,128)(2,1)}, u32[]{:S(2)}, u32[]{:S(2)}) collective-permute-start(bf16[224,1280]{1,0:T(8,128)(2,1)} %reduce-scatter.15.cloned.1.call-done), channel_id=1, source_target_pairs={{0,12},{4,8},{8,4},{12,0},{1,13},{5,9},{9,5},{13,1},{2,14},{6,10},... | collective-permute-start | bytes 1720328 | tf_op jit(solution)/shard_map/ppermute | solution.py:218
  (62 other events, 708.3 us)
Sparse Core Ops, SparseCore 0:
  14.4 43.8 all-gather.8
  60.4 54.8 all-gather.4
  116.9 28.1 all-gather.6
  342.3 18.7 reduce-scatter.6
  371.1 15.2 reduce-scatter.10
  389.1 23.3 reduce-scatter.8
  415.4 23.2 reduce-scatter.12
  441.6 28.3 reduce-scatter.16
  472.8 45.7 reduce-scatter.14

commit v2 on v1

v2 whole, which is shorter than its diff:
```python
import functools
import math

import jax
import jax.numpy as jnp
from jax import lax
from jax.experimental import pallas as pl
from jax.experimental.pallas import tpu as pltpu
from jax.sharding import PartitionSpec as P

HEADS = 14
KV_HEADS = 2
HEAD = 64
GROUP = HEADS // KV_HEADS
NORM_EPS = 1e-06
ROPE_BASE = 1000000.0
MASKED = -1e30
BF16 = jnp.bfloat16
F32 = jnp.float32


def rope_tables(positions, head_dim):
    half_dim = head_dim // 2
    inverse = jnp.exp(
        jnp.arange(half_dim, dtype=jnp.float32) * (-math.log(ROPE_BASE) * 2.0 / head_dim)
    )
    angles = positions.astype(jnp.float32)[:, None] * inverse[None, :]
    return (jnp.cos(angles)[:, None, :], jnp.sin(angles)[:, None, :])


def rotate(values, cosine_table, sine_table):
    half_dim = values.shape[-1] // 2
    front_half = values[..., :half_dim]
    back_half = values[..., half_dim:]
    return jnp.concatenate(
        [
            front_half * cosine_table - back_half * sine_table,
            back_half * cosine_table + front_half * sine_table,
        ],
        -1,
    )


def matmul(left_side, right_side):
    return jnp.dot(left_side, right_side, preferred_element_type=F32)


def contract_rows(left_side, right_side):
    return lax.dot_general(
        left_side, right_side, (((0,), (0,)), ((), ())), preferred_element_type=F32
    )


def times_transposed(left_side, right_side):
    return lax.dot_general(
        left_side, right_side, (((1,), (1,)), ((), ())), preferred_element_type=F32
    )


def rms_forward(values, gain_vec):
    inv_scale = lax.rsqrt(jnp.mean(values * values, -1, keepdims=True) + NORM_EPS)
    normed = values * inv_scale
    return (normed, inv_scale, (normed * gain_vec).astype(BF16))


def rms_backward(grad_out, normed, inv_scale, gain_vec):
    gain_grad = jnp.sum(grad_out * normed, 0)
    scaled = grad_out * gain_vec
    grad_in = inv_scale * (scaled - normed * jnp.mean(scaled * normed, -1, keepdims=True))
    return (grad_in, gain_grad)


def cut_heads(ref, head):
    tile = ref[:, (head // 2) * 128 : (head // 2 + 1) * 128].astype(F32)
    group = head // GROUP
    if head % 2 != group:
        tile = jnp.concatenate([tile[:, HEAD:], tile[:, :HEAD]], 1)
    lane = lax.broadcasted_iota(jnp.int32, tile.shape, 1)
    return jnp.where((lane >= HEAD) if group else (lane < HEAD), tile, 0.0)


def split_lanes(column, shape):
    high = column.astype(BF16).astype(F32)
    mid = (column - high).astype(BF16).astype(F32)
    low = column - high - mid
    lane = lax.broadcasted_iota(jnp.int32, shape, 1)
    return jnp.where(
        lane == 0, high, jnp.where(lane == 1, mid, jnp.where(lane == 2, low, 0.0))
    ).astype(BF16)


def piece_shift(at, zed, tokens_here, keys_here):
    pieces = keys_here // tokens_here
    shift = jnp.zeros(at.shape, jnp.int32)
    for k in range(pieces):
        here = (jnp.bitwise_xor(zed, k) - k - zed) * tokens_here
        shift = jnp.where(at >= k * tokens_here, here, shift)
    return shift


def forward_kernel(info_ref, q_ref, kv_ref, att_ref, qext_ref, top_ref, acc_ref):
    step = pl.program_id(0)
    last = pl.num_programs(0) - 1
    tokens_here = q_ref.shape[0]
    keys_here = kv_ref.shape[1]
    own = info_ref[0]
    zed = info_ref[1]
    block = info_ref[2 + step]

    @pl.when(step == 0)
    def _():
        for h in range(HEADS):
            qext_ref[h * tokens_here : (h + 1) * tokens_here, :128] = cut_heads(q_ref, h).astype(
                BF16
            )
        top_ref[...] = jnp.full(top_ref.shape, MASKED, F32)
        acc_ref[...] = jnp.zeros(acc_ref.shape, F32)

    def attend(masked):
        keys = kv_ref[0, :, :128]
        values = jnp.concatenate(
            [kv_ref[0, :, 128:], jnp.ones((keys_here, 128), BF16)], 1
        )
        if masked:
            row = lax.broadcasted_iota(jnp.int32, (tokens_here, keys_here), 0)
            col = lax.broadcasted_iota(jnp.int32, (tokens_here, keys_here), 1)
            allowed = col + piece_shift(col, zed, tokens_here, keys_here) <= row
        for h in range(HEADS):
            rows = slice(h * tokens_here, (h + 1) * tokens_here)
            scores = times_transposed(qext_ref[rows, :128], keys)
            if masked:
                scores = jnp.where(allowed, scores, MASKED)
            old = top_ref[rows, :]
            top = jnp.maximum(old, jnp.max(scores, -1, keepdims=True))
            probs = jnp.exp(scores - top[:, :1]).astype(BF16)
            shrink = jnp.exp(old - top)
            top_ref[rows, :] = top
            acc_ref[rows, :] = acc_ref[rows, :] * jnp.concatenate([shrink, shrink], 1) + matmul(
                probs, values
            )

    @pl.when(block == own)
    def _():
        attend(True)

    @pl.when(block < own)
    def _():
        attend(False)

    @pl.when(step == last)
    def _():
        lane = lax.broadcasted_iota(jnp.int32, (tokens_here, 128), 1)
        for pair in range(HEADS // 2):
            outs = []
            for h in (2 * pair, 2 * pair + 1):
                rows = slice(h * tokens_here, (h + 1) * tokens_here)
                total = acc_ref[rows, 128:]
                out = acc_ref[rows, :128] / total
                if h // GROUP != h % 2:
                    out = jnp.concatenate([out[:, HEAD:], out[:, :HEAD]], 1)
                outs.append(out)
                log_total = top_ref[rows, :] + jnp.log(total)
                qext_ref[rows, 128:] = split_lanes(-log_total, (tokens_here, 128))
            att_ref[:, pair * 128 : (pair + 1) * 128] = jnp.where(
                lane < HEAD, outs[0], outs[1]
            ).astype(BF16)


def backward_kernel(
    info_ref, qext_ref, do_ref, att_ref, kv_ref, dq_ref, dkv_ref, doext_ref, dqt_ref
):
    step = pl.program_id(0)
    last = pl.num_programs(0) - 1
    tokens_here = do_ref.shape[0]
    keys_here = kv_ref.shape[1]
    own = info_ref[0]
    zed = info_ref[1]
    block = info_ref[2 + step]
    span = 2 * tokens_here

    @pl.when(step == 0)
    def _():
        for h in range(HEADS):
            rows = slice(h * tokens_here, (h + 1) * tokens_here)
            grad = cut_heads(do_ref, h)
            delta = jnp.sum(grad * cut_heads(att_ref, h), -1, keepdims=True)
            doext_ref[rows, :128] = grad.astype(BF16)
            doext_ref[rows, 128:] = split_lanes(-delta, (tokens_here, 128))
        dqt_ref[...] = jnp.zeros(dqt_ref.shape, F32)

    def attend(masked):
        lane = lax.broadcasted_iota(jnp.int32, (keys_here, 128), 1)
        ones = jnp.where(lane < 3, 1.0, 0.0).astype(BF16)
        keys = kv_ref[0, :, :128]
        keys_ext = jnp.concatenate([keys, ones], 1)
        values_ext = jnp.concatenate([kv_ref[0, :, 128:], ones], 1)
        keys_t = keys.astype(F32).T.astype(BF16)
        if masked:
            row = lax.broadcasted_iota(jnp.int32, (keys_here, tokens_here), 0)
            col = lax.broadcasted_iota(jnp.int32, (keys_here, tokens_here), 1)
            allowed = row + piece_shift(row, zed, tokens_here, keys_here) <= col
            allowed = allowed.astype(F32)
            allowed = jnp.concatenate([allowed, allowed], 1) > 0.5
        dk = jnp.zeros((keys_here, 128), F32)
        dv = jnp.zeros((keys_here, 128), F32)
        for pair in range(HEADS // 2):
            rows = slice(pair * span, (pair + 1) * span)
            probs = jnp.exp(times_transposed(keys_ext, qext_ref[rows, :]))
            if masked:
                probs = jnp.where(allowed, probs, 0.0)
            slope = (probs * times_transposed(values_ext, doext_ref[rows, :])).astype(BF16)
            dv = dv + matmul(probs.astype(BF16), doext_ref[rows, :128])
            dk = dk + matmul(slope, qext_ref[rows, :128])
            dqt_ref[pair] = dqt_ref[pair] + matmul(keys_t, slope)
        dkv_ref[0] = jnp.concatenate([dk, dv], 1).astype(BF16)

    @pl.when(block == own)
    def _():
        attend(True)

    @pl.when(block < own)
    def _():
        attend(False)

    @pl.when(block > own)
    def _():
        dkv_ref[...] = jnp.zeros(dkv_ref.shape, BF16)

    @pl.when(step == last)
    def _():
        lane = lax.broadcasted_iota(jnp.int32, (tokens_here, 128), 1)
        for pair in range(HEADS // 2):
            turned = dqt_ref[pair].T
            outs = []
            for j in range(2):
                h = 2 * pair + j
                out = turned[j * tokens_here : (j + 1) * tokens_here]
                if h // GROUP != j:
                    out = jnp.concatenate([out[:, HEAD:], out[:, :HEAD]], 1)
                outs.append(out)
            dq_ref[:, pair * 128 : (pair + 1) * 128] = (
                jnp.where(lane < HEAD, outs[0], outs[1]) * HEAD ** (-0.5)
            )


def whole_spec(shape):
    return pl.BlockSpec(shape, lambda i, info: (0,) * len(shape))


def attend_forward(info, queries, kv):
    blocks, block_len, kv_width = kv.shape
    tokens_here, q_width = queries.shape
    rows = HEADS * tokens_here
    return pl.pallas_call(
        forward_kernel,
        grid_spec=pltpu.PrefetchScalarGridSpec(
            num_scalar_prefetch=1,
            grid=(blocks,),
            in_specs=[
                whole_spec((tokens_here, q_width)),
                pl.BlockSpec((1, block_len, kv_width), lambda i, info: (i, 0, 0)),
            ],
            out_specs=[whole_spec((tokens_here, q_width)), whole_spec((rows, 256))],
            scratch_shapes=[pltpu.VMEM((rows, 128), F32), pltpu.VMEM((rows, 256), F32)],
        ),
        out_shape=[
            jax.ShapeDtypeStruct((tokens_here, q_width), BF16),
            jax.ShapeDtypeStruct((rows, 256), BF16),
        ],
        compiler_params=pltpu.CompilerParams(
            dimension_semantics=("arbitrary",), vmem_limit_bytes=40 * 2**20
        ),
        cost_estimate=pl.CostEstimate(
            flops=4 * rows * blocks * block_len * 256,
            bytes_accessed=6 * 2**20,
            transcendentals=rows * blocks * block_len,
        ),
        name="attend_forward",
    )(info, queries, kv)


def attend_backward(info, queries_ext, grad_att, attended, kv):
    blocks, block_len, kv_width = kv.shape
    tokens_here, q_width = grad_att.shape
    rows = HEADS * tokens_here
    return pl.pallas_call(
        backward_kernel,
        grid_spec=pltpu.PrefetchScalarGridSpec(
            num_scalar_prefetch=1,
            grid=(blocks,),
            in_specs=[
                whole_spec((rows, 256)),
                whole_spec((tokens_here, q_width)),
                whole_spec((tokens_here, q_width)),
                pl.BlockSpec((1, block_len, kv_width), lambda i, info: (i, 0, 0)),
            ],
            out_specs=[
                whole_spec((tokens_here, q_width)),
                pl.BlockSpec((1, block_len, kv_width), lambda i, info: (i, 0, 0)),
            ],
            scratch_shapes=[
                pltpu.VMEM((rows, 256), BF16),
                pltpu.VMEM((HEADS // 2, 128, 2 * tokens_here), F32),
            ],
        ),
        out_shape=[
            jax.ShapeDtypeStruct((tokens_here, q_width), F32),
            jax.ShapeDtypeStruct(kv.shape, BF16),
        ],
        compiler_params=pltpu.CompilerParams(
            dimension_semantics=("arbitrary",), vmem_limit_bytes=40 * 2**20
        ),
        cost_estimate=pl.CostEstimate(
            flops=10 * rows * blocks * block_len * 256,
            bytes_accessed=8 * 2**20,
            transcendentals=rows * blocks * block_len,
        ),
        name="attend_backward",
    )(info, queries_ext, grad_att, attended, kv)


def spread_columns_kernel(n_z, where_ref, *refs):
    pieces, (gate_ref, up_ref, held) = refs[:-3], refs[-3:]
    n_part = len(pieces)
    for r in range(n_part):
        held[where_ref[r]] = pieces[r][...].astype(F32)
    half = held.shape[2] // 2
    pad = half // n_z
    piece = gate_ref.shape[1] // (n_z * n_part)
    for out, start in ((gate_ref, 0), (up_ref, half)):
        cuts = []
        for j in range(n_z):
            for e in range(n_part):
                cuts.append(held[e, :, start + j * pad : start + j * pad + piece])
        out[...] = jnp.concatenate(cuts, 1)


def spread_columns(where_at, pieces, n_z, ff):
    rows, cols = pieces[0].shape
    tile = 32
    n_part = len(pieces)
    return pl.pallas_call(
        functools.partial(spread_columns_kernel, n_z),
        grid_spec=pltpu.PrefetchScalarGridSpec(
            num_scalar_prefetch=1,
            grid=(rows // tile,),
            in_specs=[pl.BlockSpec((tile, cols), lambda i, w: (i, 0))] * n_part,
            out_specs=[pl.BlockSpec((tile, ff), lambda i, w: (i, 0))] * 2,
            scratch_shapes=[pltpu.VMEM((n_part, tile, cols), F32)],
        ),
        out_shape=[jax.ShapeDtypeStruct((rows, ff), F32)] * 2,
        compiler_params=pltpu.CompilerParams(
            dimension_semantics=("arbitrary",), vmem_limit_bytes=40 * 2**20
        ),
        cost_estimate=pl.CostEstimate(
            flops=0, bytes_accessed=rows * ff * 12, transcendentals=0
        ),
        name="spread_columns",
    )(where_at, *pieces)


def spread_rows_kernel(where_ref, *refs):
    pieces, out_ref = refs[:-1], refs[-1]
    piece = out_ref.shape[0] // len(pieces)
    for r in range(len(pieces)):
        start = pl.multiple_of(where_ref[r] * piece, 8)
        out_ref[pl.ds(start, piece), :] = pieces[r][...].astype(F32)[:piece]


def spread_rows(where_at, pieces, rows_out):
    rows, cols = pieces[0].shape
    tile = 128
    return pl.pallas_call(
        spread_rows_kernel,
        grid_spec=pltpu.PrefetchScalarGridSpec(
            num_scalar_prefetch=1,
            grid=(cols // tile,),
            in_specs=[pl.BlockSpec((rows, tile), lambda i, w: (0, i))] * len(pieces),
            out_specs=pl.BlockSpec((rows_out, tile), lambda i, w: (0, i)),
        ),
        out_shape=jax.ShapeDtypeStruct((rows_out, cols), F32),
        compiler_params=pltpu.CompilerParams(
            dimension_semantics=("arbitrary",), vmem_limit_bytes=40 * 2**20
        ),
        cost_estimate=pl.CostEstimate(
            flops=0, bytes_accessed=rows_out * cols * 6, transcendentals=0
        ),
        name="spread_rows",
    )(where_at, *pieces)


def local(
    tokens,
    out_grad,
    block_order,
    norm1_gain,
    q_weight,
    q_bias,
    k_weight,
    k_bias,
    v_weight,
    v_bias,
    o_weight,
    norm2_gain,
    gate_weight,
    up_weight,
    down_weight,
):
    n_ctx = lax.axis_size("ctx")
    n_z = lax.axis_size("fsdp")
    tp = 4 if n_ctx % 4 == 0 else (2 if n_ctx % 2 == 0 else 1)
    here = lax.axis_index("ctx")
    zed = lax.axis_index("fsdp")
    core = lax.axis_index("seq")
    n_part = 2 * tp
    part = lax.rem(here, tp) * 2 + core
    first_core = core == 0

    def swap(v):
        return lax.ppermute(v, "seq", [(0, 1), (1, 0)])

    def hop(v, k):
        if k == 0:
            return v
        return lax.ppermute(v, "ctx", [(i, i ^ k) for i in range(n_ctx)])

    def hop_z(v, k):
        if k == 0:
            return v
        return lax.ppermute(v, "fsdp", [(i, i ^ k) for i in range(n_z)])

    def gather_z(v):
        return lax.all_gather(v, "fsdp", axis=0, tiled=True)

    def scatter_z(v):
        return lax.psum_scatter(v, "fsdp", scatter_dimension=0, tiled=True)

    tokens_here, width = tokens.shape[1:]
    ff = gate_weight.shape[1]
    rows_here = q_weight.shape[0]
    q_half = GROUP * HEAD
    key_width = KV_HEADS * HEAD
    block_len = tokens_here * n_z

    vec_len = 3 * rows_here + 2 * k_bias.shape[0]
    vec = jnp.concatenate([norm1_gain, norm2_gain, q_bias, k_bias, v_bias])
    half_width = q_half + 2 * HEAD
    vec_rows = 16
    vec = jnp.pad(vec, (0, vec_rows * half_width - vec_len)).reshape(vec_rows, half_width)
    qkv_half = jnp.concatenate(
        [
            lax.dynamic_slice_in_dim(q_weight, core * q_half, q_half, 1),
            lax.dynamic_slice_in_dim(k_weight, core * HEAD, HEAD, 1),
            lax.dynamic_slice_in_dim(v_weight, core * HEAD, HEAD, 1),
        ],
        1,
    )
    got = gather_z(jnp.concatenate([qkv_half, vec], 0)).reshape(n_z, -1, half_width)
    w_qkv_own = got[:, :rows_here].reshape(width, half_width)
    w_qkv_oth = swap(w_qkv_own)
    vecs = got[:, rows_here:].reshape(n_z, -1)
    gain_one = vecs[:, :rows_here].reshape(-1)
    gain_two = vecs[:, rows_here : 2 * rows_here].reshape(-1)
    b_query = vecs[:, 2 * rows_here : 3 * rows_here].reshape(-1)
    kb = k_bias.shape[0]
    b_key = vecs[:, 3 * rows_here : 3 * rows_here + kb].reshape(-1)
    b_value = vecs[:, 3 * rows_here + kb : 3 * rows_here + 2 * kb].reshape(-1)

    ff_z = ff // n_z
    piece = ff_z // n_part
    piece_pad = -(-piece // 32) * 32
    ff_half = n_z * piece_pad

    def ff_columns(w):
        cuts = []
        for j in range(n_z):
            cut = lax.dynamic_slice_in_dim(w, j * ff_z + part * piece, piece, 1)
            cuts.append(jnp.pad(cut, ((0, 0), (0, piece_pad - piece))))
        return jnp.concatenate(cuts, 1)

    o_rows = rows_here // 2
    down_cut = lax.dynamic_slice_in_dim(down_weight, part * piece, piece, 0)
    do_cut = jnp.concatenate(
        [
            jnp.pad(down_cut, ((0, piece_pad - piece), (0, 0))),
            lax.dynamic_slice_in_dim(o_weight, core * o_rows, o_rows, 0),
        ],
        0,
    )
    gu_cut = jnp.concatenate([ff_columns(gate_weight), ff_columns(up_weight)], 1)
    w_qkv_own, do_cut, gu_cut = lax.optimization_barrier((w_qkv_own, do_cut, gu_cut))
    do_own = gather_z(do_cut)
    do_own, gu_cut = lax.optimization_barrier((do_own, gu_cut))
    gu_own = gather_z(gu_cut)
    gu_oth = swap(gu_own)
    do_oth = swap(do_own)
    do_own = do_own.reshape(n_z, -1, width)
    do_oth = do_oth.reshape(n_z, -1, width)
    down_own = do_own[:, :piece_pad].reshape(ff_half, width)
    down_oth = do_oth[:, :piece_pad].reshape(ff_half, width)
    o_own = do_own[:, piece_pad:]
    o_oth = do_oth[:, piece_pad:]
    w_out = jnp.where(
        first_core, jnp.stack([o_own, o_oth], 1), jnp.stack([o_oth, o_own], 1)
    ).reshape(width, width)
    og_here = out_grad[0]
    og_all = jnp.concatenate([hop(og_here, k) for k in range(tp)], 0)

    order_row = block_order[0]
    query_pos = (
        order_row[here] * block_len
        + zed * tokens_here
        + jnp.arange(tokens_here, dtype=jnp.int32)
    )
    if n_ctx == tp:
        block_at = jnp.stack([order_row[here ^ k] for k in range(n_ctx)])
    else:
        block_at = order_row
    info = jnp.concatenate([jnp.stack([order_row[here], zed]).astype(jnp.int32), block_at])
    cosine_table, sine_table = rope_tables(query_pos, HEAD)

    inputs = tokens[0].astype(F32)
    normed_one, scale_one, hidden_one = rms_forward(inputs, gain_one)
    pre_own = matmul(hidden_one, w_qkv_own)
    pre_oth = matmul(hidden_one, w_qkv_oth)
    pre_a = jnp.where(first_core, pre_own, pre_oth)
    pre_b = jnp.where(first_core, pre_oth, pre_own)
    query_pre = jnp.concatenate([pre_a[:, :q_half], pre_b[:, :q_half]], 1) + b_query
    key_pre = (
        jnp.concatenate([pre_a[:, q_half : q_half + HEAD], pre_b[:, q_half : q_half + HEAD]], 1)
        + b_key
    )
    value_pre = jnp.concatenate([pre_a[:, q_half + HEAD :], pre_b[:, q_half + HEAD :]], 1) + b_value
    queries = rotate(query_pre.reshape(tokens_here, HEADS, HEAD), cosine_table, sine_table)
    queries = queries.astype(BF16).reshape(tokens_here, HEADS * HEAD) * BF16(HEAD ** (-0.5))
    key_rot = rotate(key_pre.reshape(tokens_here, KV_HEADS, HEAD), cosine_table, sine_table)
    kv_local = jnp.concatenate(
        [key_rot.astype(BF16).reshape(tokens_here, key_width), value_pre.astype(BF16)], 1
    )
    kv_block = jnp.concatenate([hop_z(kv_local, k) for k in range(n_z)], 0)
    if n_ctx == tp:
        kv_whole = jnp.stack([hop(kv_block, k) for k in range(n_ctx)])
    else:
        kv_whole = lax.all_gather(kv_block, "ctx", axis=0, tiled=False)
    attended, queries_ext = attend_forward(info, queries, kv_whole)
    resid = inputs + matmul(attended, w_out)
    normed_two, scale_two, hidden_two = rms_forward(resid, gain_two)

    h2_all = jnp.concatenate([hop(hidden_two, k) for k in range(tp)], 0)

    def scatter_plane(v):
        parts = v.astype(BF16).reshape(tp, tokens_here, width)
        total = parts[0].astype(F32)
        for k in range(1, tp):
            total = total + hop(parts[k], k).astype(F32)
        return total

    def ff_half_pass(w_gu, w_d):
        gu = matmul(h2_all, w_gu)
        gate = gu[:, :ff_half]
        up = gu[:, ff_half:]
        sig = jax.nn.sigmoid(gate)
        silu = gate * sig
        act = (silu * up).astype(BF16)
        grad_act = times_transposed(og_all, w_d)
        grad_gate = (grad_act * up * sig * (1.0 + gate * (1.0 - sig))).astype(BF16)
        grad_up = (grad_act * silu).astype(BF16)
        return act, jnp.concatenate([grad_gate, grad_up], 1)

    act_own, ggu_own = ff_half_pass(gu_own, down_own)
    act_oth, ggu_oth = ff_half_pass(gu_oth, down_oth)
    grad_h2 = scatter_plane(times_transposed(ggu_own, gu_own) + times_transposed(ggu_oth, gu_oth))
    result = resid + scatter_plane(matmul(act_own, down_own) + matmul(act_oth, down_oth))
    layer_out = result.astype(BF16)[None]

    idx = jnp.arange(n_part, dtype=jnp.int32)
    where_at = ((idx // 2) ^ lax.rem(here, tp)) * 2 + ((idx % 2) ^ core)

    def reduce_start(part_sum):
        cols = part_sum.shape[1]
        cut = part_sum.astype(BF16).reshape(n_z, 2, rows_here // 2, cols)
        own = lax.dynamic_index_in_dim(cut, core, 1, keepdims=False)
        oth = lax.dynamic_index_in_dim(cut, 1 - core, 1, keepdims=False)
        return (own.astype(F32) + swap(oth).astype(F32)).astype(BF16).reshape(-1, cols)

    def scatter_hops(v):
        cut = v.reshape(n_z, -1, v.shape[1])
        total = lax.dynamic_index_in_dim(cut, zed, 0, keepdims=False).astype(F32)
        for k in range(1, n_z):
            out = lax.dynamic_index_in_dim(cut, zed ^ k, 0, keepdims=False)
            total = total + hop_z(out, k).astype(F32)
        return total.astype(BF16)

    def reduce_end(mine):
        if n_ctx == tp:
            k = 1
            while k < n_ctx:
                mine = lax.optimization_barrier(mine)
                mine = (mine.astype(F32) + hop(mine, k).astype(F32)).astype(BF16)
                k *= 2
            mine = lax.optimization_barrier(mine)
        else:
            mine = lax.psum(mine, "ctx")
        other = swap(mine)
        whole = jnp.where(
            first_core, jnp.concatenate([mine, other], 0), jnp.concatenate([other, mine], 0)
        )
        return whole.astype(F32)

    def core_sum(own, oth):
        return (own + swap(oth.astype(BF16)).astype(F32)).astype(BF16)

    def ff_pieces(mine):
        if n_ctx != tp:
            groups = [[g * tp + c for g in range(n_ctx // tp)] for c in range(tp)]
            mine = lax.psum(mine, "ctx", axis_index_groups=groups)
        pieces = []
        for k in range(tp):
            pieces.append(hop(mine, k))
            pieces.append(swap(pieces[-1]))
        return pieces

    d_gu = core_sum(contract_rows(h2_all, ggu_own), contract_rows(h2_all, ggu_oth))
    d_down = core_sum(contract_rows(act_own, og_all), contract_rows(act_oth, og_all))

    grad_norm_two, grad_gain_two = rms_backward(grad_h2, normed_two, scale_two, gain_two)
    grad_resid = og_here.astype(F32) + grad_norm_two
    grad_proj = grad_resid.astype(BF16)
    grad_att = times_transposed(grad_proj, w_out).astype(BF16)
    d_out = reduce_start(contract_rows(attended, grad_proj))
    grad_att, d_gu, d_down, d_out = lax.optimization_barrier((grad_att, d_gu, d_down, d_out))
    d_gu = scatter_z(d_gu)
    d_down = scatter_z(d_down)
    d_out = scatter_z(d_out)
    grad_queries, grad_terms = attend_backward(info, queries_ext, grad_att, attended, kv_whole)
    if n_ctx == tp:
        kv_sum = grad_terms[0].astype(F32)
        for k in range(1, n_ctx):
            kv_sum = kv_sum + hop(grad_terms[k], k).astype(F32)
        kv_sum = kv_sum.astype(BF16)
    else:
        kv_sum = lax.psum_scatter(grad_terms, "ctx", scatter_dimension=0, tiled=False)
    kv_sum = kv_sum.reshape(n_z, tokens_here, 2 * key_width)
    grad_kv = kv_sum[0].astype(F32)
    for k in range(1, n_z):
        grad_kv = grad_kv + hop_z(kv_sum[k], k).astype(F32)

    grad_q_pre = (
        rotate(grad_queries.reshape(tokens_here, HEADS, HEAD), cosine_table, -sine_table)
        .reshape(tokens_here, HEADS * HEAD)
        .astype(BF16)
    )
    grad_k_pre = (
        rotate(
            grad_kv[:, :key_width].reshape(tokens_here, KV_HEADS, HEAD), cosine_table, -sine_table
        )
        .reshape(tokens_here, key_width)
        .astype(BF16)
    )
    grad_v_pre = grad_kv[:, key_width:].astype(BF16)

    def column_halves(q, k, v):
        return [
            jnp.concatenate(
                [
                    q[:, g * q_half : (g + 1) * q_half],
                    k[:, g * HEAD : (g + 1) * HEAD],
                    v[:, g * HEAD : (g + 1) * HEAD],
                ],
                1,
            )
            for g in range(2)
        ]

    halves = column_halves(grad_q_pre, grad_k_pre, grad_v_pre)
    g_own = jnp.where(first_core, halves[0], halves[1])
    g_oth = jnp.where(first_core, halves[1], halves[0])
    grad_hidden_one = times_transposed(g_own, w_qkv_own) + times_transposed(g_oth, w_qkv_oth)
    grad_norm_one, grad_gain_one = rms_backward(grad_hidden_one, normed_one, scale_one, gain_one)
    tokens_grad = (grad_resid + grad_norm_one)[None]

    def by_rows(v):
        share = v.shape[0] // n_z
        return jnp.pad(v.reshape(n_z, share), ((0, 0), (0, rows_here - share))).reshape(width)

    columns = jnp.stack(
        [
            grad_gain_one,
            grad_gain_two,
            jnp.sum(grad_q_pre.astype(F32), 0),
            by_rows(jnp.sum(grad_k_pre.astype(F32), 0)),
            by_rows(jnp.sum(grad_v_pre.astype(F32), 0)),
        ],
        1,
    )
    grad_w_query = reduce_end(
        scatter_hops(reduce_start(contract_rows(hidden_one, grad_q_pre)))
    )
    grad_w_kv = jnp.concatenate(
        [
            contract_rows(hidden_one, jnp.concatenate([grad_k_pre, grad_v_pre], 1)),
            jnp.pad(columns, ((0, 0), (0, 128 - columns.shape[1]))),
        ],
        1,
    )
    grad_w_kv = reduce_end(scatter_hops(reduce_start(grad_w_kv)))
    sums = grad_w_kv[:, 2 * key_width :]
    grad_w_out = reduce_end(d_out)
    grad_w_gate, grad_w_up = spread_columns(where_at, ff_pieces(d_gu), n_z, ff)
    grad_w_down = spread_rows(where_at, ff_pieces(d_down), ff_z)

    return (
        layer_out,
        tokens_grad,
        sums[:, 0],
        grad_w_query,
        sums[:, 2],
        grad_w_kv[:, :key_width],
        sums[:kb, 3],
        grad_w_kv[:, key_width : 2 * key_width],
        sums[:kb, 4],
        grad_w_out,
        sums[:, 1],
        grad_w_gate,
        grad_w_up,
        grad_w_down,
    )


def solution(mesh):
    in_specs = (
        P("seq", ("ctx", "fsdp"), None),
        P("seq", ("ctx", "fsdp"), None),
        P("seq", None),
        P("fsdp"),
        P("fsdp", None),
        P("fsdp"),
        P("fsdp", None),
        P("fsdp"),
        P("fsdp", None),
        P("fsdp"),
        P("fsdp", None),
        P("fsdp"),
        P("fsdp", None),
        P("fsdp", None),
        P("fsdp", None),
    )
    out_specs = (
        P("seq", ("ctx", "fsdp"), None),
        P("seq", ("ctx", "fsdp"), None),
        P("fsdp"),
        P("fsdp", None),
        P("fsdp"),
        P("fsdp", None),
        P("fsdp"),
        P("fsdp", None),
        P("fsdp"),
        P("fsdp", None),
        P("fsdp"),
        P("fsdp", None),
        P("fsdp", None),
        P("fsdp", None),
    )
    return jax.shard_map(local, mesh=mesh, in_specs=in_specs, out_specs=out_specs, check_vma=False)
```

time: 615 us -> 462 us (0.75)
  blocking collectives: 88.3 us -> 0 us
  waiting for transfers between devices: 147 us -> 208 us
  local copies, waits for them, and re-layouts: 100 us -> 47.1 us
  Pallas kernels: 0 us -> 45.9 us
  matrix products: 89 us -> 46.6 us
  starting transfers between devices: 104 us -> 69.8 us
  other arithmetic: 51 us -> 20.3 us
  loops' own time: 11.2 us -> 0 us
    all_gather x3, waiting for transfers between devices: 0.02 us -> 55.8 us  [gather_z(): return lax.all_gather(v, 'fsdp', axis=0, tiled=True)]
    ppermute x0 -> x12, waiting for transfers between devices: none -> 53.5 us  [hop_z(): return lax.ppermute(v, 'fsdp', [(i, i ^ k) for i in range(n_z)])]
    all_gather x2 -> x0, blocking collectives: 50.1 us -> none  [gather_z(): return lax.all_gather(v, 'fsdp', axis=0, tiled=True)]
    reduce_scatter x6 -> x3, waiting for transfers between devices: 48.2 us -> 0.02 us  [scatter_z(): return lax.psum_scatter(v, 'fsdp', scatter_dimension=0, tiled=True)]
    ppermute x30, starting transfers between devices: 83.8 us -> 36.5 us  [hop(): return lax.ppermute(v, 'ctx', [(i, i ^ k) for i in range(n_ctx)])]
    pallas_call x0 -> x4, Pallas kernels: none -> 45.9 us  [the longest x1 21.3 us: attend_backward(): pl.pallas_call(backward_kernel, grid_spec=pltpu.PrefetchScalarGridSpec(nu...]
    psum x1 -> x0, blocking collectives: 38.2 us -> none  [local(): lax.psum(jnp.concatenate([grad_gain_one, grad_gain_two, jnp.sum(grad_q_pr...]
    dot_general x14 -> x0, matrix products: 34.6 us -> none  [the longest x4 13.4 us: scores_of(): jnp.einsum('gqd,kgd->gqk', queries, keys_block, preferred_element_type=F32)]
  transfers between devices with their start and end apart: 53 -> 67, of which waited for: 25 -> 25; matrix products, arithmetic and copies ran while one was open for 23% -> 18% of each run, Pallas kernels for 0% -> 9%
where the time goes in v2:
time: 462 us; the launch traced here: 454 us
  waiting for transfers between devices  208 us (45%)
  starting transfers between devices  69.8 us (15%)
  local copies, waits for them, and re-layouts  47.1 us (10%)
  matrix products  46.6 us (10%)
  Pallas kernels  45.9 us (10%)
  other arithmetic  20.3 us (4%)
  between operations  16.6 us (4%)
    ppermute x30, waiting for transfers between devices, hop(): return lax.ppermute(v, 'ctx', [(i, i ^ k) for i in range(n_ctx)])  97.7 us
    all_gather x3, waiting for transfers between devices, gather_z(): return lax.all_gather(v, 'fsdp', axis=0, tiled=True)  55.8 us
    ppermute x12, waiting for transfers between devices, hop_z(): return lax.ppermute(v, 'fsdp', [(i, i ^ k) for i in range(n_z)])  53.5 us
    ppermute x30, starting transfers between devices, hop(): return lax.ppermute(v, 'ctx', [(i, i ^ k) for i in range(n_ctx)])  36.5 us
    pallas_call x1, Pallas kernels, attend_backward(): pl.pallas_call(backward_kernel, grid_spec=pltpu.PrefetchScalarGridSpec(nu...  21.3 us
    dot_general x7, matrix products, contract_rows(): lax.dot_general(left_side, right_side, (((0,), (0,)), ((), ())), preferre...  18.9 us
    ppermute x12, starting transfers between devices, hop_z(): return lax.ppermute(v, 'fsdp', [(i, i ^ k) for i in range(n_z)])  17.4 us
    dot_general x7, matrix products, times_transposed(): lax.dot_general(left_side, right_side, (((1,), (1,)), ((), ())), preferre...  15.9 us
  transfers between devices with their start and end apart: 67, of which 25 were waited for; matrix products, arithmetic and copies ran while one was open for 18% of the time, Pallas kernels for 9%

profile of v2, /device:TPU:1, one launch (start us, length us, event | category | flops | bytes accessed | tf_op | source)
XLA Modules:
  0.0 454.1 jit_solution(2646121374821686358)
XLA Ops:
  7.2 3.6 concatenate.105
  19.9 26.6 %all-gather.9.cloned.1.call-done = bf16[4,240,576]{1,2,0:T(8,128)(2,1)} async-done(((bf16[1,240,576]{1,2,0:T(8,128)(2,1)}), bf16[4,240,576]{1,2,0:T(8,128)(2,1)}) %all-gather.9.cloned.1.call-update) | async-done | bytes 1105936 | tf_op jit(solution)/shard_map/all_gather | solution.py:433
  62.3 29.2 %all-gather.5.cloned.1.call-done = bf16[1088,896]{1,0:T(8,128)(2,1)} async-done(((bf16[272,896]{1,0:T(8,128)(2,1)}), bf16[1088,896]{1,0:T(8,128)(2,1)}) %all-gather.5.cloned.1.call-update) | async-done | bytes 1949712 | tf_op jit(solution)/shard_map/all_gather | solution.py:433
  97.7 5.2 %collective-permute-done.2 = bf16[192,256]{1,0:T(8,128)(2,1)S(1)} collective-permute-done((bf16[192,256]{1,0:T(8,128)(2,1)S(1)}, bf16[192,256]{1,0:T(8,128)(2,1)S(1)}, u32[]{:S(2)}, u32[]{:S(2)}) %collective-permute-start.2) | collective-permute-done | bytes 98336 | tf_op jit(solution)/shard_map/ppermute | solution.py:430
  107.3 7.9 %collective-permute-done.6 = bf16[768,256]{1,0:T(8,128)(2,1)S(1)} collective-permute-done((bf16[768,256]{1,0:T(8,128)(2,1)}, bf16[768,256]{1,0:T(8,128)(2,1)S(1)}, u32[]{:S(2)}, u32[]{:S(2)}) %collective-permute-start.6) | collective-permute-done | bytes 393248 | tf_op jit(solution)/shard_map/ppermute | solution.py:425
  115.2 9.1 %collective-permute-done.5 = bf16[768,256]{1,0:T(8,128)(2,1)S(1)} collective-permute-done((bf16[768,256]{1,0:T(8,128)(2,1)}, bf16[768,256]{1,0:T(8,128)(2,1)S(1)}, u32[]{:S(2)}, u32[]{:S(2)}) %collective-permute-start.5) | collective-permute-done | bytes 393248 | tf_op jit(solution)/shard_map/ppermute | solution.py:425
  126.7 13.2 %attend_forward.1 = (bf16[192,896]{1,0:T(8,128)(2,1)S(1)}, bf16[2688,256]{1,0:T(8,128)(2,1)S(1)}) custom-call(s32[6]{0:T(128)S(1)} %concatenate.103.info_ref, bf16[192,896]{1,0:T(8,128)(2,1)S(1)} %copy.135.q_ref, bf16[4,768,256]{2,1,0:T(8,128)(2,1)S(1)} %pad_maximum_fusion.2.kv_ref), custom_call_target="tpu_custom_call" | custom-call | flops 8455716864 | bytes 6291456 | tf_op jit(solution)/shard_map/attend_forward/pallas_call | solution.py:254
  144.5 4.7 %collective-permute-start.9 = (bf16[192,896]{1,0:T(8,128)(2,1)S(1)}, bf16[192,896]{1,0:T(8,128)(2,1)}, u32[]{:S(2)}, u32[]{:S(2)}) collective-permute-start(bf16[192,896]{1,0:T(8,128)(2,1)S(1)} %multiply_convert_fusion.6), channel_id=1, source_target_pairs={{0,8},{4,12},{8,0},{12,4},{1,9},{5,13},{9,1},{13,5},{2,10},{6,14},... | collective-permute-start | bytes 1032200 | tf_op jit(solution)/shard_map/ppermute | solution.py:425
  154.8 3.6 collective-permute-start.16
  158.4 7.1 %collective-permute-done.9 = bf16[192,896]{1,0:T(8,128)(2,1)} collective-permute-done((bf16[192,896]{1,0:T(8,128)(2,1)S(1)}, bf16[192,896]{1,0:T(8,128)(2,1)}, u32[]{:S(2)}, u32[]{:S(2)}) %collective-permute-start.9) | collective-permute-done | bytes 344096 | tf_op jit(solution)/shard_map/ppermute | solution.py:425
  169.8 7.7 %collective-permute-done.16 = bf16[192,896]{1,0:T(8,128)(2,1)S(1)} collective-permute-done((bf16[192,896]{1,0:T(8,128)(2,1)S(1)}, bf16[192,896]{1,0:T(8,128)(2,1)S(1)}, u32[]{:S(2)}, u32[]{:S(2)}) %collective-permute-start.16) | collective-permute-done | bytes 344096 | tf_op jit(solution)/shard_map/ppermute | solution.py:425
  184.2 4.1 fusion.75
  191.0 4.0 add_convert_fusion.1
  202.6 4.5 convolution_convert_fusion
  210.3 4.0 collective-permute-done.19
  215.4 4.6 %collective-permute-done.14 = bf16[192,896]{1,0:T(8,128)(2,1)S(1)} collective-permute-done((bf16[192,896]{1,0:T(8,128)(2,1)S(1)}, bf16[192,896]{1,0:T(8,128)(2,1)S(1)}, u32[]{:S(2)}, u32[]{:S(2)}) %collective-permute-start.14) | collective-permute-done | bytes 344096 | tf_op jit(solution)/shard_map/ppermute | solution.py:425
  220.0 8.2 %collective-permute-done.13 = bf16[192,896]{1,0:T(8,128)(2,1)S(1)} collective-permute-done((bf16[192,896]{1,0:T(8,128)(2,1)S(1)}, bf16[192,896]{1,0:T(8,128)(2,1)S(1)}, u32[]{:S(2)}, u32[]{:S(2)}) %collective-permute-start.13) | collective-permute-done | bytes 344096 | tf_op jit(solution)/shard_map/ppermute | solution.py:425
  236.8 3.6 add_convert_fusion.3
  240.5 5.8 %add_convert_fusion = bf16[896,1280]{1,0:T(8,128)(2,1)} fusion(bf16[896,1280]{1,0:T(8,128)(2,1)} %collective-permute-done.21, bf16[768,640]{1,0:T(8,128)(2,1)} %copy-done.60, bf16[768,640]{1,0:T(8,128)(2,1)} %copy-done.59, bf16[192,896]{1,0:T(8,128)(2,1)S(1)} %copy-done.52, bf16[192,896]{1,0:T(8,128)(2,1)} %collective-permute-done.9, ...), kind=kOutput, calls=%fused_computation | convolution fusion | flops 1774485504 | bytes 7929856 | tf_op jit(solution)/shard_map/dot_general | solution.py:49
  249.6 21.3 %attend_backward.1 = (f32[192,896]{1,0:T(8,128)S(1)}, bf16[4,768,256]{2,1,0:T(8,128)(2,1)S(1)}) custom-call(s32[6]{0:T(128)S(1)} %concatenate.103.info_ref, bf16[2688,256]{1,0:T(8,128)(2,1)S(1)} %copy-done.8, bf16[192,896]{1,0:T(8,128)(2,1)S(1)} %copy-done.5, bf16[192,896]{1,0:T(8,128)(2,1)S(1)} %get-tuple-element.30.att_ref, ...), custom_call_target="tpu_custom_call" | custom-call | flops 21139292160 | bytes 8388608 | tf_op jit(solution)/shard_map/attend_backward/pallas_call | solution.py:286
  272.8 7.0 %collective-permute-start.25 = (bf16[768,256]{1,0:T(8,128)(2,1)}, bf16[768,256]{1,0:T(8,128)(2,1)}, u32[]{:S(2)}, u32[]{:S(2)}) collective-permute-start(bf16[768,256]{1,0:T(8,128)(2,1)} %get-tuple-element.75), channel_id=1, source_target_pairs={{0,8},{4,12},{8,0},{12,4},{1,9},{5,13},{9,1},{13,5},{2,10},{6,14},... | collective-permute-start | bytes 1179656 | tf_op jit(solution)/shard_map/ppermute | solution.py:425
  286.4 6.6 %collective-permute-done.25 = bf16[768,256]{1,0:T(8,128)(2,1)} collective-permute-done((bf16[768,256]{1,0:T(8,128)(2,1)}, bf16[768,256]{1,0:T(8,128)(2,1)}, u32[]{:S(2)}, u32[]{:S(2)}) %collective-permute-start.25) | collective-permute-done | bytes 393248 | tf_op jit(solution)/shard_map/ppermute | solution.py:425
  303.1 4.1 collective-permute-done.28
  323.8 5.3 %collective-permute-start.38 = (bf16[112,896]{1,0:T(8,128)(2,1)S(1)}, bf16[112,896]{1,0:T(8,128)(2,1)S(1)}, u32[]{:S(2)}, u32[]{:S(2)}) collective-permute-start(bf16[112,896]{1,0:T(8,128)(2,1)S(1)} %get-tuple-element.88), channel_id=1, source_target_pairs={{0,1},{1,0},{2,3},{3,2},{4,5},{5,4},{6,7},{7,6},{8,9},{9,8},{10,11... | collective-permute-start | bytes 602120 | tf_op jit(solution)/shard_map/ppermute | solution.py:430
  329.1 8.0 %collective-permute-done.32 = bf16[112,384]{1,0:T(8,128)(2,1)S(1)} collective-permute-done((bf16[112,384]{1,0:T(8,128)(2,1)S(1)}, bf16[112,384]{1,0:T(8,128)(2,1)S(1)}, u32[]{:S(2)}, u32[]{:S(2)}) %collective-permute-start.32) | collective-permute-done | bytes 86048 | tf_op jit(solution)/shard_map/ppermute | solution.py:430
  339.7 29.6 %collective-permute-done.39 = bf16[112,896]{1,0:T(8,128)(2,1)S(1)} collective-permute-done((bf16[112,896]{1,0:T(8,128)(2,1)S(1)}, bf16[112,896]{1,0:T(8,128)(2,1)S(1)}, u32[]{:S(2)}, u32[]{:S(2)}) %collective-permute-start.39) | collective-permute-done | bytes 200736 | tf_op jit(solution)/shard_map/ppermute | solution.py:430
  371.5 4.0 collective-permute-done.41
  375.6 4.2 collective-permute-done.44
  393.7 3.9 collective-permute-done.55.refs_2_
  402.8 26.0 %collective-permute-done.59.refs_6_ = bf16[160,896]{1,0:T(8,128)(2,1)S(1)} collective-permute-done((bf16[160,896]{1,0:T(8,128)(2,1)}, bf16[160,896]{1,0:T(8,128)(2,1)S(1)}, u32[]{:S(2)}, u32[]{:S(2)}) %collective-permute-start.59) | collective-permute-done | bytes 286752 | tf_op jit(solution)/shard_map/ppermute | solution.py:425
  435.4 4.4 spread_rows.1
  439.8 7.0 %spread_columns.1 = (f32[224,4864]{1,0:T(8,128)}, f32[224,4864]{1,0:T(8,128)}) custom-call(s32[8]{0:T(128)S(1)} %fusion.58.where_ref, bf16[224,1280]{1,0:T(8,128)(2,1)S(1)} %copy-done.4, bf16[224,1280]{1,0:T(8,128)(2,1)S(1)} %collective-permute-done.47.refs_1_, bf16[224,1280]{1,0:T(8,128)(2,1)S(1)} %collective-permute-done.48.refs_2_, ...), custom_call_target="tpu_custom_call" | custom-call | bytes 13074432 | tf_op jit(solution)/shard_map/spread_columns/pallas_call | solution.py:342
  (393 shorter events, 149.5 us)
Async XLA Ops:
  7.2 39.2 %all-gather.9.cloned.1.call-start = ((), (), s32[]{:S(2)}) async-start(), calls=%async_computation.8 | async-start | bytes 1474560 | tf_op jit(solution)/shard_map/all_gather | solution.py:433
  14.3 77.3 %all-gather.5.cloned.1.call-start = ((), (), s32[]{:S(2)}) async-start(), calls=%async_computation.3 | async-start | bytes 2437120 | tf_op jit(solution)/shard_map/all_gather | solution.py:433
  48.1 102.2 %all-gather.7.cloned.1.call-start = ((), (), s32[]{:S(2)}) async-start(), calls=%async_computation.4 | async-start | bytes 2867200 | tf_op jit(solution)/shard_map/all_gather | solution.py:433
  91.6 279.4 %reduce-scatter.4.cloned.1.call-start = ((), (), s32[]{:S(2)}) async-start(), calls=%async_computation.5 | async-start | bytes 1003520 | tf_op jit(solution)/shard_map/reduce_scatter | solution.py:436
  95.9 45.7 %collective-permute-start.7 = (bf16[1088,896]{1,0:T(8,128)(2,1)}, bf16[1088,896]{1,0:T(8,128)(2,1)}, u32[]{:S(2)}, u32[]{:S(2)}) collective-permute-start(bf16[1088,896]{1,0:T(8,128)(2,1)} %all-gather.5.cloned.1.call-done), channel_id=1, source_target_pairs={{0,16},{16,0},{1,17},{17,1},{2,18},{18,2},{3,19},{19,3},{4,20},{20... | collective-permute-start | bytes 5849096 | tf_op jit(solution)/shard_map/ppermute | solution.py:420
  105.8 18.6 %collective-permute-start.5 = (bf16[768,256]{1,0:T(8,128)(2,1)}, bf16[768,256]{1,0:T(8,128)(2,1)S(1)}, u32[]{:S(2)}, u32[]{:S(2)}) collective-permute-start(bf16[768,256]{1,0:T(8,128)(2,1)} %pad_maximum_fusion.9), channel_id=1, source_target_pairs={{0,8},{4,12},{8,0},{12,4},{1,9},{5,13},{9,1},{13,5},{2,10},{6,14},... | collective-permute-start | bytes 1179656 | tf_op jit(solution)/shard_map/ppermute | solution.py:425
  106.0 18.3 %collective-permute-start.4 = (bf16[768,256]{1,0:T(8,128)(2,1)}, bf16[768,256]{1,0:T(8,128)(2,1)S(1)}, u32[]{:S(2)}, u32[]{:S(2)}) collective-permute-start(bf16[768,256]{1,0:T(8,128)(2,1)} %pad_maximum_fusion.9), channel_id=1, source_target_pairs={{0,4},{4,0},{8,12},{12,8},{1,5},{5,1},{9,13},{13,9},{2,6},{6,2},{1... | collective-permute-start | bytes 1179656 | tf_op jit(solution)/shard_map/ppermute | solution.py:425
  144.5 20.9 %collective-permute-start.9 = (bf16[192,896]{1,0:T(8,128)(2,1)S(1)}, bf16[192,896]{1,0:T(8,128)(2,1)}, u32[]{:S(2)}, u32[]{:S(2)}) collective-permute-start(bf16[192,896]{1,0:T(8,128)(2,1)S(1)} %multiply_convert_fusion.6), channel_id=1, source_target_pairs={{0,8},{4,12},{8,0},{12,4},{1,9},{5,13},{9,1},{13,5},{2,10},{6,14},... | collective-permute-start | bytes 1032200 | tf_op jit(solution)/shard_map/ppermute | solution.py:425
  150.3 33.9 %collective-permute-start.11 = (bf16[896,1280]{1,0:T(8,128)(2,1)}, bf16[896,1280]{1,0:T(8,128)(2,1)}, u32[]{:S(2)}, u32[]{:S(2)}) collective-permute-start(bf16[896,1280]{1,0:T(8,128)(2,1)} %all-gather.7.cloned.1.call-done), channel_id=1, source_target_pairs={{0,16},{16,0},{1,17},{17,1},{2,18},{18,2},{3,19},{19,3},{4,20},{20... | collective-permute-start | bytes 6881288 | tf_op jit(solution)/shard_map/ppermute | solution.py:420
  151.9 17.9 %collective-permute-start.17 = (bf16[192,896]{1,0:T(8,128)(2,1)}, bf16[192,896]{1,0:T(8,128)(2,1)}, u32[]{:S(2)}, u32[]{:S(2)}) collective-permute-start(bf16[192,896]{1,0:T(8,128)(2,1)} %bitcast.192), channel_id=1, source_target_pairs={{0,12},{4,8},{8,4},{12,0},{1,13},{5,9},{9,5},{13,1},{2,14},{6,10},... | collective-permute-start | bytes 1032200 | tf_op jit(solution)/shard_map/ppermute | solution.py:425
  154.8 22.7 %collective-permute-start.16 = (bf16[192,896]{1,0:T(8,128)(2,1)S(1)}, bf16[192,896]{1,0:T(8,128)(2,1)S(1)}, u32[]{:S(2)}, u32[]{:S(2)}) collective-permute-start(bf16[192,896]{1,0:T(8,128)(2,1)S(1)} %bitcast.193), channel_id=1, source_target_pairs={{0,8},{4,12},{8,0},{12,4},{1,9},{5,13},{9,1},{13,5},{2,10},{6,14},... | collective-permute-start | bytes 1032200 | tf_op jit(solution)/shard_map/ppermute | solution.py:425
  197.0 17.3 %collective-permute-start.19 = (bf16[192,896]{1,0:T(8,128)(2,1)S(1)}, bf16[192,896]{1,0:T(8,128)(2,1)S(1)}, u32[]{:S(2)}, u32[]{:S(2)}) collective-permute-start(bf16[192,896]{1,0:T(8,128)(2,1)S(1)} %get-tuple-element.78), channel_id=1, source_target_pairs={{0,8},{4,12},{8,0},{12,4},{1,9},{5,13},{9,1},{13,5},{2,10},{6,14},... | collective-permute-start | bytes 1032200 | tf_op jit(solution)/shard_map/ppermute | solution.py:425
  199.9 20.2 %collective-permute-start.14 = (bf16[192,896]{1,0:T(8,128)(2,1)S(1)}, bf16[192,896]{1,0:T(8,128)(2,1)S(1)}, u32[]{:S(2)}, u32[]{:S(2)}) collective-permute-start(bf16[192,896]{1,0:T(8,128)(2,1)S(1)} %get-tuple-element.80), channel_id=1, source_target_pairs={{0,12},{4,8},{8,4},{12,0},{1,13},{5,9},{9,5},{13,1},{2,14},{6,10},... | collective-permute-start | bytes 1032200 | tf_op jit(solution)/shard_map/ppermute | solution.py:425
  201.1 27.1 %collective-permute-start.13 = (bf16[192,896]{1,0:T(8,128)(2,1)S(1)}, bf16[192,896]{1,0:T(8,128)(2,1)S(1)}, u32[]{:S(2)}, u32[]{:S(2)}) collective-permute-start(bf16[192,896]{1,0:T(8,128)(2,1)S(1)} %get-tuple-element.81), channel_id=1, source_target_pairs={{0,8},{4,12},{8,0},{12,4},{1,9},{5,13},{9,1},{13,5},{2,10},{6,14},... | collective-permute-start | bytes 1032200 | tf_op jit(solution)/shard_map/ppermute | solution.py:425
  210.3 17.9 %collective-permute-start.12 = (bf16[192,896]{1,0:T(8,128)(2,1)S(1)}, bf16[192,896]{1,0:T(8,128)(2,1)S(1)}, u32[]{:S(2)}, u32[]{:S(2)}) collective-permute-start(bf16[192,896]{1,0:T(8,128)(2,1)S(1)} %get-tuple-element.79), channel_id=1, source_target_pairs={{0,4},{4,0},{8,12},{12,8},{1,5},{5,1},{9,13},{13,9},{2,6},{6,2},{1... | collective-permute-start | bytes 1032200 | tf_op jit(solution)/shard_map/ppermute | solution.py:425
  214.3 26.2 %collective-permute-start.21 = (bf16[896,1280]{1,0:T(8,128)(2,1)}, bf16[896,1280]{1,0:T(8,128)(2,1)}, u32[]{:S(2)}, u32[]{:S(2)}) collective-permute-start(bf16[896,1280]{1,0:T(8,128)(2,1)} %convolution_convert_fusion), channel_id=1, source_target_pairs={{0,16},{16,0},{1,17},{17,1},{2,18},{18,2},{3,19},{19,3},{4,20},{20... | collective-permute-start | bytes 6881288 | tf_op jit(solution)/shard_map/ppermute | solution.py:420
  215.0 21.8 %collective-permute-start.22 = (bf16[640,896]{1,0:T(8,128)(2,1)}, bf16[640,896]{1,0:T(8,128)(2,1)}, u32[]{:S(2)}, u32[]{:S(2)}) collective-permute-start(bf16[640,896]{1,0:T(8,128)(2,1)} %convolution_convert_fusion.3), channel_id=1, source_target_pairs={{0,16},{16,0},{1,17},{17,1},{2,18},{18,2},{3,19},{19,3},{4,20},{20... | collective-permute-start | bytes 3440648 | tf_op jit(solution)/shard_map/ppermute | solution.py:420
  246.3 142.0 %reduce-scatter.8.cloned.1.call-start = ((), (), s32[]{:S(2)}) async-start(), calls=%async_computation.7 | async-start | bytes 1433600 | tf_op jit(solution)/shard_map/reduce_scatter | solution.py:436
  247.2 143.8 %reduce-scatter.6.cloned.1.call-start = ((), (), s32[]{:S(2)}) async-start(), calls=%async_computation.6 | async-start | bytes 2867200 | tf_op jit(solution)/shard_map/reduce_scatter | solution.py:436
  272.8 20.1 %collective-permute-start.25 = (bf16[768,256]{1,0:T(8,128)(2,1)}, bf16[768,256]{1,0:T(8,128)(2,1)}, u32[]{:S(2)}, u32[]{:S(2)}) collective-permute-start(bf16[768,256]{1,0:T(8,128)(2,1)} %get-tuple-element.75), channel_id=1, source_target_pairs={{0,8},{4,12},{8,0},{12,4},{1,9},{5,13},{9,1},{13,5},{2,10},{6,14},... | collective-permute-start | bytes 1179656 | tf_op jit(solution)/shard_map/ppermute | solution.py:425
  316.9 20.1 %collective-permute-start.32 = (bf16[112,384]{1,0:T(8,128)(2,1)S(1)}, bf16[112,384]{1,0:T(8,128)(2,1)S(1)}, u32[]{:S(2)}, u32[]{:S(2)}) collective-permute-start(bf16[112,384]{1,0:T(8,128)(2,1)S(1)} %get-tuple-element.111), channel_id=1, source_target_pairs={{0,2},{1,3},{2,0},{3,1},{4,6},{5,7},{6,4},{7,5},{8,10},{9,11},{10,... | collective-permute-start | bytes 258056 | tf_op jit(solution)/shard_map/ppermute | solution.py:430
  316.9 20.1 %collective-permute-start.31 = (bf16[112,384]{1,0:T(8,128)(2,1)S(1)}, bf16[112,384]{1,0:T(8,128)(2,1)S(1)}, u32[]{:S(2)}, u32[]{:S(2)}) collective-permute-start(bf16[112,384]{1,0:T(8,128)(2,1)S(1)} %get-tuple-element.109), channel_id=1, source_target_pairs={{0,1},{1,0},{2,3},{3,2},{4,5},{5,4},{6,7},{7,6},{8,9},{9,8},{10,11... | collective-permute-start | bytes 258056 | tf_op jit(solution)/shard_map/ppermute | solution.py:430
  319.4 20.4 %collective-permute-start.40 = (bf16[112,896]{1,0:T(8,128)(2,1)S(1)}, bf16[112,896]{1,0:T(8,128)(2,1)S(1)}, u32[]{:S(2)}, u32[]{:S(2)}) collective-permute-start(bf16[112,896]{1,0:T(8,128)(2,1)S(1)} %get-tuple-element.89), channel_id=1, source_target_pairs={{0,3},{1,2},{2,1},{3,0},{4,7},{5,6},{6,5},{7,4},{8,11},{9,10},{10,... | collective-permute-start | bytes 602120 | tf_op jit(solution)/shard_map/ppermute | solution.py:430
  320.6 48.7 %collective-permute-start.39 = (bf16[112,896]{1,0:T(8,128)(2,1)S(1)}, bf16[112,896]{1,0:T(8,128)(2,1)S(1)}, u32[]{:S(2)}, u32[]{:S(2)}) collective-permute-start(bf16[112,896]{1,0:T(8,128)(2,1)S(1)} %get-tuple-element.90), channel_id=1, source_target_pairs={{0,2},{1,3},{2,0},{3,1},{4,6},{5,7},{6,4},{7,5},{8,10},{9,11},{10,... | collective-permute-start | bytes 602120 | tf_op jit(solution)/shard_map/ppermute | solution.py:430
  323.8 45.5 %collective-permute-start.38 = (bf16[112,896]{1,0:T(8,128)(2,1)S(1)}, bf16[112,896]{1,0:T(8,128)(2,1)S(1)}, u32[]{:S(2)}, u32[]{:S(2)}) collective-permute-start(bf16[112,896]{1,0:T(8,128)(2,1)S(1)} %get-tuple-element.88), channel_id=1, source_target_pairs={{0,1},{1,0},{2,3},{3,2},{4,5},{5,4},{6,7},{7,6},{8,9},{9,8},{10,11... | collective-permute-start | bytes 602120 | tf_op jit(solution)/shard_map/ppermute | solution.py:430
  337.1 33.2 %collective-permute-start.34 = (bf16[112,384]{1,0:T(8,128)(2,1)S(1)}, bf16[112,384]{1,0:T(8,128)(2,1)S(1)}, u32[]{:S(2)}, u32[]{:S(2)}) collective-permute-start(bf16[112,384]{1,0:T(8,128)(2,1)S(1)} %fusion.50), channel_id=1, source_target_pairs={{0,4},{4,0},{8,12},{12,8},{1,5},{5,1},{9,13},{13,9},{2,6},{6,2},{1... | collective-permute-start | bytes 258056 | tf_op jit(solution)/shard_map/ppermute | solution.py:425
  370.3 18.2 %collective-permute-start.35 = (bf16[112,384]{1,0:T(8,128)(2,1)S(1)}, bf16[112,384]{1,0:T(8,128)(2,1)S(1)}, u32[]{:S(2)}, u32[]{:S(2)}) collective-permute-start(bf16[112,384]{1,0:T(8,128)(2,1)S(1)} %add_convert_fusion.12), channel_id=1, source_target_pairs={{0,8},{4,12},{8,0},{12,4},{1,9},{5,13},{9,1},{13,5},{2,10},{6,14},... | collective-permute-start | bytes 258056 | tf_op jit(solution)/shard_map/ppermute | solution.py:425
  391.0 39.6 %collective-permute-start.48 = (bf16[224,1280]{1,0:T(8,128)(2,1)}, bf16[224,1280]{1,0:T(8,128)(2,1)S(1)}, u32[]{:S(2)}, u32[]{:S(2)}) collective-permute-start(bf16[224,1280]{1,0:T(8,128)(2,1)} %reduce-scatter.6.cloned.1.call-done.refs_0_), channel_id=1, source_target_pairs={{0,4},{4,0},{8,12},{12,8},{1,5},{5,1},{9,13},{13,9},{2,6},{6,2},{1... | collective-permute-start | bytes 1720328 | tf_op jit(solution)/shard_map/ppermute | solution.py:425
  392.1 39.0 %collective-permute-start.50 = (bf16[224,1280]{1,0:T(8,128)(2,1)}, bf16[224,1280]{1,0:T(8,128)(2,1)S(1)}, u32[]{:S(2)}, u32[]{:S(2)}) collective-permute-start(bf16[224,1280]{1,0:T(8,128)(2,1)} %reduce-scatter.6.cloned.1.call-done.refs_0_), channel_id=1, source_target_pairs={{0,8},{4,12},{8,0},{12,4},{1,9},{5,13},{9,1},{13,5},{2,10},{6,14},... | collective-permute-start | bytes 1720328 | tf_op jit(solution)/shard_map/ppermute | solution.py:425
  392.7 38.5 %collective-permute-start.52 = (bf16[224,1280]{1,0:T(8,128)(2,1)}, bf16[224,1280]{1,0:T(8,128)(2,1)S(1)}, u32[]{:S(2)}, u32[]{:S(2)}) collective-permute-start(bf16[224,1280]{1,0:T(8,128)(2,1)} %reduce-scatter.6.cloned.1.call-done.refs_0_), channel_id=1, source_target_pairs={{0,12},{4,8},{8,4},{12,0},{1,13},{5,9},{9,5},{13,1},{2,14},{6,10},... | collective-permute-start | bytes 1720328 | tf_op jit(solution)/shard_map/ppermute | solution.py:425
  397.6 31.2 %collective-permute-start.59 = (bf16[160,896]{1,0:T(8,128)(2,1)}, bf16[160,896]{1,0:T(8,128)(2,1)S(1)}, u32[]{:S(2)}, u32[]{:S(2)}) collective-permute-start(bf16[160,896]{1,0:T(8,128)(2,1)} %reduce-scatter.8.cloned.1.call-done.refs_0_), channel_id=1, source_target_pairs={{0,12},{4,8},{8,4},{12,0},{1,13},{5,9},{9,5},{13,1},{2,14},{6,10},... | collective-permute-start | bytes 860168 | tf_op jit(solution)/shard_map/ppermute | solution.py:425
  399.1 31.5 %collective-permute-start.56 = (bf16[160,896]{1,0:T(8,128)(2,1)S(1)}, bf16[160,896]{1,0:T(8,128)(2,1)S(1)}, u32[]{:S(2)}, u32[]{:S(2)}) collective-permute-start(bf16[160,896]{1,0:T(8,128)(2,1)S(1)} %collective-permute-done.55.refs_2_), channel_id=1, source_target_pairs={{0,16},{16,0},{1,17},{17,1},{2,18},{18,2},{3,19},{19,3},{4,20},{20... | collective-permute-start | bytes 860168 | tf_op jit(solution)/shard_map/ppermute | solution.py:420
  (96 other events, 887.7 us)
Sparse Core Ops, SparseCore 0:
  14.4 31.9 all-gather.8
  48.6 42.9 all-gather.4
  93.7 48.1 all-gather.6
  246.5 21.4 reduce-scatter.3
  270.7 28.4 reduce-scatter.7
  302.0 63.8 reduce-scatter.5

commit v3 on v2

--- a/solution.py
+++ b/solution.py
@@ -166,11 +166,17 @@
             ).astype(BF16)
 
 
-def backward_kernel(
-    info_ref, qext_ref, do_ref, att_ref, kv_ref, dq_ref, dkv_ref, doext_ref, dqt_ref
-):
+def backward_kernel(first, last, info_ref, qext_ref, do_ref, att_ref, kv_ref, *refs):
+    if first:
+        dkv_ref, doext_ref, dqt_ref = refs[-3:]
+        prior_ref = None
+    else:
+        prior_ref, doext_ref = refs[:2]
+        dkv_ref, dqt_ref = refs[-2:]
+    if last:
+        dq_ref = refs[0] if first else refs[2]
     step = pl.program_id(0)
-    last = pl.num_programs(0) - 1
+    end = pl.num_programs(0) - 1
     tokens_here = do_ref.shape[0]
     keys_here = kv_ref.shape[1]
     own = info_ref[0]
@@ -180,13 +186,16 @@
 
     @pl.when(step == 0)
     def _():
-        for h in range(HEADS):
-            rows = slice(h * tokens_here, (h + 1) * tokens_here)
-            grad = cut_heads(do_ref, h)
-            delta = jnp.sum(grad * cut_heads(att_ref, h), -1, keepdims=True)
-            doext_ref[rows, :128] = grad.astype(BF16)
-            doext_ref[rows, 128:] = split_lanes(-delta, (tokens_here, 128))
-        dqt_ref[...] = jnp.zeros(dqt_ref.shape, F32)
+        if first:
+            for h in range(HEADS):
+                rows = slice(h * tokens_here, (h + 1) * tokens_here)
+                grad = cut_heads(do_ref, h)
+                delta = jnp.sum(grad * cut_heads(att_ref, h), -1, keepdims=True)
+                doext_ref[rows, :128] = grad.astype(BF16)
+                doext_ref[rows, 128:] = split_lanes(-delta, (tokens_here, 128))
+            dqt_ref[...] = jnp.zeros(dqt_ref.shape, F32)
+        else:
+            dqt_ref[...] = prior_ref[...]
 
     def attend(masked):
         lane = lax.broadcasted_iota(jnp.int32, (keys_here, 128), 1)
@@ -226,21 +235,23 @@
     def _():
         dkv_ref[...] = jnp.zeros(dkv_ref.shape, BF16)
 
-    @pl.when(step == last)
-    def _():
-        lane = lax.broadcasted_iota(jnp.int32, (tokens_here, 128), 1)
-        for pair in range(HEADS // 2):
-            turned = dqt_ref[pair].T
-            outs = []
-            for j in range(2):
-                h = 2 * pair + j
-                out = turned[j * tokens_here : (j + 1) * tokens_here]
-                if h // GROUP != j:
-                    out = jnp.concatenate([out[:, HEAD:], out[:, :HEAD]], 1)
-                outs.append(out)
-            dq_ref[:, pair * 128 : (pair + 1) * 128] = (
-                jnp.where(lane < HEAD, outs[0], outs[1]) * HEAD ** (-0.5)
-            )
+    if last:
+
+        @pl.when(step == end)
+        def _():
+            lane = lax.broadcasted_iota(jnp.int32, (tokens_here, 128), 1)
+            for pair in range(HEADS // 2):
+                turned = dqt_ref[pair].T
+                outs = []
+                for j in range(2):
+                    h = 2 * pair + j
+                    out = turned[j * tokens_here : (j + 1) * tokens_here]
+                    if h // GROUP != j:
+                        out = jnp.concatenate([out[:, HEAD:], out[:, :HEAD]], 1)
+                    outs.append(out)
+                dq_ref[:, pair * 128 : (pair + 1) * 128] = (
+                    jnp.where(lane < HEAD, outs[0], outs[1]) * HEAD ** (-0.5)
+                )
 
 
 def whole_spec(shape):
@@ -279,34 +290,48 @@
     )(info, queries, kv)
 
 
-def attend_backward(info, queries_ext, grad_att, attended, kv):
+def attend_backward(info, queries_ext, grad_att, attended, kv, prior, last):
     blocks, block_len, kv_width = kv.shape
     tokens_here, q_width = grad_att.shape
     rows = HEADS * tokens_here
+    first = prior is None
+    turned = (HEADS // 2, 128, 2 * tokens_here)
+    in_specs = [
+        whole_spec((rows, 256)),
+        whole_spec((tokens_here, q_width)),
+        whole_spec((tokens_here, q_width)),
+        pl.BlockSpec((1, block_len, kv_width), lambda i, info: (i, 0, 0)),
+    ]
+    out_specs = [pl.BlockSpec((1, block_len, kv_width), lambda i, info: (i, 0, 0))]
+    out_shape = [jax.ShapeDtypeStruct(kv.shape, BF16)]
+    scratch = []
+    args = [info, queries_ext, grad_att, attended, kv]
+    if first:
+        if last:
+            scratch.append(pltpu.VMEM((rows, 256), BF16))
+        else:
+            out_specs.append(whole_spec((rows, 256)))
+            out_shape.append(jax.ShapeDtypeStruct((rows, 256), BF16))
+    else:
+        args += [prior[0], prior[1]]
+        in_specs += [whole_spec(turned), whole_spec((rows, 256))]
+    if last:
+        out_specs.insert(0, whole_spec((tokens_here, q_width)))
+        out_shape.insert(0, jax.ShapeDtypeStruct((tokens_here, q_width), F32))
+        scratch.append(pltpu.VMEM(turned, F32))
+    else:
+        out_specs.append(whole_spec(turned))
+        out_shape.append(jax.ShapeDtypeStruct(turned, F32))
     return pl.pallas_call(
-        backward_kernel,
+        functools.partial(backward_kernel, first, last),
         grid_spec=pltpu.PrefetchScalarGridSpec(
             num_scalar_prefetch=1,
             grid=(blocks,),
-            in_specs=[
-                whole_spec((rows, 256)),
-                whole_spec((tokens_here, q_width)),
-                whole_spec((tokens_here, q_width)),
-                pl.BlockSpec((1, block_len, kv_width), lambda i, info: (i, 0, 0)),
-            ],
-            out_specs=[
-                whole_spec((tokens_here, q_width)),
-                pl.BlockSpec((1, block_len, kv_width), lambda i, info: (i, 0, 0)),
-            ],
-            scratch_shapes=[
-                pltpu.VMEM((rows, 256), BF16),
-                pltpu.VMEM((HEADS // 2, 128, 2 * tokens_here), F32),
-            ],
-        ),
-        out_shape=[
-            jax.ShapeDtypeStruct((tokens_here, q_width), F32),
-            jax.ShapeDtypeStruct(kv.shape, BF16),
-        ],
+            in_specs=in_specs,
+            out_specs=out_specs,
+            scratch_shapes=scratch,
+        ),
+        out_shape=out_shape,
         compiler_params=pltpu.CompilerParams(
             dimension_semantics=("arbitrary",), vmem_limit_bytes=40 * 2**20
         ),
@@ -316,23 +341,21 @@
             transcendentals=rows * blocks * block_len,
         ),
         name="attend_backward",
-    )(info, queries_ext, grad_att, attended, kv)
+    )(*args)
 
 
 def spread_columns_kernel(n_z, where_ref, *refs):
-    pieces, (gate_ref, up_ref, held) = refs[:-3], refs[-3:]
+    pieces, (out_ref, held) = refs[:-2], refs[-2:]
     n_part = len(pieces)
     for r in range(n_part):
         held[where_ref[r]] = pieces[r][...].astype(F32)
-    half = held.shape[2] // 2
-    pad = half // n_z
-    piece = gate_ref.shape[1] // (n_z * n_part)
-    for out, start in ((gate_ref, 0), (up_ref, half)):
-        cuts = []
-        for j in range(n_z):
-            for e in range(n_part):
-                cuts.append(held[e, :, start + j * pad : start + j * pad + piece])
-        out[...] = jnp.concatenate(cuts, 1)
+    pad = held.shape[2] // n_z
+    piece = out_ref.shape[1] // (n_z * n_part)
+    cuts = []
+    for j in range(n_z):
+        for e in range(n_part):
+            cuts.append(held[e, :, j * pad : j * pad + piece])
+    out_ref[...] = jnp.concatenate(cuts, 1)
 
 
 def spread_columns(where_at, pieces, n_z, ff):
@@ -345,33 +368,36 @@
             num_scalar_prefetch=1,
             grid=(rows // tile,),
             in_specs=[pl.BlockSpec((tile, cols), lambda i, w: (i, 0))] * n_part,
-            out_specs=[pl.BlockSpec((tile, ff), lambda i, w: (i, 0))] * 2,
+            out_specs=pl.BlockSpec((tile, ff), lambda i, w: (i, 0)),
             scratch_shapes=[pltpu.VMEM((n_part, tile, cols), F32)],
         ),
-        out_shape=[jax.ShapeDtypeStruct((rows, ff), F32)] * 2,
+        out_shape=jax.ShapeDtypeStruct((rows, ff), F32),
         compiler_params=pltpu.CompilerParams(
             dimension_semantics=("arbitrary",), vmem_limit_bytes=40 * 2**20
         ),
         cost_estimate=pl.CostEstimate(
-            flops=0, bytes_accessed=rows * ff * 12, transcendentals=0
+            flops=0, bytes_accessed=rows * ff * 6, transcendentals=0
         ),
         name="spread_columns",
     )(where_at, *pieces)
 
 
-def spread_rows_kernel(where_ref, *refs):
+def spread_rows_kernel(piece, where_ref, *refs):
     pieces, out_ref = refs[:-1], refs[-1]
-    piece = out_ref.shape[0] // len(pieces)
+    room = out_ref.shape[0] // piece
     for r in range(len(pieces)):
-        start = pl.multiple_of(where_ref[r] * piece, 8)
-        out_ref[pl.ds(start, piece), :] = pieces[r][...].astype(F32)[:piece]
-
-
-def spread_rows(where_at, pieces, rows_out):
+
+        @pl.when(where_ref[r] < room)
+        def _():
+            start = pl.multiple_of(where_ref[r] * piece, 8)
+            out_ref[pl.ds(start, piece), :] = pieces[r][...].astype(F32)[:piece]
+
+
+def spread_rows(where_at, pieces, piece, rows_out):
     rows, cols = pieces[0].shape
     tile = 128
     return pl.pallas_call(
-        spread_rows_kernel,
+        functools.partial(spread_rows_kernel, piece),
         grid_spec=pltpu.PrefetchScalarGridSpec(
             num_scalar_prefetch=1,
             grid=(cols // tile,),
@@ -387,6 +413,41 @@
         ),
         name="spread_rows",
     )(where_at, *pieces)
+
+
+def join_weight_kernel(where_ref, *refs):
+    pieces, out_ref = refs[:-1], refs[-1]
+    n_part = len(pieces)
+    n_z, part_rows = pieces[0].shape[:2]
+    room = out_ref.shape[1] // part_rows
+    for r in range(n_part):
+
+        @pl.when(where_ref[r] < room)
+        def _():
+            start = pl.multiple_of(where_ref[r] * part_rows, 16)
+            for k in range(n_z):
+                out_ref[where_ref[n_part + k], pl.ds(start, part_rows), :] = pieces[r][k]
+
+
+def join_weight(where_at, pieces, rows_here):
+    n_z, part_rows, cols = pieces[0].shape
+    return pl.pallas_call(
+        join_weight_kernel,
+        grid_spec=pltpu.PrefetchScalarGridSpec(
+            num_scalar_prefetch=1,
+            grid=(1,),
+            in_specs=[pl.BlockSpec(p.shape, lambda i, w: (0, 0, 0)) for p in pieces],
+            out_specs=pl.BlockSpec((n_z, rows_here, cols), lambda i, w: (0, 0, 0)),
+        ),
+        out_shape=jax.ShapeDtypeStruct((n_z, rows_here, cols), BF16),
+        compiler_params=pltpu.CompilerParams(
+            dimension_semantics=("arbitrary",), vmem_limit_bytes=40 * 2**20
+        ),
+        cost_estimate=pl.CostEstimate(
+            flops=0, bytes_accessed=4 * n_z * rows_here * cols, transcendentals=0
+        ),
+        name="join_weight",
+    )(where_at, *pieces).reshape(n_z * rows_here, cols)
 
 
 def local(
@@ -414,7 +475,6 @@
     core = lax.axis_index("seq")
     n_part = 2 * tp
     part = lax.rem(here, tp) * 2 + core
-    first_core = core == 0
 
     def swap(v):
         return lax.ppermute(v, "seq", [(0, 1), (1, 0)])
@@ -438,33 +498,43 @@
     tokens_here, width = tokens.shape[1:]
     ff = gate_weight.shape[1]
     rows_here = q_weight.shape[0]
-    q_half = GROUP * HEAD
     key_width = KV_HEADS * HEAD
     block_len = tokens_here * n_z
 
-    vec_len = 3 * rows_here + 2 * k_bias.shape[0]
+    idx = jnp.arange(n_part, dtype=jnp.int32)
+    where_at = ((idx // 2) ^ lax.rem(here, tp)) * 2 + ((idx % 2) ^ core)
+    where_z = jnp.arange(n_z, dtype=jnp.int32) ^ zed
+    part_rows = -(-rows_here // (n_part * 32)) * 32
+
+    kb = k_bias.shape[0]
     vec = jnp.concatenate([norm1_gain, norm2_gain, q_bias, k_bias, v_bias])
-    half_width = q_half + 2 * HEAD
-    vec_rows = 16
-    vec = jnp.pad(vec, (0, vec_rows * half_width - vec_len)).reshape(vec_rows, half_width)
-    qkv_half = jnp.concatenate(
-        [
-            lax.dynamic_slice_in_dim(q_weight, core * q_half, q_half, 1),
-            lax.dynamic_slice_in_dim(k_weight, core * HEAD, HEAD, 1),
-            lax.dynamic_slice_in_dim(v_weight, core * HEAD, HEAD, 1),
-        ],
-        1,
-    )
-    got = gather_z(jnp.concatenate([qkv_half, vec], 0)).reshape(n_z, -1, half_width)
-    w_qkv_own = got[:, :rows_here].reshape(width, half_width)
-    w_qkv_oth = swap(w_qkv_own)
-    vecs = got[:, rows_here:].reshape(n_z, -1)
+    vec_rows = -(-vec.shape[0] // (16 * 2 * key_width)) * 16
+    vec = jnp.pad(vec, (0, vec_rows * 2 * key_width - vec.shape[0])).reshape(vec_rows, -1)
+    kv_pack = jnp.concatenate([jnp.concatenate([k_weight, v_weight], 1), vec], 0)
+    kv_pack, q_weight, o_weight, gate_weight, up_weight, down_weight = lax.optimization_barrier(
+        (kv_pack, q_weight, o_weight, gate_weight, up_weight, down_weight)
+    )
+    kv_got = jnp.stack([hop_z(kv_pack, k) for k in range(n_z)])
+    kv_got = jnp.take(kv_got, where_z, axis=0)
+    w_kv = kv_got[:, :rows_here].reshape(width, 2 * key_width)
+    vecs = kv_got[:, rows_here:].reshape(n_z, -1)
     gain_one = vecs[:, :rows_here].reshape(-1)
     gain_two = vecs[:, rows_here : 2 * rows_here].reshape(-1)
     b_query = vecs[:, 2 * rows_here : 3 * rows_here].reshape(-1)
-    kb = k_bias.shape[0]
     b_key = vecs[:, 3 * rows_here : 3 * rows_here + kb].reshape(-1)
     b_value = vecs[:, 3 * rows_here + kb : 3 * rows_here + 2 * kb].reshape(-1)
+
+    def gather_shared(w):
+        mine = lax.dynamic_slice_in_dim(w, part * part_rows, part_rows, 0)
+        mine = jnp.stack([hop_z(mine, k) for k in range(n_z)])
+        pieces = []
+        for k in range(tp):
+            pieces.append(hop(mine, k))
+            pieces.append(swap(pieces[-1]))
+        return join_weight(jnp.concatenate([where_at, where_z]), pieces, rows_here)
+
+    w_query = gather_shared(q_weight)
+    w_out = gather_shared(o_weight)
 
     ff_z = ff // n_z
     piece = ff_z // n_part
@@ -478,31 +548,11 @@
             cuts.append(jnp.pad(cut, ((0, 0), (0, piece_pad - piece))))
         return jnp.concatenate(cuts, 1)
 
-    o_rows = rows_here // 2
+    gu_own = gather_z(jnp.concatenate([ff_columns(gate_weight), ff_columns(up_weight)], 1))
+    gu_oth = swap(gu_own)
     down_cut = lax.dynamic_slice_in_dim(down_weight, part * piece, piece, 0)
-    do_cut = jnp.concatenate(
-        [
-            jnp.pad(down_cut, ((0, piece_pad - piece), (0, 0))),
-            lax.dynamic_slice_in_dim(o_weight, core * o_rows, o_rows, 0),
-        ],
-        0,
-    )
-    gu_cut = jnp.concatenate([ff_columns(gate_weight), ff_columns(up_weight)], 1)
-    w_qkv_own, do_cut, gu_cut = lax.optimization_barrier((w_qkv_own, do_cut, gu_cut))
-    do_own = gather_z(do_cut)
-    do_own, gu_cut = lax.optimization_barrier((do_own, gu_cut))
-    gu_own = gather_z(gu_cut)
-    gu_oth = swap(gu_own)
-    do_oth = swap(do_own)
-    do_own = do_own.reshape(n_z, -1, width)
-    do_oth = do_oth.reshape(n_z, -1, width)
-    down_own = do_own[:, :piece_pad].reshape(ff_half, width)
-    down_oth = do_oth[:, :piece_pad].reshape(ff_half, width)
-    o_own = do_own[:, piece_pad:]
-    o_oth = do_oth[:, piece_pad:]
-    w_out = jnp.where(
-        first_core, jnp.stack([o_own, o_oth], 1), jnp.stack([o_oth, o_own], 1)
-    ).reshape(width, width)
+    down_own = gather_z(jnp.pad(down_cut, ((0, piece_pad - piece), (0, 0))))
+    down_oth = swap(down_own)
     og_here = out_grad[0]
     og_all = jnp.concatenate([hop(og_here, k) for k in range(tp)], 0)
 
@@ -521,16 +571,10 @@
 
     inputs = tokens[0].astype(F32)
     normed_one, scale_one, hidden_one = rms_forward(inputs, gain_one)
-    pre_own = matmul(hidden_one, w_qkv_own)
-    pre_oth = matmul(hidden_one, w_qkv_oth)
-    pre_a = jnp.where(first_core, pre_own, pre_oth)
-    pre_b = jnp.where(first_core, pre_oth, pre_own)
-    query_pre = jnp.concatenate([pre_a[:, :q_half], pre_b[:, :q_half]], 1) + b_query
-    key_pre = (
-        jnp.concatenate([pre_a[:, q_half : q_half + HEAD], pre_b[:, q_half : q_half + HEAD]], 1)
-        + b_key
-    )
-    value_pre = jnp.concatenate([pre_a[:, q_half + HEAD :], pre_b[:, q_half + HEAD :]], 1) + b_value
+    key_value = matmul(hidden_one, w_kv)
+    key_pre = key_value[:, :key_width] + b_key
+    value_pre = key_value[:, key_width:] + b_value
+    query_pre = matmul(hidden_one, w_query) + b_query
     queries = rotate(query_pre.reshape(tokens_here, HEADS, HEAD), cosine_table, sine_table)
     queries = queries.astype(BF16).reshape(tokens_here, HEADS * HEAD) * BF16(HEAD ** (-0.5))
     key_rot = rotate(key_pre.reshape(tokens_here, KV_HEADS, HEAD), cosine_table, sine_table)
@@ -539,7 +583,8 @@
     )
     kv_block = jnp.concatenate([hop_z(kv_local, k) for k in range(n_z)], 0)
     if n_ctx == tp:
-        kv_whole = jnp.stack([hop(kv_block, k) for k in range(n_ctx)])
+        kv_blocks = [hop(kv_block, k) for k in range(n_ctx)]
+        kv_whole = jnp.stack(kv_blocks)
     else:
         kv_whole = lax.all_gather(kv_block, "ctx", axis=0, tiled=False)
     attended, queries_ext = attend_forward(info, queries, kv_whole)
@@ -550,10 +595,7 @@
 
     def scatter_plane(v):
         parts = v.astype(BF16).reshape(tp, tokens_here, width)
-        total = parts[0].astype(F32)
-        for k in range(1, tp):
-            total = total + hop(parts[k], k).astype(F32)
-        return total
+        return [hop(parts[k], k) for k in range(tp)]
 
     def ff_half_pass(w_gu, w_d):
         gu = matmul(h2_all, w_gu)
@@ -565,80 +607,99 @@
         grad_act = times_transposed(og_all, w_d)
         grad_gate = (grad_act * up * sig * (1.0 + gate * (1.0 - sig))).astype(BF16)
         grad_up = (grad_act * silu).astype(BF16)
-        return act, jnp.concatenate([grad_gate, grad_up], 1)
-
-    act_own, ggu_own = ff_half_pass(gu_own, down_own)
-    act_oth, ggu_oth = ff_half_pass(gu_oth, down_oth)
-    grad_h2 = scatter_plane(times_transposed(ggu_own, gu_own) + times_transposed(ggu_oth, gu_oth))
-    result = resid + scatter_plane(matmul(act_own, down_own) + matmul(act_oth, down_oth))
+        return act, grad_gate, grad_up
+
+    act_own, gg_own, gup_own = ff_half_pass(gu_own, down_own)
+    act_oth, gg_oth, gup_oth = ff_half_pass(gu_oth, down_oth)
+    grad_h2_parts = scatter_plane(
+        times_transposed(jnp.concatenate([gg_own, gup_own], 1), gu_own)
+        + times_transposed(jnp.concatenate([gg_oth, gup_oth], 1), gu_oth)
+    )
+    ff_out = scatter_plane(matmul(act_own, down_own) + matmul(act_oth, down_oth))
+    result = resid + sum(v.astype(F32) for v in ff_out)
     layer_out = result.astype(BF16)[None]
-
-    idx = jnp.arange(n_part, dtype=jnp.int32)
-    where_at = ((idx // 2) ^ lax.rem(here, tp)) * 2 + ((idx % 2) ^ core)
 
     def reduce_start(part_sum):
         cols = part_sum.shape[1]
-        cut = part_sum.astype(BF16).reshape(n_z, 2, rows_here // 2, cols)
-        own = lax.dynamic_index_in_dim(cut, core, 1, keepdims=False)
-        oth = lax.dynamic_index_in_dim(cut, 1 - core, 1, keepdims=False)
-        return (own.astype(F32) + swap(oth).astype(F32)).astype(BF16).reshape(-1, cols)
-
-    def scatter_hops(v):
-        cut = v.reshape(n_z, -1, v.shape[1])
-        total = lax.dynamic_index_in_dim(cut, zed, 0, keepdims=False).astype(F32)
-        for k in range(1, n_z):
-            out = lax.dynamic_index_in_dim(cut, zed ^ k, 0, keepdims=False)
-            total = total + hop_z(out, k).astype(F32)
-        return total.astype(BF16)
-
-    def reduce_end(mine):
+        cut = part_sum.astype(BF16).reshape(n_z, rows_here, cols)
+        cut = jnp.pad(cut, ((0, 0), (0, n_part * part_rows - rows_here), (0, 0)))
+        cut = cut.reshape(n_z, tp, 2, part_rows, cols)
+        own = lax.dynamic_index_in_dim(cut, core, 2, keepdims=False)
+        oth = lax.dynamic_index_in_dim(cut, 1 - core, 2, keepdims=False)
+        return (own.astype(F32) + swap(oth).astype(F32)).astype(BF16)
+
+    def reduce_end(cut):
+        cols = cut.shape[-1]
+        total = 0.0
+        for k in range(tp):
+            at = lax.rem(here, tp) ^ k
+            total = total + hop(lax.dynamic_index_in_dim(cut, at, 1, keepdims=False), k).astype(F32)
+        cut = total.astype(BF16)
+        total = 0.0
+        for k in range(n_z):
+            total = total + hop_z(
+                lax.dynamic_index_in_dim(cut, zed ^ k, 0, keepdims=False), k
+            ).astype(F32)
+        total = ctx_groups_sum(total.astype(BF16))
+        total = lax.optimization_barrier(total)
+        pieces = []
+        for k in range(tp):
+            pieces.append(hop(total, k))
+            pieces.append(swap(pieces[-1]))
+        return spread_rows(where_at, pieces, part_rows, rows_here)
+
+    def ctx_groups_sum(v):
         if n_ctx == tp:
-            k = 1
-            while k < n_ctx:
-                mine = lax.optimization_barrier(mine)
-                mine = (mine.astype(F32) + hop(mine, k).astype(F32)).astype(BF16)
-                k *= 2
-            mine = lax.optimization_barrier(mine)
-        else:
-            mine = lax.psum(mine, "ctx")
-        other = swap(mine)
-        whole = jnp.where(
-            first_core, jnp.concatenate([mine, other], 0), jnp.concatenate([other, mine], 0)
-        )
-        return whole.astype(F32)
+            return v
+        groups = [[g * tp + c for g in range(n_ctx // tp)] for c in range(tp)]
+        return lax.psum(v, "ctx", axis_index_groups=groups)
 
     def core_sum(own, oth):
         return (own + swap(oth.astype(BF16)).astype(F32)).astype(BF16)
 
     def ff_pieces(mine):
-        if n_ctx != tp:
-            groups = [[g * tp + c for g in range(n_ctx // tp)] for c in range(tp)]
-            mine = lax.psum(mine, "ctx", axis_index_groups=groups)
+        mine = ctx_groups_sum(mine)
         pieces = []
         for k in range(tp):
             pieces.append(hop(mine, k))
             pieces.append(swap(pieces[-1]))
         return pieces
 
-    d_gu = core_sum(contract_rows(h2_all, ggu_own), contract_rows(h2_all, ggu_oth))
     d_down = core_sum(contract_rows(act_own, og_all), contract_rows(act_oth, og_all))
+    d_gate = core_sum(contract_rows(h2_all, gg_own), contract_rows(h2_all, gg_oth))
+    d_up = core_sum(contract_rows(h2_all, gup_own), contract_rows(h2_all, gup_oth))
+    grad_h2_parts, d_down, d_gate, d_up = lax.optimization_barrier(
+        (grad_h2_parts, d_down, d_gate, d_up)
+    )
+    d_down = scatter_z(d_down)
+    d_gate = scatter_z(d_gate)
+    d_up = scatter_z(d_up)
+    grad_h2 = sum(v.astype(F32) for v in grad_h2_parts)
 
     grad_norm_two, grad_gain_two = rms_backward(grad_h2, normed_two, scale_two, gain_two)
     grad_resid = og_here.astype(F32) + grad_norm_two
     grad_proj = grad_resid.astype(BF16)
     grad_att = times_transposed(grad_proj, w_out).astype(BF16)
-    d_out = reduce_start(contract_rows(attended, grad_proj))
-    grad_att, d_gu, d_down, d_out = lax.optimization_barrier((grad_att, d_gu, d_down, d_out))
-    d_gu = scatter_z(d_gu)
-    d_down = scatter_z(d_down)
-    d_out = scatter_z(d_out)
-    grad_queries, grad_terms = attend_backward(info, queries_ext, grad_att, attended, kv_whole)
     if n_ctx == tp:
-        kv_sum = grad_terms[0].astype(F32)
-        for k in range(1, n_ctx):
-            kv_sum = kv_sum + hop(grad_terms[k], k).astype(F32)
-        kv_sum = kv_sum.astype(BF16)
+        state = None
+        sent = [None] * n_ctx
+        for k in list(range(1, n_ctx)) + [0]:
+            block_info = jnp.concatenate([info[:2], info[2 + k : 3 + k]])
+            got = attend_backward(
+                block_info, queries_ext, grad_att, attended, kv_blocks[k][None], state, k == 0
+            )
+            if k == 0:
+                grad_queries, sent[0] = got
+            elif state is None:
+                sent[k], ext, turned = got
+            else:
+                sent[k], turned = got
+            state = (turned, ext)
+        kv_sum = sum(hop(sent[k][0], k).astype(F32) for k in range(n_ctx)).astype(BF16)
     else:
+        grad_queries, grad_terms = attend_backward(
+            info, queries_ext, grad_att, attended, kv_whole, None, True
+        )
         kv_sum = lax.psum_scatter(grad_terms, "ctx", scatter_dimension=0, tiled=False)
     kv_sum = kv_sum.reshape(n_z, tokens_here, 2 * key_width)
     grad_kv = kv_sum[0].astype(F32)
@@ -659,23 +720,8 @@
     )
     grad_v_pre = grad_kv[:, key_width:].astype(BF16)
 
-    def column_halves(q, k, v):
-        return [
-            jnp.concatenate(
-                [
-                    q[:, g * q_half : (g + 1) * q_half],
-                    k[:, g * HEAD : (g + 1) * HEAD],
-                    v[:, g * HEAD : (g + 1) * HEAD],
-                ],
-                1,
-            )
-            for g in range(2)
-        ]
-
-    halves = column_halves(grad_q_pre, grad_k_pre, grad_v_pre)
-    g_own = jnp.where(first_core, halves[0], halves[1])
-    g_oth = jnp.where(first_core, halves[1], halves[0])
-    grad_hidden_one = times_transposed(g_own, w_qkv_own) + times_transposed(g_oth, w_qkv_oth)
+    grad_kv_pre = jnp.concatenate([grad_k_pre, grad_v_pre], 1)
+    grad_hidden_one = times_transposed(grad_q_pre, w_query) + times_transposed(grad_kv_pre, w_kv)
     grad_norm_one, grad_gain_one = rms_backward(grad_hidden_one, normed_one, scale_one, gain_one)
     tokens_grad = (grad_resid + grad_norm_one)[None]
 
@@ -693,21 +739,20 @@
         ],
         1,
     )
-    grad_w_query = reduce_end(
-        scatter_hops(reduce_start(contract_rows(hidden_one, grad_q_pre)))
-    )
+    grad_w_query = reduce_end(reduce_start(contract_rows(hidden_one, grad_q_pre)))
     grad_w_kv = jnp.concatenate(
         [
-            contract_rows(hidden_one, jnp.concatenate([grad_k_pre, grad_v_pre], 1)),
+            contract_rows(hidden_one, grad_kv_pre),
             jnp.pad(columns, ((0, 0), (0, 128 - columns.shape[1]))),
         ],
         1,
     )
-    grad_w_kv = reduce_end(scatter_hops(reduce_start(grad_w_kv)))
+    grad_w_kv = reduce_end(reduce_start(grad_w_kv))
     sums = grad_w_kv[:, 2 * key_width :]
-    grad_w_out = reduce_end(d_out)
-    grad_w_gate, grad_w_up = spread_columns(where_at, ff_pieces(d_gu), n_z, ff)
-    grad_w_down = spread_rows(where_at, ff_pieces(d_down), ff_z)
+    grad_w_out = reduce_end(reduce_start(contract_rows(attended, grad_proj)))
+    grad_w_down = spread_rows(where_at, ff_pieces(d_down), piece, ff_z)
+    grad_w_gate = spread_columns(where_at, ff_pieces(d_gate), n_z, ff)
+    grad_w_up = spread_columns(where_at, ff_pieces(d_up), n_z, ff)
 
     return (
         layer_out,

time: 462 us -> 481 us (1.041)
  waiting for transfers between devices: 208 us -> 76.2 us
  starting transfers between devices: 69.8 us -> 145 us
  Pallas kernels: 45.9 us -> 88.3 us
  other arithmetic: 20.3 us -> 35 us
  local copies, waits for them, and re-layouts: 47.1 us -> 58.8 us
  matrix products: 46.6 us -> 54 us
    all_gather x3 -> x2, waiting for transfers between devices: 55.8 us -> 0.01 us  [gather_z(): return lax.all_gather(v, 'fsdp', axis=0, tiled=True)]
    ppermute x30 -> x51, waiting for transfers between devices: 97.7 us -> 51.6 us  [hop(): return lax.ppermute(v, 'ctx', [(i, i ^ k) for i in range(n_ctx)])]
    ppermute x19 -> x40, starting transfers between devices: 15.5 us -> 60.2 us  [swap(): return lax.ppermute(v, 'seq', [(0, 1), (1, 0)])]
    pallas_call x2 -> x10, Pallas kernels: 25.7 us -> 60.2 us  [the longest x4 45 us: attend_backward(): pl.pallas_call(functools.partial(backward_kernel, first, last), grid_spec...]
    ppermute x12 -> x24, waiting for transfers between devices: 53.5 us -> 24.4 us  [hop_z(): return lax.ppermute(v, 'fsdp', [(i, i ^ k) for i in range(n_z)])]
    ppermute x12 -> x24, starting transfers between devices: 17.4 us -> 38.6 us  [hop_z(): return lax.ppermute(v, 'fsdp', [(i, i ^ k) for i in range(n_z)])]
    unnamed x130 -> x179, local copies, waits for them, and re-layouts: 10.8 us -> 21.3 us
    ppermute x30 -> x51, starting transfers between devices: 36.5 us -> 45.8 us  [hop(): return lax.ppermute(v, 'ctx', [(i, i ^ k) for i in range(n_ctx)])]
  transfers between devices with their start and end apart: 67 -> 120, of which waited for: 25 -> 25; matrix products, arithmetic and copies ran while one was open for 18% -> 22% of each run, Pallas kernels for 9% -> 18%
where the time goes in v3:
time: 481 us; the launch traced here: 473 us
  starting transfers between devices  145 us (30%)
  Pallas kernels  88.3 us (18%)
  waiting for transfers between devices  76.2 us (16%)
  local copies, waits for them, and re-layouts  58.8 us (12%)
  matrix products  54 us (11%)
  other arithmetic  35 us (7%)
  between operations  16.1 us (3%)
    ppermute x40, starting transfers between devices, swap(): return lax.ppermute(v, 'seq', [(0, 1), (1, 0)])  60.2 us
    ppermute x51, waiting for transfers between devices, hop(): return lax.ppermute(v, 'ctx', [(i, i ^ k) for i in range(n_ctx)])  51.6 us
    ppermute x51, starting transfers between devices, hop(): return lax.ppermute(v, 'ctx', [(i, i ^ k) for i in range(n_ctx)])  45.8 us
    pallas_call x4, Pallas kernels, attend_backward(): pl.pallas_call(functools.partial(backward_kernel, first, last), grid_spec...  45 us
    ppermute x24, starting transfers between devices, hop_z(): return lax.ppermute(v, 'fsdp', [(i, i ^ k) for i in range(n_z)])  38.6 us
    dot_general x9, matrix products, contract_rows(): lax.dot_general(left_side, right_side, (((0,), (0,)), ((), ())), preferre...  24.7 us
    ppermute x24, waiting for transfers between devices, hop_z(): return lax.ppermute(v, 'fsdp', [(i, i ^ k) for i in range(n_z)])  24.4 us
    unnamed x179, local copies, waits for them, and re-layouts  21.3 us
  transfers between devices with their start and end apart: 120, of which 25 were waited for; matrix products, arithmetic and copies ran while one was open for 22% of the time, Pallas kernels for 18%

profile of v3, /device:TPU:1, one launch (start us, length us, event | category | flops | bytes accessed | tf_op | source)
XLA Modules:
  0.0 473.3 jit_solution(18094481975952354056)
XLA Ops:
  17.3 4.2 collective-permute-start.5
  31.2 3.7 concatenate.79.info_ref
  38.9 8.8 %collective-permute-done.1 = bf16[240,256]{1,0:T(8,128)(2,1)S(1)} collective-permute-done((bf16[240,256]{1,0:T(8,128)(2,1)S(1)}, bf16[240,256]{1,0:T(8,128)(2,1)S(1)}, u32[]{:S(2)}, u32[]{:S(2)}) %collective-permute-start.1) | collective-permute-done | bytes 122912 | tf_op jit(solution)/shard_map/ppermute | solution.py:490
  50.8 4.5 collective-permute-start.15
  55.3 5.2 %collective-permute-start.6 = (bf16[4,32,896]{2,1,0:T(8,128)(2,1)S(1)}, bf16[4,32,896]{2,1,0:T(8,128)(2,1)S(1)}, u32[]{:S(2)}, u32[]{:S(2)}) collective-permute-start(bf16[4,32,896]{2,1,0:T(8,128)(2,1)S(1)} %pad_maximum_fusion.6.refs_0_), channel_id=1, source_target_pairs={{0,16},{16,0},{1,17},{17,1},{2,18},{18,2},{3,19},{19,3},{4,20},{20... | collective-permute-start | bytes 688136 | tf_op jit(solution)/shard_map/ppermute | solution.py:480
  62.0 8.3 %collective-permute-start.14 = (bf16[192,256]{1,0:T(8,128)(2,1)S(1)}, bf16[192,256]{1,0:T(8,128)(2,1)S(1)}, u32[]{:S(2)}, u32[]{:S(2)}) collective-permute-start(bf16[192,256]{1,0:T(8,128)(2,1)S(1)} %pad_maximum_fusion.9), channel_id=1, source_target_pairs={{0,2},{1,3},{2,0},{3,1},{4,6},{5,7},{6,4},{7,5},{8,10},{9,11},{10,... | collective-permute-start | bytes 294920 | tf_op jit(solution)/shard_map/ppermute | solution.py:490
  70.3 4.7 %collective-permute-start.8 = (bf16[4,32,896]{2,1,0:T(8,128)(2,1)S(1)}, bf16[4,32,896]{2,1,0:T(8,128)(2,1)S(1)}, u32[]{:S(2)}, u32[]{:S(2)}) collective-permute-start(bf16[4,32,896]{2,1,0:T(8,128)(2,1)S(1)} %collective-permute-done.7.refs_2_), channel_id=1, source_target_pairs={{0,16},{16,0},{1,17},{17,1},{2,18},{18,2},{3,19},{19,3},{4,20},{20... | collective-permute-start | bytes 688136 | tf_op jit(solution)/shard_map/ppermute | solution.py:480
  78.2 5.6 %collective-permute-done.13 = bf16[192,256]{1,0:T(8,128)(2,1)S(1)} collective-permute-done((bf16[192,256]{1,0:T(8,128)(2,1)S(1)}, bf16[192,256]{1,0:T(8,128)(2,1)S(1)}, u32[]{:S(2)}, u32[]{:S(2)}) %collective-permute-start.13) | collective-permute-done | bytes 98336 | tf_op jit(solution)/shard_map/ppermute | solution.py:490
  83.8 5.5 %collective-permute-start.22 = (bf16[4,32,896]{2,1,0:T(8,128)(2,1)S(1)}, bf16[4,32,896]{2,1,0:T(8,128)(2,1)S(1)}, u32[]{:S(2)}, u32[]{:S(2)}) collective-permute-start(bf16[4,32,896]{2,1,0:T(8,128)(2,1)S(1)} %pad_maximum_fusion.7.refs_0_), channel_id=1, source_target_pairs={{0,16},{16,0},{1,17},{17,1},{2,18},{18,2},{3,19},{19,3},{4,20},{20... | collective-permute-start | bytes 688136 | tf_op jit(solution)/shard_map/ppermute | solution.py:480
  99.3 12.3 %collective-permute-start.24 = (bf16[4,32,896]{2,1,0:T(8,128)(2,1)S(1)}, bf16[4,32,896]{2,1,0:T(8,128)(2,1)S(1)}, u32[]{:S(2)}, u32[]{:S(2)}) collective-permute-start(bf16[4,32,896]{2,1,0:T(8,128)(2,1)S(1)} %collective-permute-done.23.refs_2_), channel_id=1, source_target_pairs={{0,16},{16,0},{1,17},{17,1},{2,18},{18,2},{3,19},{19,3},{4,20},{20... | collective-permute-start | bytes 688136 | tf_op jit(solution)/shard_map/ppermute | solution.py:480
  128.4 17.4 %attend_forward.1 = (bf16[192,896]{1,0:T(8,128)(2,1)S(1)}, bf16[2688,256]{1,0:T(8,128)(2,1)S(1)}) custom-call(s32[6]{0:T(128)S(1)} %copy-done.38, bf16[192,896]{1,0:T(8,128)(2,1)S(1)} %copy-done.5, bf16[4,768,256]{2,1,0:T(8,128)(2,1)S(1)} %pad_maximum_fusion.kv_ref), custom_call_target="tpu_custom_call" | custom-call | flops 8455716864 | bytes 6291456 | tf_op jit(solution)/shard_map/attend_forward/pallas_call | solution.py:265
  158.6 6.5 %collective-permute-done.30 = bf16[192,896]{1,0:T(8,128)(2,1)} collective-permute-done((bf16[192,896]{1,0:T(8,128)(2,1)}, bf16[192,896]{1,0:T(8,128)(2,1)}, u32[]{:S(2)}, u32[]{:S(2)}) %collective-permute-start.30) | collective-permute-done | bytes 344096 | tf_op jit(solution)/shard_map/ppermute | solution.py:485
  165.8 4.3 fusion.82
  182.0 4.3 fusion.81
  189.1 3.9 add_convert_fusion
  217.3 4.3 add_convert_fusion.2
  221.6 4.2 add_convert_fusion.4
  229.9 7.3 %collective-permute-done.35 = bf16[192,896]{1,0:T(8,128)(2,1)} collective-permute-done((bf16[192,896]{1,0:T(8,128)(2,1)}, bf16[192,896]{1,0:T(8,128)(2,1)}, u32[]{:S(2)}, u32[]{:S(2)}) %collective-permute-start.35) | collective-permute-done | bytes 344096 | tf_op jit(solution)/shard_map/ppermute | solution.py:485
  245.4 9.0 %attend_backward.4 = (bf16[1,768,256]{2,1,0:T(8,128)(2,1)S(1)}, bf16[2688,256]{1,0:T(8,128)(2,1)S(1)}, f32[7,128,384]{2,1,0:T(8,128)S(1)}) custom-call(s32[3]{0:T(128)S(1)} %copy-done.41, bf16[2688,256]{1,0:T(8,128)(2,1)S(1)} %copy-done.44, bf16[192,896]{1,0:T(8,128)(2,1)S(1)} %copy-done.4, bf16[192,896]{1,0:T(8,128)(2,1)S(1)} %get-tuple-element.40.att_ref, ...), custom_call_target="tpu_custom_call" | custom-call | flops 5284823040 | bytes 8388608 | tf_op jit(solution)/shard_map/attend_backward/pallas_call | solution.py:325
  254.4 13.8 %attend_backward.5 = (bf16[1,768,256]{2,1,0:T(8,128)(2,1)}, f32[7,128,384]{2,1,0:T(8,128)S(1)}) custom-call(s32[3]{0:T(128)S(1)} %copy-done.40, bf16[2688,256]{1,0:T(8,128)(2,1)S(1)} %copy-done.44, bf16[192,896]{1,0:T(8,128)(2,1)S(1)} %copy-done.4, bf16[192,896]{1,0:T(8,128)(2,1)S(1)} %get-tuple-element.40.att_ref, bf16[1,768,256]{2,1,0:T(8,128)(2,1)} %bitcast.25.kv_ref, ...), custom_call_target="tpu_custom_call" | custom-call | flops 5284823040 | bytes 8388608 | tf_op jit(solution)/shard_map/attend_backward/pallas_call | solution.py:325
  268.2 13.8 %attend_backward.6 = (bf16[1,768,256]{2,1,0:T(8,128)(2,1)}, f32[7,128,384]{2,1,0:T(8,128)S(1)}) custom-call(s32[3]{0:T(128)S(1)} %copy-done.39, bf16[2688,256]{1,0:T(8,128)(2,1)S(1)} %copy-done.44, bf16[192,896]{1,0:T(8,128)(2,1)S(1)} %copy-done.4, bf16[192,896]{1,0:T(8,128)(2,1)S(1)} %get-tuple-element.40.att_ref, bf16[1,768,256]{2,1,0:T(8,128)(2,1)} %bitcast.26.kv_ref, ...), custom_call_target="tpu_custom_call" | custom-call | flops 5284823040 | bytes 8388608 | tf_op jit(solution)/shard_map/attend_backward/pallas_call | solution.py:325
  284.7 8.4 %attend_backward.7 = (f32[192,896]{1,0:T(8,128)S(1)}, bf16[1,768,256]{2,1,0:T(8,128)(2,1)S(1)}) custom-call(s32[3]{0:T(128)S(1)} %copy-done.42, bf16[2688,256]{1,0:T(8,128)(2,1)S(1)} %copy-done.44, bf16[192,896]{1,0:T(8,128)(2,1)S(1)} %copy-done.4, bf16[192,896]{1,0:T(8,128)(2,1)S(1)} %get-tuple-element.40.att_ref, bf16[1,768,256]{2,1,0:T(8,128)(2,1)S(1)} %copy-done.3, ...), custom_call_target="tpu_custom_call" | custom-call | flops 5284823040 | bytes 8388608 | tf_op jit(solution)/shard_map/attend_backward/pallas_call | solution.py:325
  352.7 3.8 collective-permute-start.59
  358.3 3.8 collective-permute-done.82
  398.9 3.7 collective-permute-done.95.refs_2_
  405.1 4.8 %collective-permute-done.99.refs_6_ = bf16[224,640]{1,0:T(8,128)(2,1)S(1)} collective-permute-done((bf16[224,640]{1,0:T(8,128)(2,1)}, bf16[224,640]{1,0:T(8,128)(2,1)S(1)}, u32[]{:S(2)}, u32[]{:S(2)}) %collective-permute-start.99) | collective-permute-done | bytes 286752 | tf_op jit(solution)/shard_map/ppermute | solution.py:485
  416.3 6.1 %collective-permute-done.104.refs_4_ = bf16[224,640]{1,0:T(8,128)(2,1)S(1)} collective-permute-done((bf16[224,640]{1,0:T(8,128)(2,1)}, bf16[224,640]{1,0:T(8,128)(2,1)S(1)}, u32[]{:S(2)}, u32[]{:S(2)}) %collective-permute-start.104) | collective-permute-done | bytes 286752 | tf_op jit(solution)/shard_map/ppermute | solution.py:485
  423.6 3.6 collective-permute-done.109.refs_2_
  429.4 4.5 collective-permute-start.103
  451.3 5.3 %spread_columns.2 = f32[224,4864]{1,0:T(8,128)} custom-call(s32[8]{0:T(128)S(1)} %copy-done.36, bf16[224,640]{1,0:T(8,128)(2,1)S(1)} %copy-done.6, bf16[224,640]{1,0:T(8,128)(2,1)S(1)} %collective-permute-done.94.refs_1_, bf16[224,640]{1,0:T(8,128)(2,1)S(1)} %collective-permute-done.95.refs_2_, bf16[224,640]{1,0:T(8,128)(2,1)S(1)} %collective-permute-done.96.refs_3_, ...), custom_call_target="tpu_custom_call" | custom-call | bytes 6537216 | tf_op jit(solution)/shard_map/spread_columns/pallas_call | solution.py:365
  456.7 5.3 %spread_columns.3 = f32[224,4864]{1,0:T(8,128)} custom-call(s32[8]{0:T(128)S(1)} %copy-done.37, bf16[224,640]{1,0:T(8,128)(2,1)S(1)} %copy-done.7, bf16[224,640]{1,0:T(8,128)(2,1)S(1)} %collective-permute-done.101.refs_1_, bf16[224,640]{1,0:T(8,128)(2,1)S(1)} %collective-permute-done.102.refs_2_, bf16[224,640]{1,0:T(8,128)(2,1)S(1)} %collective-permute-done.103.refs_3_, ...), custom_call_target="tpu_custom_call" | custom-call | bytes 6537216 | tf_op jit(solution)/shard_map/spread_columns/pallas_call | solution.py:365
  462.0 4.6 spread_rows.7
  (551 shorter events, 251.5 us)
Async XLA Ops:
  7.2 145.0 %all-gather.3.cloned.1.call-start = ((), (), s32[]{:S(2)}) async-start(), calls=%async_computation.3 | async-start | bytes 2867200 | tf_op jit(solution)/shard_map/all_gather | solution.py:493
  16.5 148.7 %all-gather.5.cloned.1.call-start = ((), (), s32[]{:S(2)}) async-start(), calls=%async_computation.4 | async-start | bytes 1433600 | tf_op jit(solution)/shard_map/all_gather | solution.py:493
  25.0 22.6 %collective-permute-start.1 = (bf16[240,256]{1,0:T(8,128)(2,1)S(1)}, bf16[240,256]{1,0:T(8,128)(2,1)S(1)}, u32[]{:S(2)}, u32[]{:S(2)}) collective-permute-start(bf16[240,256]{1,0:T(8,128)(2,1)S(1)} %pad_maximum_fusion.8), channel_id=1, source_target_pairs={{0,2},{1,3},{2,0},{3,1},{4,6},{5,7},{6,4},{7,5},{8,10},{9,11},{10,... | collective-permute-start | bytes 368648 | tf_op jit(solution)/shard_map/ppermute | solution.py:490
  25.8 354.0 %reduce-scatter.4.cloned.1.call-start = ((), (), s32[]{:S(2)}) async-start(), calls=%async_computation.5 | async-start | bytes 1433600 | tf_op jit(solution)/shard_map/reduce_scatter | solution.py:496
  34.9 20.4 %collective-permute-start.21 = (bf16[32,896]{1,0:T(8,128)(2,1)S(1)}, bf16[32,896]{1,0:T(8,128)(2,1)S(1)}, u32[]{:S(2)}, u32[]{:S(2)}) collective-permute-start(bf16[32,896]{1,0:T(8,128)(2,1)S(1)} %constant_dynamic-slice_fusion.15), channel_id=1, source_target_pairs={{0,3},{1,2},{2,1},{3,0},{4,7},{5,6},{6,5},{7,4},{8,11},{9,10},{10,... | collective-permute-start | bytes 172040 | tf_op jit(solution)/shard_map/ppermute | solution.py:490
  38.1 22.4 %collective-permute-start.20 = (bf16[32,896]{1,0:T(8,128)(2,1)S(1)}, bf16[32,896]{1,0:T(8,128)(2,1)S(1)}, u32[]{:S(2)}, u32[]{:S(2)}) collective-permute-start(bf16[32,896]{1,0:T(8,128)(2,1)S(1)} %constant_dynamic-slice_fusion.15), channel_id=1, source_target_pairs={{0,2},{1,3},{2,0},{3,1},{4,6},{5,7},{6,4},{7,5},{8,10},{9,11},{10,... | collective-permute-start | bytes 172040 | tf_op jit(solution)/shard_map/ppermute | solution.py:490
  38.2 23.7 %collective-permute-start.19 = (bf16[32,896]{1,0:T(8,128)(2,1)S(1)}, bf16[32,896]{1,0:T(8,128)(2,1)S(1)}, u32[]{:S(2)}, u32[]{:S(2)}) collective-permute-start(bf16[32,896]{1,0:T(8,128)(2,1)S(1)} %constant_dynamic-slice_fusion.15), channel_id=1, source_target_pairs={{0,1},{1,0},{2,3},{3,2},{4,5},{5,4},{6,7},{7,6},{8,9},{9,8},{10,11... | collective-permute-start | bytes 172040 | tf_op jit(solution)/shard_map/ppermute | solution.py:490
  47.7 22.6 %collective-permute-start.7 = (bf16[4,32,896]{2,1,0:T(8,128)(2,1)S(1)}, bf16[4,32,896]{2,1,0:T(8,128)(2,1)S(1)}, u32[]{:S(2)}, u32[]{:S(2)}) collective-permute-start(bf16[4,32,896]{2,1,0:T(8,128)(2,1)S(1)} %pad_maximum_fusion.6.refs_0_), channel_id=1, source_target_pairs={{0,4},{4,0},{8,12},{12,8},{1,5},{5,1},{9,13},{13,9},{2,6},{6,2},{1... | collective-permute-start | bytes 688136 | tf_op jit(solution)/shard_map/ppermute | solution.py:485
  55.3 33.9 %collective-permute-start.6 = (bf16[4,32,896]{2,1,0:T(8,128)(2,1)S(1)}, bf16[4,32,896]{2,1,0:T(8,128)(2,1)S(1)}, u32[]{:S(2)}, u32[]{:S(2)}) collective-permute-start(bf16[4,32,896]{2,1,0:T(8,128)(2,1)S(1)} %pad_maximum_fusion.6.refs_0_), channel_id=1, source_target_pairs={{0,16},{16,0},{1,17},{17,1},{2,18},{18,2},{3,19},{19,3},{4,20},{20... | collective-permute-start | bytes 688136 | tf_op jit(solution)/shard_map/ppermute | solution.py:480
  60.5 30.0 %collective-permute-start.9 = (bf16[4,32,896]{2,1,0:T(8,128)(2,1)S(1)}, bf16[4,32,896]{2,1,0:T(8,128)(2,1)S(1)}, u32[]{:S(2)}, u32[]{:S(2)}) collective-permute-start(bf16[4,32,896]{2,1,0:T(8,128)(2,1)S(1)} %pad_maximum_fusion.6.refs_0_), channel_id=1, source_target_pairs={{0,8},{4,12},{8,0},{12,4},{1,9},{5,13},{9,1},{13,5},{2,10},{6,14},... | collective-permute-start | bytes 688136 | tf_op jit(solution)/shard_map/ppermute | solution.py:485
  61.8 29.9 %collective-permute-start.11 = (bf16[4,32,896]{2,1,0:T(8,128)(2,1)S(1)}, bf16[4,32,896]{2,1,0:T(8,128)(2,1)S(1)}, u32[]{:S(2)}, u32[]{:S(2)}) collective-permute-start(bf16[4,32,896]{2,1,0:T(8,128)(2,1)S(1)} %pad_maximum_fusion.6.refs_0_), channel_id=1, source_target_pairs={{0,12},{4,8},{8,4},{12,0},{1,13},{5,9},{9,5},{13,1},{2,14},{6,10},... | collective-permute-start | bytes 688136 | tf_op jit(solution)/shard_map/ppermute | solution.py:485
  70.3 22.0 %collective-permute-start.8 = (bf16[4,32,896]{2,1,0:T(8,128)(2,1)S(1)}, bf16[4,32,896]{2,1,0:T(8,128)(2,1)S(1)}, u32[]{:S(2)}, u32[]{:S(2)}) collective-permute-start(bf16[4,32,896]{2,1,0:T(8,128)(2,1)S(1)} %collective-permute-done.7.refs_2_), channel_id=1, source_target_pairs={{0,16},{16,0},{1,17},{17,1},{2,18},{18,2},{3,19},{19,3},{4,20},{20... | collective-permute-start | bytes 688136 | tf_op jit(solution)/shard_map/ppermute | solution.py:480
  94.0 19.5 %collective-permute-start.27 = (bf16[4,32,896]{2,1,0:T(8,128)(2,1)S(1)}, bf16[4,32,896]{2,1,0:T(8,128)(2,1)}, u32[]{:S(2)}, u32[]{:S(2)}) collective-permute-start(bf16[4,32,896]{2,1,0:T(8,128)(2,1)S(1)} %pad_maximum_fusion.7.refs_0_), channel_id=1, source_target_pairs={{0,12},{4,8},{8,4},{12,0},{1,13},{5,9},{9,5},{13,1},{2,14},{6,10},... | collective-permute-start | bytes 688136 | tf_op jit(solution)/shard_map/ppermute | solution.py:485
  94.2 32.6 %collective-permute-start.18 = (bf16[768,256]{1,0:T(8,128)(2,1)}, bf16[768,256]{1,0:T(8,128)(2,1)}, u32[]{:S(2)}, u32[]{:S(2)}) collective-permute-start(bf16[768,256]{1,0:T(8,128)(2,1)} %pad_maximum_fusion.5), channel_id=1, source_target_pairs={{0,12},{4,8},{8,4},{12,0},{1,13},{5,9},{9,5},{13,1},{2,14},{6,10},... | collective-permute-start | bytes 1179656 | tf_op jit(solution)/shard_map/ppermute | solution.py:485
  98.8 28.1 %collective-permute-start.17 = (bf16[768,256]{1,0:T(8,128)(2,1)}, bf16[768,256]{1,0:T(8,128)(2,1)}, u32[]{:S(2)}, u32[]{:S(2)}) collective-permute-start(bf16[768,256]{1,0:T(8,128)(2,1)} %pad_maximum_fusion.5), channel_id=1, source_target_pairs={{0,8},{4,12},{8,0},{12,4},{1,9},{5,13},{9,1},{13,5},{2,10},{6,14},... | collective-permute-start | bytes 1179656 | tf_op jit(solution)/shard_map/ppermute | solution.py:485
  99.0 27.9 %collective-permute-start.16 = (bf16[768,256]{1,0:T(8,128)(2,1)}, bf16[768,256]{1,0:T(8,128)(2,1)}, u32[]{:S(2)}, u32[]{:S(2)}) collective-permute-start(bf16[768,256]{1,0:T(8,128)(2,1)} %pad_maximum_fusion.5), channel_id=1, source_target_pairs={{0,4},{4,0},{8,12},{12,8},{1,5},{5,1},{9,13},{13,9},{2,6},{6,2},{1... | collective-permute-start | bytes 1179656 | tf_op jit(solution)/shard_map/ppermute | solution.py:485
  117.1 53.0 %collective-permute-start.39 = (bf16[192,896]{1,0:T(8,128)(2,1)}, bf16[192,896]{1,0:T(8,128)(2,1)}, u32[]{:S(2)}, u32[]{:S(2)}) collective-permute-start(bf16[192,896]{1,0:T(8,128)(2,1)} %bitcast.230), channel_id=1, source_target_pairs={{0,12},{4,8},{8,4},{12,0},{1,13},{5,9},{9,5},{13,1},{2,14},{6,10},... | collective-permute-start | bytes 1032200 | tf_op jit(solution)/shard_map/ppermute | solution.py:485
  152.2 29.8 %collective-permute-start.32 = (bf16[896,1280]{1,0:T(8,128)(2,1)}, bf16[896,1280]{1,0:T(8,128)(2,1)}, u32[]{:S(2)}, u32[]{:S(2)}) collective-permute-start(bf16[896,1280]{1,0:T(8,128)(2,1)} %all-gather.3.cloned.1.call-done), channel_id=1, source_target_pairs={{0,16},{16,0},{1,17},{17,1},{2,18},{18,2},{3,19},{19,3},{4,20},{20... | collective-permute-start | bytes 6881288 | tf_op jit(solution)/shard_map/ppermute | solution.py:480
  165.2 21.1 %collective-permute-start.33 = (bf16[640,896]{1,0:T(8,128)(2,1)}, bf16[640,896]{1,0:T(8,128)(2,1)S(1)}, u32[]{:S(2)}, u32[]{:S(2)}) collective-permute-start(bf16[640,896]{1,0:T(8,128)(2,1)} %all-gather.5.cloned.1.call-done), channel_id=1, source_target_pairs={{0,16},{16,0},{1,17},{17,1},{2,18},{18,2},{3,19},{19,3},{4,20},{20... | collective-permute-start | bytes 3440648 | tf_op jit(solution)/shard_map/ppermute | solution.py:480
  194.1 31.8 %collective-permute-start.40 = (bf16[192,896]{1,0:T(8,128)(2,1)}, bf16[192,896]{1,0:T(8,128)(2,1)}, u32[]{:S(2)}, u32[]{:S(2)}) collective-permute-start(bf16[192,896]{1,0:T(8,128)(2,1)} %get-tuple-element.95), channel_id=1, source_target_pairs={{0,4},{4,0},{8,12},{12,8},{1,5},{5,1},{9,13},{13,9},{2,6},{6,2},{1... | collective-permute-start | bytes 1032200 | tf_op jit(solution)/shard_map/ppermute | solution.py:485
  194.5 33.0 %collective-permute-start.41 = (bf16[192,896]{1,0:T(8,128)(2,1)}, bf16[192,896]{1,0:T(8,128)(2,1)}, u32[]{:S(2)}, u32[]{:S(2)}) collective-permute-start(bf16[192,896]{1,0:T(8,128)(2,1)} %get-tuple-element.94), channel_id=1, source_target_pairs={{0,8},{4,12},{8,0},{12,4},{1,9},{5,13},{9,1},{13,5},{2,10},{6,14},... | collective-permute-start | bytes 1032200 | tf_op jit(solution)/shard_map/ppermute | solution.py:485
  242.4 154.5 %reduce-scatter.6.cloned.1.call-start = ((), (), s32[]{:S(2)}) async-start(), calls=%async_computation.6 | async-start | bytes 1433600 | tf_op jit(solution)/shard_map/reduce_scatter | solution.py:496
  282.1 19.3 %collective-permute-start.47 = (bf16[768,256]{1,0:T(8,128)(2,1)}, bf16[768,256]{1,0:T(8,128)(2,1)}, u32[]{:S(2)}, u32[]{:S(2)}) collective-permute-start(bf16[768,256]{1,0:T(8,128)(2,1)} %bitcast.38), channel_id=1, source_target_pairs={{0,8},{4,12},{8,0},{12,4},{1,9},{5,13},{9,1},{13,5},{2,10},{6,14},... | collective-permute-start | bytes 1179656 | tf_op jit(solution)/shard_map/ppermute | solution.py:485
  282.1 19.3 %collective-permute-start.46 = (bf16[768,256]{1,0:T(8,128)(2,1)S(1)}, bf16[768,256]{1,0:T(8,128)(2,1)}, u32[]{:S(2)}, u32[]{:S(2)}) collective-permute-start(bf16[768,256]{1,0:T(8,128)(2,1)S(1)} %bitcast.213), channel_id=1, source_target_pairs={{0,4},{4,0},{8,12},{12,8},{1,5},{5,1},{9,13},{13,9},{2,6},{6,2},{1... | collective-permute-start | bytes 1179656 | tf_op jit(solution)/shard_map/ppermute | solution.py:485
  309.2 27.5 %collective-permute-start.66 = (bf16[4,4,32,896]{3,2,0,1:T(8,128)(2,1)}, bf16[4,4,32,896]{3,2,0,1:T(8,128)(2,1)}, u32[]{:S(2)}, u32[]{:S(2)}) collective-permute-start(bf16[4,4,32,896]{3,2,0,1:T(8,128)(2,1)} %bitcast.207), channel_id=1, source_target_pairs={{0,16},{16,0},{1,17},{17,1},{2,18},{18,2},{3,19},{19,3},{4,20},{20... | collective-permute-start | bytes 2752520 | tf_op jit(solution)/shard_map/ppermute | solution.py:480
  311.1 94.0 %reduce-scatter.8.cloned.1.call-start = ((), (), s32[]{:S(2)}) async-start(), calls=%async_computation.7 | async-start | bytes 1433600 | tf_op jit(solution)/shard_map/reduce_scatter | solution.py:496
  402.6 19.8 %collective-permute-start.104 = (bf16[224,640]{1,0:T(8,128)(2,1)}, bf16[224,640]{1,0:T(8,128)(2,1)S(1)}, u32[]{:S(2)}, u32[]{:S(2)}) collective-permute-start(bf16[224,640]{1,0:T(8,128)(2,1)} %reduce-scatter.6.cloned.1.call-done.refs_0_), channel_id=1, source_target_pairs={{0,8},{4,12},{8,0},{12,4},{1,9},{5,13},{9,1},{13,5},{2,10},{6,14},... | collective-permute-start | bytes 860168 | tf_op jit(solution)/shard_map/ppermute | solution.py:485
  414.9 19.7 %collective-permute-start.113 = (bf16[160,896]{1,0:T(8,128)(2,1)}, bf16[160,896]{1,0:T(8,128)(2,1)S(1)}, u32[]{:S(2)}, u32[]{:S(2)}) collective-permute-start(bf16[160,896]{1,0:T(8,128)(2,1)} %reduce-scatter.8.cloned.1.call-done.refs_0_), channel_id=1, source_target_pairs={{0,12},{4,8},{8,4},{12,0},{1,13},{5,9},{9,5},{13,1},{2,14},{6,10},... | collective-permute-start | bytes 860168 | tf_op jit(solution)/shard_map/ppermute | solution.py:485
  422.4 19.3 %collective-permute-start.96 = (bf16[224,640]{1,0:T(8,128)(2,1)S(1)}, bf16[224,640]{1,0:T(8,128)(2,1)S(1)}, u32[]{:S(2)}, u32[]{:S(2)}) collective-permute-start(bf16[224,640]{1,0:T(8,128)(2,1)S(1)} %collective-permute-done.95.refs_2_), channel_id=1, source_target_pairs={{0,16},{16,0},{1,17},{17,1},{2,18},{18,2},{3,19},{19,3},{4,20},{20... | collective-permute-start | bytes 860168 | tf_op jit(solution)/shard_map/ppermute | solution.py:480
  441.8 20.2 %collective-permute-start.108 = (bf16[160,896]{1,0:T(8,128)(2,1)}, bf16[160,896]{1,0:T(8,128)(2,1)S(1)}, u32[]{:S(2)}, u32[]{:S(2)}) collective-permute-start(bf16[160,896]{1,0:T(8,128)(2,1)} %reduce-scatter.8.cloned.1.call-done.refs_0_), channel_id=1, source_target_pairs={{0,16},{16,0},{1,17},{17,1},{2,18},{18,2},{3,19},{19,3},{4,20},{20... | collective-permute-start | bytes 860168 | tf_op jit(solution)/shard_map/ppermute | solution.py:480
  442.3 19.7 %collective-permute-start.110 = (bf16[160,896]{1,0:T(8,128)(2,1)S(1)}, bf16[160,896]{1,0:T(8,128)(2,1)S(1)}, u32[]{:S(2)}, u32[]{:S(2)}) collective-permute-start(bf16[160,896]{1,0:T(8,128)(2,1)S(1)} %collective-permute-done.109.refs_2_), channel_id=1, source_target_pairs={{0,16},{16,0},{1,17},{17,1},{2,18},{18,2},{3,19},{19,3},{4,20},{20... | collective-permute-start | bytes 860168 | tf_op jit(solution)/shard_map/ppermute | solution.py:480
  442.4 19.6 %collective-permute-start.112 = (bf16[160,896]{1,0:T(8,128)(2,1)S(1)}, bf16[160,896]{1,0:T(8,128)(2,1)S(1)}, u32[]{:S(2)}, u32[]{:S(2)}) collective-permute-start(bf16[160,896]{1,0:T(8,128)(2,1)S(1)} %collective-permute-done.111.refs_4_), channel_id=1, source_target_pairs={{0,16},{16,0},{1,17},{17,1},{2,18},{18,2},{3,19},{19,3},{4,20},{20... | collective-permute-start | bytes 860168 | tf_op jit(solution)/shard_map/ppermute | solution.py:480
  (176 other events, 1801.1 us)
Sparse Core Ops, SparseCore 0:
  16.6 71.5 all-gather.2
  90.3 29.4 all-gather.4
  242.5 26.4 reduce-scatter.3
  311.2 26.3 reduce-scatter.5
  339.7 28.1 reduce-scatter.7
